TPU v7x, 128 devices: a whole 4x4x4 slice. The times are simulated.
128 devices in a mesh: gx: 16 (over z, x), gy: 8 (over y, core).
Axes of the slice: x: 4, y: 4, z: 4, core: 2. Of those that a mesh axis runs over, the one named last changes fastest.
Arguments:
- coarse_state: float32 [5, 256, 128, 128], P(None, 'gx', 'gy'), may hold values from -0.64 to 4.4, as said below
- patch_state: float32 [16, 8, 4, 5, 32, 1024], P('gx', 'gy'), may hold values from -0.64 to 4.4, as said below
- patch_anchor: int32 [16, 8, 4, 3], P(None, 'gy'), may hold values from 0 to 240, as said below
- patch_count: int32 [16, 8], P(None, 'gy'), may hold values from 1 to 4, as said below
Outputs:
- coarse_next: float32 [5, 256, 128, 128], P(None, 'gx', 'gy')
- patch_next: float32 [16, 8, 4, 5, 32, 1024], P('gx', 'gy')
Inputs may be any that keep to these rules, and one draw needn't show every extreme that they name: `coarse_state`: density and pressure of every cell lie in [0.625, 1.6] and each velocity component in [-0.4, 0.4]. `patch_state`: density and pressure of every cell lie in [0.625, 1.6] and each velocity component in [-0.4, 0.4]. `patch_anchor`: entry [o, r, s] is 0 for s >= patch_count[o, r]. A live patch of device (o, r) has its second component r * 16 and its first and third multiples of 16; its z block index (third component / 16) has the parity of the sum of its pencil's two indices, so no two patches share a face. Every pencil of 16 x 16 coarse columns holds exactly 2 patches, owned by devices of its own gy index, no two by the same device. `patch_count`: each gy index's counts sum to 2 * 16.
All inputs are finite; a program needn't handle non-finite values.
Results may differ from a plain program's by a relative error of at most 0.0003.
Values sent between devices are 32-bit elements; how exact they have to be, the bound alone decides.
A program may use at most 192 MiB of HBM per device.

v0:
```python
import jax
import jax.numpy as jnp
from jax import lax
from jax.sharding import PartitionSpec as P

RIEMANN = 2


gamma_ratio = 1.4
courant = 0.12


def padded_2(cells, sides, width):
    for axis, dim in sides:
        count = lax.axis_size(axis)
        head = lax.slice_in_dim(cells, 0, width, axis=dim)
        tail = lax.slice_in_dim(cells, cells.shape[dim] - width, cells.shape[dim], axis=dim)
        cells = jnp.concatenate(
            [
                lax.ppermute(tail, axis, [(i, (i + 1) % count) for i in range(count)]),
                cells,
                lax.ppermute(head, axis, [((i + 1) % count, i) for i in range(count)]),
            ],
            axis=dim,
        )
    return cells


def primitives(conserved):
    density = conserved[0]
    velocity = conserved[1:4] / density
    pressure = (gamma_ratio - 1.0) * (
        conserved[4] - 0.5 * density * jnp.sum(velocity * velocity, axis=0)
    )
    return (density, velocity, pressure)


def physical_flux(conserved, velocity, pressure, normal):
    normal_speed = velocity[normal]
    pieces = [conserved[0] * normal_speed]
    for component in range(3):
        momentum_term = conserved[1 + component] * normal_speed
        if component == normal:
            momentum_term = momentum_term + pressure
        pieces.append(momentum_term)
    pieces.append((conserved[4] + pressure) * normal_speed)
    return jnp.stack(pieces)


def branch_terms(star_press, side_press, side_dens, side_sound):
    exponent = (gamma_ratio - 1.0) / (2.0 * gamma_ratio)
    coef_a = 2.0 / ((gamma_ratio + 1.0) * side_dens)
    coef_b = (gamma_ratio - 1.0) / (gamma_ratio + 1.0) * side_press
    root_term = jnp.sqrt(coef_a / (star_press + coef_b))
    shock_term = (star_press - side_press) * root_term
    shock_slope = root_term * (1.0 - 0.5 * (star_press - side_press) / (star_press + coef_b))
    press_ratio = star_press / side_press
    rarefy_term = 2.0 * side_sound / (gamma_ratio - 1.0) * (press_ratio**exponent - 1.0)
    rarefy_slope = press_ratio ** (-(gamma_ratio + 1.0) / (2.0 * gamma_ratio)) / (
        side_dens * side_sound
    )
    compressed = star_press > side_press
    return (
        jnp.where(compressed, shock_term, rarefy_term),
        jnp.where(compressed, shock_slope, rarefy_slope),
    )


def face_flux(lower_state, upper_state, normal):
    dens_left, vel_left, press_left = primitives(lower_state)
    dens_right, vel_right, press_right = primitives(upper_state)
    speed_left = vel_left[normal]
    speed_right = vel_right[normal]
    sound_left = jnp.sqrt(gamma_ratio * press_left / dens_left)
    sound_right = jnp.sqrt(gamma_ratio * press_right / dens_right)
    exponent = (gamma_ratio - 1.0) / (2.0 * gamma_ratio)
    star_press = (
        (sound_left + sound_right - 0.5 * (gamma_ratio - 1.0) * (speed_right - speed_left))
        / (sound_left * press_left ** (-exponent) + sound_right * press_right ** (-exponent))
    ) ** (1.0 / exponent)
    for newton_step in range(RIEMANN):
        value_left, slope_left = branch_terms(star_press, press_left, dens_left, sound_left)
        value_right, slope_right = branch_terms(star_press, press_right, dens_right, sound_right)
        star_press = star_press - (value_left + value_right + speed_right - speed_left) / (
            slope_left + slope_right
        )
    factor = (gamma_ratio + 1.0) / (2.0 * gamma_ratio)
    lift_left = jnp.where(
        star_press > press_left, jnp.sqrt(1.0 + factor * (star_press / press_left - 1.0)), 1.0
    )
    lift_right = jnp.where(
        star_press > press_right, jnp.sqrt(1.0 + factor * (star_press / press_right - 1.0)), 1.0
    )
    wave_low = speed_left - sound_left * lift_left
    wave_high = speed_right + sound_right * lift_right
    flux_left = physical_flux(lower_state, vel_left, press_left, normal)
    flux_right = physical_flux(upper_state, vel_right, press_right, normal)
    blended = (
        wave_high * flux_left
        - wave_low * flux_right
        + wave_low * wave_high * (upper_state - lower_state)
    ) / (wave_high - wave_low)
    return jnp.where(wave_low >= 0.0, flux_left, jnp.where(wave_high <= 0.0, flux_right, blended))


def coarsen(fine_faces):
    fine_cells = fine_faces.shape[-1]
    half_cells = fine_cells // 2
    shaped = fine_faces.reshape(fine_faces.shape[:-2] + (half_cells, 2, half_cells, 2))
    return jnp.sum(shaped, axis=(-3, -1))


def advance(one_patch, one_shell):
    fine_cells = one_patch.shape[1]
    half_cells = fine_cells // 2
    padded_side = fine_cells + 2
    plane_size = padded_side * padded_side
    block_cells = one_patch.reshape(5, fine_cells, fine_cells, fine_cells)
    shell_faces = one_shell.reshape(5, 6, half_cells, half_cells)
    refined = jnp.repeat(jnp.repeat(shell_faces, 2, axis=2), 2, axis=3)
    padded = jnp.pad(block_cells, ((0, 0), (1, 1), (1, 1), (1, 1)), mode="edge")
    padded = padded.at[:, 0, 1:-1, 1:-1].set(refined[:, 0])
    padded = padded.at[:, -1, 1:-1, 1:-1].set(refined[:, 1])
    padded = padded.at[:, 1:-1, 0, 1:-1].set(refined[:, 2])
    padded = padded.at[:, 1:-1, -1, 1:-1].set(refined[:, 3])
    padded = padded.at[:, 1:-1, 1:-1, 0].set(refined[:, 4])
    padded = padded.at[:, 1:-1, 1:-1, -1].set(refined[:, 5])
    flattened = padded.reshape(5, padded_side, plane_size)
    flux_x = face_flux(flattened[:, :-1], flattened[:, 1:], 0)
    flux_y = face_flux(flattened[:, :, :-padded_side], flattened[:, :, padded_side:], 1)
    flux_z = face_flux(flattened[:, :, :-1], flattened[:, :, 1:], 2)
    full_x = jnp.concatenate([flux_x, jnp.zeros((5, 1, plane_size), flux_x.dtype)], axis=1)
    full_y = jnp.concatenate(
        [flux_y, jnp.zeros((5, padded_side, padded_side), flux_y.dtype)], axis=2
    )
    full_z = jnp.concatenate([flux_z, jnp.zeros((5, padded_side, 1), flux_z.dtype)], axis=2)
    change = (
        full_x
        - jnp.roll(full_x, 1, axis=1)
        + (full_y - jnp.roll(full_y, padded_side, axis=2))
        + (full_z - jnp.roll(full_z, 1, axis=2))
    )
    change_cells = change.reshape(5, padded_side, padded_side, padded_side)[:, 1:-1, 1:-1, 1:-1]
    updated = block_cells - courant * change_cells
    cube_x = full_x.reshape(5, padded_side, padded_side, padded_side)
    cube_y = full_y.reshape(5, padded_side, padded_side, padded_side)
    cube_z = full_z.reshape(5, padded_side, padded_side, padded_side)
    boundary = jnp.stack(
        [
            cube_x[:, 0, 1:-1, 1:-1],
            cube_x[:, fine_cells, 1:-1, 1:-1],
            cube_y[:, 1:-1, 0, 1:-1],
            cube_y[:, 1:-1, fine_cells, 1:-1],
            cube_z[:, 1:-1, 1:-1, 0],
            cube_z[:, 1:-1, 1:-1, fine_cells],
        ],
        axis=1,
    )
    return (updated.reshape(5, fine_cells, fine_cells * fine_cells), boundary)


def extend(field):
    return padded_2(field, (("gx", 1), ("gy", 2)), 1)


def coarse_step(field, padded):
    flux_x = face_flux(padded[:, :-1, 1:-1], padded[:, 1:, 1:-1], 0)
    flux_y = face_flux(padded[:, 1:-1, :-1], padded[:, 1:-1, 1:], 1)
    flux_z = face_flux(field, jnp.roll(field, -1, axis=3), 2)
    change = (
        flux_x[:, 1:]
        - flux_x[:, :-1]
        + (flux_y[:, :, 1:] - flux_y[:, :, :-1])
        + (flux_z - jnp.roll(flux_z, 1, axis=3))
    )
    return (flux_x, flux_y, flux_z, field - courant * change)


def six_local(planes, field_z, z_first, upper):
    half_cells = planes[0].shape[1]
    depth_cells = field_z.shape[3]

    def band(plane):
        return lax.dynamic_slice_in_dim(plane, z_first, half_cells, 2)

    lower_plane = lax.dynamic_index_in_dim(field_z, (z_first - 1) % depth_cells, 3, keepdims=False)
    upper_plane = lax.dynamic_index_in_dim(
        field_z, (z_first + upper) % depth_cells, 3, keepdims=False
    )
    return jnp.stack(
        [
            band(planes[0]),
            band(planes[1]),
            band(planes[2]),
            band(planes[3]),
            lower_plane,
            upper_plane,
        ],
        axis=1,
    )


def gather_shells(padded, field, z_start):
    half_cells = field.shape[1]
    planes = (padded[:, 0, 1:-1], padded[:, -1, 1:-1], padded[:, 1:-1, 0], padded[:, 1:-1, -1])
    return jax.vmap(six_local, in_axes=(None, None, 0, None))(planes, field, z_start, half_cells)


def select_row(array, index):
    return lax.dynamic_index_in_dim(array, index, 0, keepdims=False)


def put_row(array, value, index):
    return lax.dynamic_update_index_in_dim(array, value, index, 0)


def substep_round(shells, patches, sources, my_count):
    owners = shells.shape[0]
    fine_cells = patches.shape[2]
    received = lax.all_to_all(shells, "gx", split_axis=0, concat_axis=0, tiled=True)

    def advance_slot(slot_index, loop_state):
        current, outgoing = loop_state
        source = sources[slot_index]
        updated, boundary = advance(select_row(current, slot_index), select_row(received, source))
        current = put_row(current, updated, slot_index)
        outgoing = put_row(outgoing, boundary.reshape(5, 6, fine_cells * fine_cells), source)
        return (current, outgoing)

    empty = jnp.zeros((owners, 5, 6, fine_cells * fine_cells), jnp.float32)
    current, outgoing = lax.fori_loop(0, my_count, advance_slot, (patches, empty))
    arrived = lax.all_to_all(outgoing, "gx", split_axis=0, concat_axis=0, tiled=True)
    return (current, arrived.reshape(owners, 5, 6, fine_cells, fine_cells))


def reflux(advanced, deltas, z_start, present):
    half_cells = advanced.shape[1]
    depth_cells = advanced.shape[3]
    highest = lax.Precision.HIGHEST
    depth_ids = jnp.arange(depth_cells, dtype=jnp.int32)
    offsets = jnp.arange(half_cells, dtype=jnp.int32)
    placed = (
        (depth_ids[None, None, :] == z_start[:, None, None] + offsets[None, :, None])
        & present[:, None, None]
    ).astype(jnp.float32)
    x_low = jnp.einsum("oayk,okz->ayz", deltas[:, :, 0], placed, precision=highest)
    x_high = jnp.einsum("oayk,okz->ayz", deltas[:, :, 1], placed, precision=highest)
    y_low = jnp.einsum("oayk,okz->ayz", deltas[:, :, 2], placed, precision=highest)
    y_high = jnp.einsum("oayk,okz->ayz", deltas[:, :, 3], placed, precision=highest)
    below = (
        (depth_ids[None, :] == (z_start[:, None] - 1) % depth_cells) & present[:, None]
    ).astype(jnp.float32)
    above = (
        (depth_ids[None, :] == (z_start[:, None] + half_cells) % depth_cells) & present[:, None]
    ).astype(jnp.float32)
    correction = jnp.einsum(
        "oaxy,oz->axyz", deltas[:, :, 4], below, precision=highest
    ) + jnp.einsum("oaxy,oz->axyz", deltas[:, :, 5], above, precision=highest)
    rims = jnp.zeros((2, 5, half_cells, half_cells, depth_cells), jnp.float32)
    rims = rims.at[0, :, 0].set(x_low).at[0, :, -1].set(x_high)
    rims = rims.at[1, :, :, 0].set(y_low).at[1, :, :, -1].set(y_high)
    extended = padded_2(rims, (("gx", 2), ("gy", 3)), 1)
    correction = correction.at[:, 0].add(extended[0, :, 0, 1:-1])
    correction = correction.at[:, -1].add(extended[0, :, -1, 1:-1])
    correction = correction.at[:, :, 0].add(extended[1, :, 1:-1, 0])
    correction = correction.at[:, :, -1].add(extended[1, :, 1:-1, -1])
    return advanced + correction


def shards(coarse_state, patch_state, patch_anchor, patch_count):
    owners = lax.axis_size("gx")
    my_index = lax.axis_index("gx")
    half_cells = coarse_state.shape[1]
    slot_total = patch_state.shape[2]
    anchors = patch_anchor[:, 0]
    counts = patch_count[:, 0]
    slot_ids = jnp.arange(slot_total, dtype=jnp.int32)
    in_pencil = (slot_ids[None, :] < counts[:, None]) & (anchors[:, :, 0] // half_cells == my_index)
    present = jnp.any(in_pencil, axis=1)
    z_start = jnp.sum(jnp.where(in_pencil, anchors[:, :, 2], 0), axis=1)
    my_anchors = select_row(anchors, my_index)
    my_count = select_row(counts, my_index)
    sources = my_anchors[:, 0] // half_cells
    patches = patch_state[0, 0]
    present_mask = present.astype(jnp.float32)[:, None, None, None, None]
    padded_old = extend(coarse_state)
    flux_x, flux_y, flux_z, advanced = coarse_step(coarse_state, padded_old)
    padded_new = extend(advanced)
    shell_width = 6 * half_cells * half_cells
    shells_old = (gather_shells(padded_old, coarse_state, z_start) * present_mask).reshape(
        owners, 5, shell_width
    )
    shells_new = (gather_shells(padded_new, advanced, z_start) * present_mask).reshape(
        owners, 5, shell_width
    )
    shells_mid = 0.5 * (shells_old + shells_new)
    patches, arrived_one = substep_round(shells_old, patches, sources, my_count)
    patches, arrived_two = substep_round(shells_mid, patches, sources, my_count)
    fine_mean = 0.125 * (coarsen(arrived_one) + coarsen(arrived_two))
    planes = (flux_x[:, 0], flux_x[:, -1], flux_y[:, :, 0], flux_y[:, :, -1])
    coarse_faces = jax.vmap(six_local, in_axes=(None, None, 0, None))(
        planes, flux_z, z_start, half_cells - 1
    )
    signs = jnp.array([1.0, -1.0, 1.0, -1.0, 1.0, -1.0], dtype=jnp.float32)[
        None, None, :, None, None
    ]
    deltas = (
        courant
        * signs
        * (coarse_faces - fine_mean)
        * present.astype(jnp.float32)[:, None, None, None, None]
    )
    coarse_next = reflux(advanced, deltas, z_start, present)
    return (coarse_next, patches[None, None])


def solution(mesh):
    in_specs = (
        P(None, "gx", "gy", None),
        P("gx", "gy", None, None, None, None),
        P(None, "gy", None, None),
        P(None, "gy"),
    )
    out_specs = (P(None, "gx", "gy", None), P("gx", "gy", None, None, None, None))
    return jax.shard_map(shards, mesh=mesh, in_specs=in_specs, out_specs=out_specs, check_vma=False)
```

profile of v0, /device:TPU:0, one launch (start us, length us, event | category | flops | bytes accessed | tf_op | source)
XLA Modules:
  0.0 1882.9 jit_solution(4571911006443214880)
XLA Ops:
  154.5 770.0 %while.50 = (s32[]{:T(128)}, f32[4,5,32,1024]{3,2,1,0:T(8,128)}, f32[16,5,6,1024]{3,0,1,2:T(8,128)}, s32[]{:T(128)}, s32[4]{0:T(128)S(1)}, /*index=5*/f32[16,5,1...) while((s32[]{:T(128)}, f32[4,5,32,1024]{3,2,1,0:T(8,128)}, ...), condition=%wide.region_15.16_spmd, body=%wide.region_8.15_spmd.sunk | while | flops 41734480 | bytes 95347480 | solution.py:231
  179.6 28.6 %scatter.103 = f32[5,34,34,34]{3,2,1,0:T(8,128)} dynamic-update-slice(f32[5,34,34,34]{3,2,1,0:T(8,128)} %scatter.102, f32[5,32,1,32]{3,2,1,0:T(1,128)S(1)} %bitcast.1170, s32[]{:T(128)} %constant.1346.clone.1..sunk, s32[]{:T(128)} %constant.1284.clone.1..sunk, s32[]{:T(128)} %constant.1346.clone.1..sunk, s32[]{:T(128)} %constant.1284.clone.1..sunk) | dynamic-update-slice | bytes 40964 | tf_op jit(solution)/shard_map/while/body/scatter | solution.py:124
  208.3 28.6 %scatter.104 = f32[5,34,34,34]{3,2,1,0:T(8,128)} dynamic-update-slice(f32[5,34,34,34]{3,2,1,0:T(8,128)} %scatter.103, f32[5,32,1,32]{3,2,1,0:T(1,128)S(1)} %bitcast.1171, s32[]{:T(128)} %constant.1346.clone.1..sunk, s32[]{:T(128)} %constant.1284.clone.1..sunk, s32[]{:T(128)} %constant.1288.clone.1..sunk, s32[]{:T(128)} %constant.1284.clone.1..sunk) | dynamic-update-slice | bytes 40964 | tf_op jit(solution)/shard_map/while/body/scatter | solution.py:125
  239.1 14.1 scatter.105
  255.4 32.3 %scatter.106 = f32[5,34,34,34]{3,2,1,0:T(8,128)} dynamic-update-slice(f32[5,34,34,34]{3,2,1,0:T(8,128)} %scatter.105, f32[5,32,32,1]{3,2,1,0:T(8,128)S(1)} %copy.456, s32[]{:T(128)} %constant.1346.clone.1..sunk, s32[]{:T(128)} %constant.1284.clone.1..sunk, s32[]{:T(128)} %constant.1284.clone.1..sunk, s32[]{:T(128)} %constant.1288.clone.1..sunk) | dynamic-update-slice | bytes 40964 | tf_op jit(solution)/shard_map/while/body/scatter | solution.py:127
  371.3 28.6 %scatter.103 = f32[5,34,34,34]{3,2,1,0:T(8,128)} dynamic-update-slice(f32[5,34,34,34]{3,2,1,0:T(8,128)} %scatter.102, f32[5,32,1,32]{3,2,1,0:T(1,128)S(1)} %bitcast.1170, s32[]{:T(128)} %constant.1346.clone.1..sunk, s32[]{:T(128)} %constant.1284.clone.1..sunk, s32[]{:T(128)} %constant.1346.clone.1..sunk, s32[]{:T(128)} %constant.1284.clone.1..sunk) | dynamic-update-slice | bytes 40964 | tf_op jit(solution)/shard_map/while/body/scatter | solution.py:124
  400.0 28.6 %scatter.104 = f32[5,34,34,34]{3,2,1,0:T(8,128)} dynamic-update-slice(f32[5,34,34,34]{3,2,1,0:T(8,128)} %scatter.103, f32[5,32,1,32]{3,2,1,0:T(1,128)S(1)} %bitcast.1171, s32[]{:T(128)} %constant.1346.clone.1..sunk, s32[]{:T(128)} %constant.1284.clone.1..sunk, s32[]{:T(128)} %constant.1288.clone.1..sunk, s32[]{:T(128)} %constant.1284.clone.1..sunk) | dynamic-update-slice | bytes 40964 | tf_op jit(solution)/shard_map/while/body/scatter | solution.py:125
  430.8 14.1 scatter.105
  447.1 32.3 %scatter.106 = f32[5,34,34,34]{3,2,1,0:T(8,128)} dynamic-update-slice(f32[5,34,34,34]{3,2,1,0:T(8,128)} %scatter.105, f32[5,32,32,1]{3,2,1,0:T(8,128)S(1)} %copy.456, s32[]{:T(128)} %constant.1346.clone.1..sunk, s32[]{:T(128)} %constant.1284.clone.1..sunk, s32[]{:T(128)} %constant.1284.clone.1..sunk, s32[]{:T(128)} %constant.1288.clone.1..sunk) | dynamic-update-slice | bytes 40964 | tf_op jit(solution)/shard_map/while/body/scatter | solution.py:127
  563.0 28.6 %scatter.103 = f32[5,34,34,34]{3,2,1,0:T(8,128)} dynamic-update-slice(f32[5,34,34,34]{3,2,1,0:T(8,128)} %scatter.102, f32[5,32,1,32]{3,2,1,0:T(1,128)S(1)} %bitcast.1170, s32[]{:T(128)} %constant.1346.clone.1..sunk, s32[]{:T(128)} %constant.1284.clone.1..sunk, s32[]{:T(128)} %constant.1346.clone.1..sunk, s32[]{:T(128)} %constant.1284.clone.1..sunk) | dynamic-update-slice | bytes 40964 | tf_op jit(solution)/shard_map/while/body/scatter | solution.py:124
  591.7 28.6 %scatter.104 = f32[5,34,34,34]{3,2,1,0:T(8,128)} dynamic-update-slice(f32[5,34,34,34]{3,2,1,0:T(8,128)} %scatter.103, f32[5,32,1,32]{3,2,1,0:T(1,128)S(1)} %bitcast.1171, s32[]{:T(128)} %constant.1346.clone.1..sunk, s32[]{:T(128)} %constant.1284.clone.1..sunk, s32[]{:T(128)} %constant.1288.clone.1..sunk, s32[]{:T(128)} %constant.1284.clone.1..sunk) | dynamic-update-slice | bytes 40964 | tf_op jit(solution)/shard_map/while/body/scatter | solution.py:125
  622.5 14.1 scatter.105
  638.8 32.3 %scatter.106 = f32[5,34,34,34]{3,2,1,0:T(8,128)} dynamic-update-slice(f32[5,34,34,34]{3,2,1,0:T(8,128)} %scatter.105, f32[5,32,32,1]{3,2,1,0:T(8,128)S(1)} %copy.456, s32[]{:T(128)} %constant.1346.clone.1..sunk, s32[]{:T(128)} %constant.1284.clone.1..sunk, s32[]{:T(128)} %constant.1284.clone.1..sunk, s32[]{:T(128)} %constant.1288.clone.1..sunk) | dynamic-update-slice | bytes 40964 | tf_op jit(solution)/shard_map/while/body/scatter | solution.py:127
  755.0 28.6 %scatter.103 = f32[5,34,34,34]{3,2,1,0:T(8,128)} dynamic-update-slice(f32[5,34,34,34]{3,2,1,0:T(8,128)} %scatter.102, f32[5,32,1,32]{3,2,1,0:T(1,128)S(1)} %bitcast.1170, s32[]{:T(128)} %constant.1346.clone.1..sunk, s32[]{:T(128)} %constant.1284.clone.1..sunk, s32[]{:T(128)} %constant.1346.clone.1..sunk, s32[]{:T(128)} %constant.1284.clone.1..sunk) | dynamic-update-slice | bytes 40964 | tf_op jit(solution)/shard_map/while/body/scatter | solution.py:124
  783.7 28.6 %scatter.104 = f32[5,34,34,34]{3,2,1,0:T(8,128)} dynamic-update-slice(f32[5,34,34,34]{3,2,1,0:T(8,128)} %scatter.103, f32[5,32,1,32]{3,2,1,0:T(1,128)S(1)} %bitcast.1171, s32[]{:T(128)} %constant.1346.clone.1..sunk, s32[]{:T(128)} %constant.1284.clone.1..sunk, s32[]{:T(128)} %constant.1288.clone.1..sunk, s32[]{:T(128)} %constant.1284.clone.1..sunk) | dynamic-update-slice | bytes 40964 | tf_op jit(solution)/shard_map/while/body/scatter | solution.py:125
  830.8 32.3 %scatter.106 = f32[5,34,34,34]{3,2,1,0:T(8,128)} dynamic-update-slice(f32[5,34,34,34]{3,2,1,0:T(8,128)} %scatter.105, f32[5,32,32,1]{3,2,1,0:T(8,128)S(1)} %copy.456, s32[]{:T(128)} %constant.1346.clone.1..sunk, s32[]{:T(128)} %constant.1284.clone.1..sunk, s32[]{:T(128)} %constant.1284.clone.1..sunk, s32[]{:T(128)} %constant.1288.clone.1..sunk) | dynamic-update-slice | bytes 40964 | tf_op jit(solution)/shard_map/while/body/scatter | solution.py:127
  926.1 772.0 %while.51 = (s32[]{:T(128)}, f32[4,5,32,1024]{3,2,1,0:T(8,128)}, f32[16,5,6,1024]{3,0,1,2:T(8,128)}, s32[]{:T(128)}, s32[4]{0:T(128)S(1)}, /*index=5*/f32[16,5,1...) while((s32[]{:T(128)}, f32[4,5,32,1024]{3,2,1,0:T(8,128)}, ...), condition=%wide.region_24.25_spmd, body=%wide.region_17.24_spmd.sunk | while | flops 41734480 | bytes 91415264 | solution.py:231
  951.4 28.6 %scatter.109 = f32[5,34,34,34]{3,2,1,0:T(8,128)} dynamic-update-slice(f32[5,34,34,34]{3,2,1,0:T(8,128)} %scatter.108, f32[5,32,1,32]{3,2,1,0:T(1,128)S(1)} %bitcast.1172, s32[]{:T(128)} %constant.1346.clone.1..sunk.1, s32[]{:T(128)} %constant.1284.clone.1..sunk.1, s32[]{:T(128)} %constant.1346.clone.1..sunk.1, s32[]{:T(128)} %constant.1284.clone.1..sunk.1) | dynamic-update-slice | bytes 40964 | tf_op jit(solution)/shard_map/while/body/scatter | solution.py:124
  980.1 28.6 %scatter.110 = f32[5,34,34,34]{3,2,1,0:T(8,128)} dynamic-update-slice(f32[5,34,34,34]{3,2,1,0:T(8,128)} %scatter.109, f32[5,32,1,32]{3,2,1,0:T(1,128)S(1)} %bitcast.1173, s32[]{:T(128)} %constant.1346.clone.1..sunk.1, s32[]{:T(128)} %constant.1284.clone.1..sunk.1, s32[]{:T(128)} %constant.1288.clone.1..sunk.1, s32[]{:T(128)} %constant.1284.clone.1..sunk.1) | dynamic-update-slice | bytes 40964 | tf_op jit(solution)/shard_map/while/body/scatter | solution.py:125
  1027.1 32.2 %scatter.112 = f32[5,34,34,34]{3,2,1,0:T(8,128)} dynamic-update-slice(f32[5,34,34,34]{3,2,1,0:T(8,128)} %scatter.111, f32[5,32,32,1]{3,2,1,0:T(8,128)S(1)} %copy.463, s32[]{:T(128)} %constant.1346.clone.1..sunk.1, s32[]{:T(128)} %constant.1284.clone.1..sunk.1, s32[]{:T(128)} %constant.1284.clone.1..sunk.1, s32[]{:T(128)} %constant.1288.clone.1..sunk.1) | dynamic-update-slice | bytes 40964 | tf_op jit(solution)/shard_map/while/body/scatter | solution.py:127
  1143.3 28.6 %scatter.109 = f32[5,34,34,34]{3,2,1,0:T(8,128)} dynamic-update-slice(f32[5,34,34,34]{3,2,1,0:T(8,128)} %scatter.108, f32[5,32,1,32]{3,2,1,0:T(1,128)S(1)} %bitcast.1172, s32[]{:T(128)} %constant.1346.clone.1..sunk.1, s32[]{:T(128)} %constant.1284.clone.1..sunk.1, s32[]{:T(128)} %constant.1346.clone.1..sunk.1, s32[]{:T(128)} %constant.1284.clone.1..sunk.1) | dynamic-update-slice | bytes 40964 | tf_op jit(solution)/shard_map/while/body/scatter | solution.py:124
  1171.9 28.6 %scatter.110 = f32[5,34,34,34]{3,2,1,0:T(8,128)} dynamic-update-slice(f32[5,34,34,34]{3,2,1,0:T(8,128)} %scatter.109, f32[5,32,1,32]{3,2,1,0:T(1,128)S(1)} %bitcast.1173, s32[]{:T(128)} %constant.1346.clone.1..sunk.1, s32[]{:T(128)} %constant.1284.clone.1..sunk.1, s32[]{:T(128)} %constant.1288.clone.1..sunk.1, s32[]{:T(128)} %constant.1284.clone.1..sunk.1) | dynamic-update-slice | bytes 40964 | tf_op jit(solution)/shard_map/while/body/scatter | solution.py:125
  1219.0 32.2 %scatter.112 = f32[5,34,34,34]{3,2,1,0:T(8,128)} dynamic-update-slice(f32[5,34,34,34]{3,2,1,0:T(8,128)} %scatter.111, f32[5,32,32,1]{3,2,1,0:T(8,128)S(1)} %copy.463, s32[]{:T(128)} %constant.1346.clone.1..sunk.1, s32[]{:T(128)} %constant.1284.clone.1..sunk.1, s32[]{:T(128)} %constant.1284.clone.1..sunk.1, s32[]{:T(128)} %constant.1288.clone.1..sunk.1) | dynamic-update-slice | bytes 40964 | tf_op jit(solution)/shard_map/while/body/scatter | solution.py:127
  1334.9 28.6 %scatter.109 = f32[5,34,34,34]{3,2,1,0:T(8,128)} dynamic-update-slice(f32[5,34,34,34]{3,2,1,0:T(8,128)} %scatter.108, f32[5,32,1,32]{3,2,1,0:T(1,128)S(1)} %bitcast.1172, s32[]{:T(128)} %constant.1346.clone.1..sunk.1, s32[]{:T(128)} %constant.1284.clone.1..sunk.1, s32[]{:T(128)} %constant.1346.clone.1..sunk.1, s32[]{:T(128)} %constant.1284.clone.1..sunk.1) | dynamic-update-slice | bytes 40964 | tf_op jit(solution)/shard_map/while/body/scatter | solution.py:124
  1363.6 28.6 %scatter.110 = f32[5,34,34,34]{3,2,1,0:T(8,128)} dynamic-update-slice(f32[5,34,34,34]{3,2,1,0:T(8,128)} %scatter.109, f32[5,32,1,32]{3,2,1,0:T(1,128)S(1)} %bitcast.1173, s32[]{:T(128)} %constant.1346.clone.1..sunk.1, s32[]{:T(128)} %constant.1284.clone.1..sunk.1, s32[]{:T(128)} %constant.1288.clone.1..sunk.1, s32[]{:T(128)} %constant.1284.clone.1..sunk.1) | dynamic-update-slice | bytes 40964 | tf_op jit(solution)/shard_map/while/body/scatter | solution.py:125
  1410.6 32.2 %scatter.112 = f32[5,34,34,34]{3,2,1,0:T(8,128)} dynamic-update-slice(f32[5,34,34,34]{3,2,1,0:T(8,128)} %scatter.111, f32[5,32,32,1]{3,2,1,0:T(8,128)S(1)} %copy.463, s32[]{:T(128)} %constant.1346.clone.1..sunk.1, s32[]{:T(128)} %constant.1284.clone.1..sunk.1, s32[]{:T(128)} %constant.1284.clone.1..sunk.1, s32[]{:T(128)} %constant.1288.clone.1..sunk.1) | dynamic-update-slice | bytes 40964 | tf_op jit(solution)/shard_map/while/body/scatter | solution.py:127
  1526.5 28.6 %scatter.109 = f32[5,34,34,34]{3,2,1,0:T(8,128)} dynamic-update-slice(f32[5,34,34,34]{3,2,1,0:T(8,128)} %scatter.108, f32[5,32,1,32]{3,2,1,0:T(1,128)S(1)} %bitcast.1172, s32[]{:T(128)} %constant.1346.clone.1..sunk.1, s32[]{:T(128)} %constant.1284.clone.1..sunk.1, s32[]{:T(128)} %constant.1346.clone.1..sunk.1, s32[]{:T(128)} %constant.1284.clone.1..sunk.1) | dynamic-update-slice | bytes 40964 | tf_op jit(solution)/shard_map/while/body/scatter | solution.py:124
  1555.2 28.6 %scatter.110 = f32[5,34,34,34]{3,2,1,0:T(8,128)} dynamic-update-slice(f32[5,34,34,34]{3,2,1,0:T(8,128)} %scatter.109, f32[5,32,1,32]{3,2,1,0:T(1,128)S(1)} %bitcast.1173, s32[]{:T(128)} %constant.1346.clone.1..sunk.1, s32[]{:T(128)} %constant.1284.clone.1..sunk.1, s32[]{:T(128)} %constant.1288.clone.1..sunk.1, s32[]{:T(128)} %constant.1284.clone.1..sunk.1) | dynamic-update-slice | bytes 40964 | tf_op jit(solution)/shard_map/while/body/scatter | solution.py:125
  1602.3 32.2 %scatter.112 = f32[5,34,34,34]{3,2,1,0:T(8,128)} dynamic-update-slice(f32[5,34,34,34]{3,2,1,0:T(8,128)} %scatter.111, f32[5,32,32,1]{3,2,1,0:T(8,128)S(1)} %copy.463, s32[]{:T(128)} %constant.1346.clone.1..sunk.1, s32[]{:T(128)} %constant.1284.clone.1..sunk.1, s32[]{:T(128)} %constant.1284.clone.1..sunk.1, s32[]{:T(128)} %constant.1288.clone.1..sunk.1) | dynamic-update-slice | bytes 40964 | tf_op jit(solution)/shard_map/while/body/scatter | solution.py:127
  1714.1 30.4 %all-to-all-done.3 = f32[16,5,6,1024]{3,2,1,0:T(8,128)S(1)} async-done(((f32[16,5,6,1024]{3,2,1,0:T(8,128)}), f32[16,5,6,1024]{3,2,1,0:T(8,128)S(1)}, u32[]{:S(2)}, u32[]{:S(2)}) %all-to-all-start.3) | async-done | bytes 1966112 | tf_op jit(solution)/shard_map/all_to_all | solution.py:232
  1801.1 16.7 reduce_sum.290
  1827.5 16.8 reduce_sum.289
  (1045 shorter events, 1023.9 us)
Async XLA Ops:
  4.9 27.2 %collective-permute-start = (f32[5,1,16,128]{3,2,1,0:T(8,128)S(1)}, f32[5,1,16,128]{3,2,1,0:T(8,128)S(1)}, u32[]{:S(2)}, u32[]{:S(2)}) collective-permute-start(f32[5,1,16,128]{3,2,1,0:T(8,128)S(1)} %get-tuple-element.912), channel_id=1, source_target_pairs={{0,8},{8,16},{16,24},{24,32},{32,40},{40,48},{48,56},{56,64},{64,7... | collective-permute-start | bytes 122888 | tf_op jit(solution)/shard_map/ppermute | solution.py:20
  6.5 27.5 %collective-permute-start.1 = (f32[5,1,16,128]{3,2,1,0:T(8,128)}, f32[5,1,16,128]{3,2,1,0:T(8,128)S(1)}, u32[]{:S(2)}, u32[]{:S(2)}) collective-permute-start(f32[5,1,16,128]{3,2,1,0:T(8,128)} %get-tuple-element.911), channel_id=1, source_target_pairs={{8,0},{16,8},{24,16},{32,24},{40,32},{48,40},{56,48},{64,56},{72,6... | collective-permute-start | bytes 122888 | tf_op jit(solution)/shard_map/ppermute | solution.py:22
  18.2 13.9 copy-start.41
  19.5 65.5 %copy-start.31 = (s32[16]{0:T(128)}, s32[16]{0:T(128)S(1)}, u32[]{:S(2)}) copy-start(s32[16]{0:T(128)S(1)} %get-tuple-element.927) | copy-start | bytes 196
  19.5 93.2 %copy-start.5 = (s32[16]{0:T(128)}, s32[16]{0:T(128)S(1)}, u32[]{:S(2)}) copy-start(s32[16]{0:T(128)S(1)} %get-tuple-element.926) | copy-start | bytes 196
  32.1 99.0 %copy-start.46 = (f32[16]{0:T(128)}, f32[16]{0:T(128)S(1)}, u32[]{:S(2)}) copy-start(f32[16]{0:T(128)S(1)} %convert_element_type.11) | copy-start | bytes 196
  34.0 30.7 %copy-start.7 = (f32[5,16,16,128]{3,2,1,0:T(8,128)}, f32[5,16,16,128]{3,2,1,0:T(8,128)S(1)}, u32[]{:S(2)}) copy-start(f32[5,16,16,128]{3,2,1,0:T(8,128)S(1)} %get-tuple-element.907) | copy-start | bytes 1966084
  40.5 18.0 collective-permute-start.2
  40.5 12.5 copy-start.29
  40.5 17.9 collective-permute-start.3
  65.6 38.0 %copy-start.10 = (f32[5,16,16,128]{3,2,1,0:T(8,128)}, f32[5,16,16,128]{3,2,1,0:T(8,128)S(1)}, u32[]{:S(2)}) copy-start(f32[5,16,16,128]{3,2,1,0:T(8,128)S(1)} %fusion.204) | copy-start | bytes 1966084
  65.6 38.0 %collective-permute-start.4 = (f32[5,1,16,128]{3,2,1,0:T(8,128)S(1)}, f32[5,1,16,128]{3,2,1,0:T(8,128)S(1)}, u32[]{:S(2)}, u32[]{:S(2)}) collective-permute-start(f32[5,1,16,128]{3,2,1,0:T(8,128)S(1)} %get-tuple-element.906), channel_id=1, source_target_pairs={{0,8},{8,16},{16,24},{24,32},{32,40},{40,48},{48,56},{56,64},{64,7... | collective-permute-start | bytes 122888 | tf_op jit(solution)/shard_map/ppermute | solution.py:20
  65.7 37.9 %collective-permute-start.5 = (f32[5,1,16,128]{3,2,1,0:T(8,128)S(1)}, f32[5,1,16,128]{3,2,1,0:T(8,128)S(1)}, u32[]{:S(2)}, u32[]{:S(2)}) collective-permute-start(f32[5,1,16,128]{3,2,1,0:T(8,128)S(1)} %get-tuple-element.905), channel_id=1, source_target_pairs={{8,0},{16,8},{24,16},{32,24},{40,32},{48,40},{56,48},{64,56},{72,6... | collective-permute-start | bytes 122888 | tf_op jit(solution)/shard_map/ppermute | solution.py:22
  103.7 6.8 collective-permute-start.6
  106.5 5.9 collective-permute-start.7
  132.5 16.2 all-to-all-start
  148.7 775.8 %all-to-all-start.2 = ((f32[16,5,1536]{2,1,0:T(8,128)}), f32[16,5,1536]{2,1,0:T(8,128)}, u32[]{:S(2)}, u32[]{:S(2)}) async-start(f32[16,5,1536]{2,1,0:T(8,128)} %copy.375), calls=%async_computation.2 | async-start | bytes 1572864 | tf_op jit(solution)/shard_map/all_to_all | solution.py:220
  328.1 10.2 copy-start.1
  711.7 10.2 copy-start.1
  1675.2 10.2 copy-start.3
  1702.4 42.1 %all-to-all-start.3 = ((f32[16,5,6,1024]{3,2,1,0:T(8,128)}), f32[16,5,6,1024]{3,2,1,0:T(8,128)S(1)}, u32[]{:S(2)}, u32[]{:S(2)}) async-start(f32[16,5,6,1024]{3,2,1,0:T(8,128)} %copy.376), calls=%async_computation.3 | async-start | bytes 5242880 | tf_op jit(solution)/shard_map/all_to_all | solution.py:232
  1714.1 35.9 %copy-start.8 = (f32[5,16,16,128]{3,2,1,0:T(8,128)S(1)}, f32[5,16,16,128]{3,2,1,0:T(8,128)}, u32[]{:S(2)}) copy-start(f32[5,16,16,128]{3,2,1,0:T(8,128)} %copy-done.7) | copy-start | bytes 1966084
  1744.4 73.4 %all-to-all-start.1 = ((f32[16,5,6,1024]{3,2,1,0:T(8,128)}), f32[16,5,6,1024]{3,2,1,0:T(8,128)}, u32[]{:S(2)}, u32[]{:S(2)}) async-start(f32[16,5,6,1024]{3,2,1,0:T(8,128)} %copy.364), calls=%async_computation.1 | async-start | bytes 5242880 | tf_op jit(solution)/shard_map/all_to_all | solution.py:232
  1757.5 10.6 copy-start.39
  1759.3 14.9 copy-start.24
  1827.5 16.8 copy-start.47
  1827.5 16.8 copy-start.48
  1858.1 23.6 %copy-start.11 = (f32[5,16,16,128]{3,2,1,0:T(8,128)S(1)}, f32[5,16,16,128]{3,2,1,0:T(8,128)}, u32[]{:S(2)}) copy-start(f32[5,16,16,128]{3,2,1,0:T(8,128)} %copy-done.10) | copy-start | bytes 1966084
  1858.8 8.7 collective-permute-start.8
  1860.9 6.6 collective-permute-start.9
  1867.6 9.5 collective-permute-start.10
  1867.7 11.7 collective-permute-start.11
  (60 other events, 242.1 us)
where the time goes:
time: 1900 us; the launch traced here: 1880 us
  local copies, waits for them, and re-layouts  1400 us (74%)
  other arithmetic  352 us (19%)
  starting transfers between devices  47.5 us (2%)
  waiting for transfers between devices  43.2 us (2%)
  loops' own time  35.7 us (2%)
    scatter x8, local copies, waits for them, and re-layouts, advance(): padded = padded.at[:, 1:-1, 1:-1, -1].set(refined[:, 5])  258 us
    scatter x8, local copies, waits for them, and re-layouts, advance(): padded = padded.at[:, 1:-1, 0, 1:-1].set(refined[:, 2])  229 us
    scatter x8, local copies, waits for them, and re-layouts, advance(): padded = padded.at[:, 1:-1, -1, 1:-1].set(refined[:, 3])  229 us
    scatter x8, local copies, waits for them, and re-layouts, advance(): padded = padded.at[:, 1:-1, 1:-1, 0].set(refined[:, 4])  112 us
    concatenate x16, other arithmetic, advance(): padded = jnp.pad(block_cells, ((0, 0), (1, 1), (1, 1), (1, 1)), mode='edge')  75.6 us
    ge x27, other arithmetic, face_flux(): wave_low >= 0.0  61.5 us
    sub x27, other arithmetic, face_flux(): star_press - (value_left + value_right + speed_right - speed_left) / (slo...  58.9 us
    another operation x30, local copies, waits for them, and re-layouts  41.2 us
  transfers between devices with their start and end apart: 16, of which 3 were waited for; matrix products, arithmetic and copies ran while one was open for 48% of the time, Pallas kernels for 0%

commit v1 on v0

v1 whole, which is shorter than its diff:
```python
import jax
import jax.numpy as jnp
from jax import lax
from jax.experimental import pallas as pl
from jax.experimental.pallas import tpu as pltpu
from jax.sharding import PartitionSpec as P

COURANT = 0.12
VMEM_LIMIT = 56 * 1024 * 1024
F32 = jnp.float32


def rcp(x):
    return pl.reciprocal(x, approx=True)


def root(x):
    return x * lax.rsqrt(x)


def primitives(U):
    r = rcp(U[0])
    u, v, w = U[1] * r, U[2] * r, U[3] * r
    p = 0.4 * (U[4] - 0.5 * (U[1] * u + U[2] * v + U[3] * w))
    c5 = root((35.0 * p) * r)
    cg5 = c5 * jnp.exp2(jnp.log2(p) * (-1.0 / 7.0))
    sa = root(r * (1.0 / 1.2))
    return [u, v, w, p, c5, cg5, sa]


def newton(s, z, scaled, L, R, du):
    value, slope = du, None
    for p6, p7, c5, cg5, sa in (L, R):
        t = s + p6
        q = lax.rsqrt(t)
        rt = sa * q
        d = t - p7
        shock = d * rt
        shock_slope = rt * (1.0 + p7 * (q * q))
        rare = cg5 * z - c5
        rare_slope = cg5 * scaled
        up = d > 0.0
        value = value + jnp.where(up, shock, rare)
        term = jnp.where(up, shock_slope, rare_slope)
        slope = term if slope is None else slope + term
    return s - (value + value) * rcp(slope)


def face_flux(UL, QL, UR, QR, n, keep=None):
    uL, pL, c5L, cg5L, saL = QL[n], QL[3], QL[4], QL[5], QL[6]
    uR, pR, c5R, cg5R, saR = QR[n], QR[3], QR[4], QR[5], QR[6]
    du = uR - uL
    L = (pL * (1.0 / 6.0), pL * (7.0 / 6.0), c5L, cg5L, saL)
    R = (pR * (1.0 / 6.0), pR * (7.0 / 6.0), c5R, cg5R, saR)
    z = (c5L + c5R - du) * rcp(cg5L + cg5R)
    z2 = z * z
    z6 = z2 * z2 * z2
    s = newton(z6 * z, z, (2.0 / 7.0) * rcp(z6), L, R, du)
    z = jnp.exp2(jnp.log2(s) * (1.0 / 7.0))
    s = newton(s, z, (2.0 / 7.0) * z * rcp(s), L, R, du)
    waves = []
    for c5, sa in ((c5L, saL), (c5R, saR)):
        cc = c5 * c5
        waves.append(0.2 * root(jnp.maximum(cc, (cc + (252.0 * s) * (sa * sa)) * (1.0 / 7.0))))
    low = jnp.minimum(uL - waves[0], 0.0)
    high = jnp.maximum(uR + waves[1], 0.0)
    inv = rcp(high - low)
    if keep is not None:
        inv = jnp.where(keep, inv, 0.0)
    wL, wR = high * inv, low * inv
    a, b = wL * (uL - low), wR * (high - uR)
    eL, eR = wL * pL, wR * pR
    F = [a * UL[i] + b * UR[i] for i in range(5)]
    F[1 + n] = F[1 + n] + (eL - eR)
    F[4] = F[4] + (eL * uL - eR * uR)
    return F


def roll(x, by, axis):
    by = by % x.shape[axis]
    return x if by == 0 else pltpu.roll(x, by, axis)


def lanes(shape):
    return lax.broadcasted_iota(jnp.int32, shape, len(shape) - 1)


def block_transpose(vs, width):
    n = len(vs)
    block = lanes(vs[0].shape) // width
    vs = list(vs)
    d = n // 2
    while d:
        low = (block & d) == 0
        for i in range(n):
            if i & d == 0:
                a, b = vs[i], vs[i + d]
                vs[i] = jnp.where(low, a, roll(b, d * width, 1))
                vs[i + d] = jnp.where(low, roll(a, -d * width, 1), b)
        d //= 2
    return vs


def pick(x, index):
    return jnp.take_along_axis(x, index, axis=1)


NORMAL = (2, 2, 0, 0, 1, 1)


def fine_load(patch, W, Q):
    def body(yg, _):
        at = pl.ds(pl.multiple_of(yg * 128, 128), 128)
        U = [[None] * 5 for _ in range(4)]
        for c in range(5):
            vs = block_transpose([patch[s, c, :, at] for s in range(4)], 32)
            for j in range(4):
                W[c, 4 * yg + j] = vs[j]
                U[j][c] = vs[j]
        for j in range(4):
            for k, q in enumerate(primitives(U[j])):
                Q[k, 4 * yg + j] = q
        return 0

    lax.fori_loop(0, 8, body, 0)


def fine_interior(W, Q, FY, B):
    shape = (32, 128)
    row = lax.broadcasted_iota(jnp.int32, shape, 0)
    lane = lanes(shape) % 32
    keep_x, keep_z = row < 31, lane < 31
    for c in range(5):
        FY[c] = jnp.zeros(shape, F32)
        B[2, c] = W[c, :, 0, :]
        B[3, c] = W[c, :, 31, :]
        B[4, c] = W[c, 0]
        B[5, c] = W[c, 31]
        B[0, c] = W[c, 0]
        B[1, c] = W[c, 0]

    def body(y, _):
        up = jnp.minimum(y + 1, 31)
        U = [W[c, y] for c in range(5)]
        S = [Q[k, y] for k in range(7)]
        here = lane == y
        for c in range(5):
            B[0, c] = jnp.where(here, pltpu.roll(U[c], y, 1), B[0, c])
            B[1, c] = jnp.where(here, pltpu.roll(U[c], y + 97, 1), B[1, c])
        total = []
        F = face_flux(U, S, [roll(a, -1, 1) for a in U], [roll(a, -1, 1) for a in S], 2, keep_z)
        for c in range(5):
            total.append(F[c] - roll(F[c], 1, 1))
        F = face_flux(U, S, [roll(a, -1, 0) for a in U], [roll(a, -1, 0) for a in S], 0, keep_x)
        for c in range(5):
            total[c] = total[c] + (F[c] - roll(F[c], 1, 0))
        keep = jnp.broadcast_to(y, shape) < 31
        F = face_flux(
            U, S, [W[c, up] for c in range(5)], [Q[k, up] for k in range(7)], 1, keep
        )
        for c in range(5):
            total[c] = total[c] + (F[c] - FY[c])
            FY[c] = F[c]
            W[c, y] = U[c] - COURANT * total[c]
        return 0

    lax.fori_loop(0, 32, body, 0)


def fine_shells(got, sources, S, mix=None):
    shape = (16, 128)
    lane = lanes(shape)
    slot = lane // 32
    column = (lane % 32) // 2
    for g in range(4):
        blocks = []
        for s in range(4):
            at = pl.ds(16 * g, 16)
            block = got[sources[s], at, :]
            if mix is not None:
                block = 0.5 * (block + mix[sources[s], at, :])
            blocks.append(block)
        for k in range(8):
            q = 8 * g + k
            if q < 30:
                out = None
                for s in range(4):
                    piece = pick(blocks[s], 16 * k + column)
                    out = piece if out is None else jnp.where(slot == s, piece, out)
                S[q // 5, q % 5, pl.ds(0, 16, 2), :] = out
                S[q // 5, q % 5, pl.ds(1, 16, 2), :] = out


def fine_boundary(B, S, FB, FS, W, first):
    def body(e2, _):
        for side in range(2):
            face = 2 * e2 + side
            inner = [B[face, c] for c in range(5)]
            outer = [S[face, c] for c in range(5)]
            for n in range(3):
                axis = (2, 0, 1)[n]

                @pl.when(e2 == n)
                def _():
                    qi, qo = primitives(inner), primitives(outer)
                    if side == 0:
                        F = face_flux(outer, qo, inner, qi, axis)
                    else:
                        F = face_flux(inner, qi, outer, qo, axis)
                    for c in range(5):
                        FB[face, c] = F[c]
                        FS[face, c] = F[c] if first else FS[face, c] + F[c]

        return 0

    lax.fori_loop(0, 3, body, 0)
    for c in range(5):
        W[c, :, 0, :] = W[c, :, 0, :] + COURANT * FB[2, c]
        W[c, :, 31, :] = W[c, :, 31, :] - COURANT * FB[3, c]
        W[c, 0] = W[c, 0] + COURANT * FB[4, c]
        W[c, 31] = W[c, 31] - COURANT * FB[5, c]


def z_boundary(value, FB, c, y, lane):
    value = value + jnp.where(lane == 0, COURANT * pltpu.roll(FB[0, c], 128 - y, 1), 0.0)
    return value - jnp.where(lane == 31, COURANT * pltpu.roll(FB[1, c], 159 - y, 1), 0.0)


def fine_again(W, FB, Q):
    lane = lanes((32, 128)) % 32

    def body(y, _):
        U = []
        for c in range(5):
            U.append(z_boundary(W[c, y], FB, c, y, lane))
            W[c, y] = U[c]
        for k, q in enumerate(primitives(U)):
            Q[k, y] = q
        return 0

    lax.fori_loop(0, 32, body, 0)


def fine_store(W, FB, patch, count, out):
    lane = lanes((32, 128)) % 32

    def body(yg, _):
        at = pl.ds(pl.multiple_of(yg * 128, 128), 128)
        for c in range(5):
            vs = []
            for j in range(4):
                y = 4 * yg + j
                vs.append(z_boundary(W[c, y], FB, c, y, lane))
            vs = block_transpose(vs, 32)
            for s in range(4):
                out[s, c, :, at] = jnp.where(s < count, vs[s], patch[s, c, :, at])
        return 0

    lax.fori_loop(0, 8, body, 0)


def fine_pack(FS, PS):
    shape = (16, 128)
    lane = lanes(shape)
    for g in range(4):
        outs = [jnp.zeros(shape, F32) for _ in range(4)]
        for k in range(8):
            q = 8 * g + k
            if q < 30:
                m = FS[q // 5, q % 5, pl.ds(0, 16, 2), :] + FS[q // 5, q % 5, pl.ds(1, 16, 2), :]
                m = m + roll(m, -1, 1)
                for s in range(4):
                    piece = pick(m, 32 * s + 2 * (lane % 16))
                    outs[s] = jnp.where(lane // 16 == k, piece, outs[s])
        for s in range(4):
            PS[s, pl.ds(16 * g, 16), :] = outs[s]


def build_shells(field, sides, planes, PZ):
    shape = (16, 128)
    lane = lanes(shape)
    zeros = jnp.zeros(shape, F32)
    T = [zeros] * 10
    for x in range(16):
        here = lane % 16 == x
        for c in range(5):
            U = field[c, x, 0:16, :]
            T[c] = jnp.where(here, roll(U, x + 1, 1), T[c])
            T[5 + c] = jnp.where(here, roll(U, x - 16, 1), T[5 + c])
    z0 = jnp.concatenate(T[:8], axis=0).T
    z1 = jnp.concatenate(T[8:] + [zeros] * 6, axis=0).T
    for zb in range(8):
        PZ[zb, 0:16] = z0[16 * zb : 16 * zb + 16]
    for g in range(1, 4):
        vs = []
        for k in range(8):
            q = 8 * g + k
            vs.append(zeros if q < 10 or q >= 30 else sides[q // 5 - 2][q % 5])
        vs = block_transpose(vs, 16)
        for zb in range(8):
            value = vs[zb]
            if g == 1:
                value = jnp.where(lane < 32, z1[16 * zb : 16 * zb + 16], value)
            PZ[zb, 16 * g : 16 * g + 16] = value


def coarse_kernel(me_ref, anchors, counts, field, xlo, xhi, ylo, yhi, adv, FP, dense, C, Q, FX, PZ):
    owners = dense.shape[0]
    for c in range(5):
        for x in range(16):
            C[c, x, 0:16] = field[c, x]
            C[c, x, 16:24] = jnp.broadcast_to(yhi[c, x : x + 1], (8, 128))
        C[c, 16, 0:16] = xhi[c]
        C[c, 16, 16:24] = xhi[c, 8:16]

    def cells(x, _):
        for k, q in enumerate(primitives([C[c, x] for c in range(5)])):
            Q[k, x] = q
        return 0

    lax.fori_loop(0, 17, cells, 0)
    R = [field[c, 0] for c in range(5)]
    L = [xlo[c] for c in range(5)]
    F = face_flux(L, primitives(L), R, primitives(R), 0)
    for c in range(5):
        FP[2, c] = F[c]
        FX[c] = F[c]
    R = [field[c, :, 0, :] for c in range(5)]
    L = [ylo[c] for c in range(5)]
    F = face_flux(L, primitives(L), R, primitives(R), 1)
    for c in range(5):
        FP[4, c] = F[c]
        FP[0, c] = jnp.zeros((16, 128), F32)
    lane = lanes((16, 128)) % 16
    row = lax.broadcasted_iota(jnp.int32, (16, 128), 0)

    def body(x, _):
        U24 = [C[c, x] for c in range(5)]
        S24 = [Q[k, x] for k in range(7)]
        U, S = [a[0:16] for a in U24], [a[0:16] for a in S24]
        F = face_flux(U, S, [roll(a, -1, 1) for a in U], [roll(a, -1, 1) for a in S], 2)
        total = []
        for c in range(5):
            FP[0, c] = jnp.where(lane == x, pltpu.roll(F[c], x + 1, 1), FP[0, c])
            total.append(F[c] - roll(F[c], 1, 1))
        F = face_flux(U, S, [roll(a, -1, 0)[0:16] for a in U24], [roll(a, -1, 0)[0:16] for a in S24], 1)
        for c in range(5):
            before = jnp.where(row == 0, FP[4, c, pl.ds(x, 1), :], roll(F[c], 1, 0))
            total[c] = total[c] + (F[c] - before)
            FP[5, c, pl.ds(x, 1), :] = F[c][15:16]
        F = face_flux(
            U, S, [C[c, x + 1, 0:16] for c in range(5)], [Q[k, x + 1, 0:16] for k in range(7)], 0
        )
        for c in range(5):
            adv[c, x] = U[c] - COURANT * (total[c] + (F[c] - FX[c]))
            FX[c] = F[c]
        return 0

    lax.fori_loop(0, 16, body, 0)
    for c in range(5):
        FP[3, c] = FX[c]
        FP[1, c] = roll(FP[0, c], -16, 1)
    shell_kernel(me_ref, anchors, counts, field, xlo, xhi, ylo, yhi, dense, PZ)


def shell_kernel(me_ref, anchors, counts, field, xlo, xhi, ylo, yhi, dense, PZ):
    owners = dense.shape[0]
    me = me_ref[0]
    build_shells(field, (xlo, xhi, ylo, yhi), None, PZ)
    for o in range(owners):
        block = jnp.int32(0)
        for s in range(4):
            at = 12 * o + 3 * s
            mine = jnp.logical_and(s < counts[o], anchors[at] == 16 * me)
            block = block + jnp.where(mine, anchors[at + 2] // 16, 0)
        dense[o] = PZ[block]


def interior_kernel(patch, W, B, Q, FY):
    fine_load(patch, W, Q)
    fine_interior(W, Q, FY, B)


def fine_kernel(
    me_ref, anchors, counts, patch, W_in, B, old, new, out, outgoing, W, Q, FY, S, FB, FS, PS, B2
):
    owners = outgoing.shape[0]
    me = me_ref[0]
    count = counts[me]
    sources = [anchors[12 * me + 3 * s] // 16 for s in range(4)]

    def copy(y, _):
        for c in range(5):
            W[c, y] = W_in[c, y]
        return 0

    lax.fori_loop(0, 32, copy, 0)
    fine_shells(old, sources, S)
    fine_boundary(B, S, FB, FS, W, True)
    fine_again(W, FB, Q)
    fine_interior(W, Q, FY, B2)
    fine_shells(old, sources, S, new)
    fine_boundary(B2, S, FB, FS, W, False)
    fine_pack(FS, PS)
    for i in range(owners):
        slot = jnp.int32(0)
        for s in range(1, 4):
            slot = jnp.where(jnp.logical_and(s < count, sources[s] == i), s, slot)
        outgoing[i] = PS[slot]
    fine_store(W, FB, patch, count, out)


def reflux_kernel(me_ref, anchors, counts, adv, FP, got, out, D):
    owners = got.shape[0]
    me = me_ref[0]
    shape = (16, 128)
    lane = lanes(shape)
    owner = [jnp.int32(0)] * 8
    present = [jnp.int32(0)] * 8
    for o in range(owners):
        for s in range(4):
            at = 12 * o + 3 * s
            mine = jnp.logical_and(s < counts[o], anchors[at] == 16 * me)
            block = anchors[at + 2] // 16
            for zb in range(8):
                hit = jnp.logical_and(mine, block == zb)
                owner[zb] = jnp.where(hit, o, owner[zb])
                present[zb] = jnp.where(hit, 1, present[zb])
    live = jnp.zeros(shape, jnp.int32)
    for zb in range(8):
        live = jnp.where(lane // 16 == zb, present[zb], live)
    live = live > 0
    delta = {}
    for g in range(4):
        vs = [got[owner[zb], pl.ds(16 * g, 16), :] for zb in range(8)]
        if g < 2:
            turned = jnp.concatenate(vs, axis=0).T
        if g > 0:
            vs = block_transpose(vs, 16)
        for k in range(8):
            q = 8 * g + k
            if q < 30:
                e, c = q // 5, q % 5
                mean = 0.125 * (turned[16 * k : 16 * k + 16] if q < 10 else vs[k])
                value = COURANT * (FP[e, c] - mean) if e % 2 == 0 else COURANT * (mean - FP[e, c])
                value = jnp.where(live, value, 0.0)
                if e < 2:
                    delta[e, c] = value
                else:
                    D[e - 2, c] = value
    for c in range(5):
        for x in range(16):
            value = adv[c, x]
            value = value + jnp.where(lane % 16 == 15, roll(delta[0, c], -(x + 1), 1), 0.0)
            value = value + jnp.where(lane % 16 == 0, roll(delta[1, c], 16 - x, 1), 0.0)
            out[c, x] = value


def rim_kernel(field, x_up, x_down, y_up, y_down, out):
    out[...] = field[...]
    for c in range(5):
        out[c, 15] = out[c, 15] + x_up[c]
        out[c, 0] = out[c, 0] + x_down[c]
        out[c, :, 15, :] = out[c, :, 15, :] + y_up[c]
        out[c, :, 0, :] = out[c, :, 0, :] + y_down[c]


def call(kernel, outs, n_scalar, n_vector, scratch=(), flops=1000000):
    return pl.pallas_call(
        kernel,
        out_shape=[jax.ShapeDtypeStruct(shape, F32) for shape in outs],
        in_specs=[pl.BlockSpec(memory_space=pltpu.SMEM)] * n_scalar
        + [pl.BlockSpec(memory_space=pltpu.VMEM)] * n_vector,
        out_specs=[pl.BlockSpec(memory_space=pltpu.VMEM)] * len(outs),
        scratch_shapes=[pltpu.VMEM(shape, F32) for shape in scratch],
        compiler_params=pltpu.CompilerParams(vmem_limit_bytes=VMEM_LIMIT),
        cost_estimate=pl.CostEstimate(flops=flops, bytes_accessed=4000000, transcendentals=0),
    )


def shift(x, axis, up):
    count = lax.axis_size(axis)
    pairs = [(i, (i + 1) % count) for i in range(count)]
    if not up:
        pairs = [(b, a) for a, b in pairs]
    return lax.ppermute(x, axis, pairs)


def halos(field):
    return (
        shift(field[:, 15], "gx", True),
        shift(field[:, 0], "gx", False),
        shift(field[:, :, 15], "gy", True),
        shift(field[:, :, 0], "gy", False),
    )


def exchange(x):
    return lax.all_to_all(x, "gx", split_axis=0, concat_axis=0, tiled=True)


def shards(coarse_state, patch_state, patch_anchor, patch_count):
    owners = lax.axis_size("gx")
    me = lax.axis_index("gx").astype(jnp.int32).reshape(1)
    anchors = patch_anchor.reshape(-1)
    counts = patch_count.reshape(-1)
    meta = (me, anchors, counts)
    patch = patch_state.reshape(4, 5, 32, 1024)
    cube = (5, 32, 32, 128)
    prim = (7, 32, 32, 128)
    planes = (6, 5, 32, 128)
    field = (5, 16, 16, 128)
    dense = (owners, 64, 128)

    W, B = call(interior_kernel, [cube, planes], 0, 1, [prim, (5, 32, 128)], 50000000)(patch)
    sides = halos(coarse_state)
    advanced, FP, dense_old = call(
        coarse_kernel,
        [field, (6, 5, 16, 128), dense],
        3,
        5,
        [(5, 17, 24, 128), (7, 17, 24, 128), (5, 16, 128), (8, 64, 128)],
        10000000,
    )(*meta, coarse_state, *sides)
    old = exchange(dense_old)
    sides = halos(advanced)
    (dense_new,) = call(shell_kernel, [dense], 3, 5, [(8, 64, 128)])(*meta, advanced, *sides)
    new = exchange(dense_new)
    out, outgoing = call(
        fine_kernel,
        [(4, 5, 32, 1024), dense],
        3,
        5,
        [cube, prim, (5, 32, 128), planes, planes, planes, (4, 64, 128), planes],
        50000000,
    )(*meta, patch, W, B, old, new)
    arrived = exchange(outgoing)
    field_next, D = call(reflux_kernel, [field, (4, 5, 16, 128)], 3, 3)(
        *meta, advanced, FP, arrived
    )
    (coarse_next,) = call(rim_kernel, [field], 0, 5)(
        field_next,
        shift(D[0], "gx", False),
        shift(D[1], "gx", True),
        shift(D[2], "gy", False),
        shift(D[3], "gy", True),
    )
    return (coarse_next, out.reshape(patch_state.shape))


def solution(mesh):
    in_specs = (
        P(None, "gx", "gy", None),
        P("gx", "gy", None, None, None, None),
        P(None, "gy", None, None),
        P(None, "gy"),
    )
    out_specs = (P(None, "gx", "gy", None), P("gx", "gy", None, None, None, None))
    return jax.shard_map(shards, mesh=mesh, in_specs=in_specs, out_specs=out_specs, check_vma=False)
```

time: 1900 us -> 141 us (0.07)
  local copies, waits for them, and re-layouts: 1400 us -> 9.7 us
  other arithmetic: 352 us -> 0 us
  Pallas kernels: 0 us -> 67.6 us
  loops' own time: 35.7 us -> 0 us
  waiting for transfers between devices: 43.2 us -> 8.85 us
    scatter x50 -> x0, local copies, waits for them, and re-layouts: 881 us -> none  [the longest x8 258 us: advance(): padded = padded.at[:, 1:-1, 1:-1, -1].set(refined[:, 5])]
    reshape x64 -> x1, local copies, waits for them, and re-layouts: 132 us -> 0.73 us  [shards(): anchors = patch_anchor.reshape(-1)]
    sub x36 -> x0, other arithmetic: 93.2 us -> none  [the longest x27 58.9 us: face_flux(): star_press - (value_left + value_right + speed_right - speed_left) / (slo...]
    concatenate x29 -> x0, other arithmetic: 93 us -> none  [the longest x16 75.6 us: advance(): padded = jnp.pad(block_cells, ((0, 0), (1, 1), (1, 1), (1, 1)), mode='edge')]
    another operation x93 -> x0, local copies, waits for them, and re-layouts: 89.9 us -> none
    pallas_call x0 -> x6, Pallas kernels: none -> 67.6 us  [the longest x1 31.9 us: shards(): call(fine_kernel, [(4, 5, 32, 1024), dense], 3, 5, [cube, prim, (5, 32, 1...]
    ge x27 -> x0, other arithmetic: 61.5 us -> none  [face_flux(): wave_low >= 0.0]
    gather x28 -> x0, local copies, waits for them, and re-layouts: 58.6 us -> none  [the longest x16 29.5 us: band(): return lax.dynamic_slice_in_dim(plane, z_first, half_cells, 2)]
  transfers between devices with their start and end apart: 16 -> 14, of which waited for: 3 -> 3; matrix products, arithmetic and copies ran while one was open for 48% -> 3% of each run, Pallas kernels for 0% -> 15%
where the time goes in v1:
time: 141 us; the launch traced here: 140 us
  Pallas kernels  67.6 us (48%)
  starting transfers between devices  35.4 us (25%)
  blocking collectives  17.5 us (12%)
  local copies, waits for them, and re-layouts  9.7 us (7%)
  waiting for transfers between devices  8.85 us (6%)
    pallas_call x1, Pallas kernels, shards(): call(fine_kernel, [(4, 5, 32, 1024), dense], 3, 5, [cube, prim, (5, 32, 1...  31.9 us
    ppermute x12, starting transfers between devices, shift(): return lax.ppermute(x, axis, pairs)  25 us
    pallas_call x1, Pallas kernels, shards(): call(interior_kernel, [cube, planes], 0, 1, [prim, (5, 32, 128)], 50000000)  17.6 us
    all_to_all x1, blocking collectives, exchange(): return lax.all_to_all(x, 'gx', split_axis=0, concat_axis=0, tiled=True)  17.5 us
    all_to_all x2, starting transfers between devices, exchange(): return lax.all_to_all(x, 'gx', split_axis=0, concat_axis=0, tiled=True)  10.4 us
    ppermute x12, waiting for transfers between devices, shift(): return lax.ppermute(x, axis, pairs)  8.84 us
    pallas_call x1, Pallas kernels, shards(): call(coarse_kernel, [field, (6, 5, 16, 128), dense], 3, 5, [(5, 17, 24, 1...  8.14 us
    pallas_call x1, Pallas kernels, shards(): call(reflux_kernel, [field, (4, 5, 16, 128)], 3, 3)  4.64 us
  transfers between devices with their start and end apart: 14, of which 3 were waited for; matrix products, arithmetic and copies ran while one was open for 3% of the time, Pallas kernels for 15%

profile of v1, /device:TPU:0, one launch (start us, length us, event | category | flops | bytes accessed | tf_op | source)
XLA Modules:
  0.0 139.7 jit_solution(4035269462482208619)
XLA Ops:
  0.6 0.8 slice_bitcast_fusion.8
  1.4 6.3 %collective-permute-start.1 = (f32[5,16,128]{2,1,0:T(8,128)S(1)}, f32[5,16,128]{2,1,0:T(8,128)S(1)}, u32[]{:S(2)}, u32[]{:S(2)}) collective-permute-start(f32[5,16,128]{2,1,0:T(8,128)S(1)} %get-tuple-element.26), channel_id=1, source_target_pairs={{8,0},{16,8},{24,16},{32,24},{40,32},{48,40},{56,48},{64,56},{72,6... | collective-permute-start | bytes 122888 | tf_op jit(solution)/shard_map/ppermute | solution.py:486
  7.8 1.1 fusion
  8.9 2.9 %collective-permute-start.3 = (f32[5,16,128]{2,1,0:T(8,128)S(1)}, f32[5,16,128]{2,1,0:T(8,128)S(1)}, u32[]{:S(2)}, u32[]{:S(2)}) collective-permute-start(f32[5,16,128]{2,1,0:T(8,128)S(1)} %bitcast.38), channel_id=1, source_target_pairs={{1,0},{2,1},{3,2},{4,3},{5,4},{6,5},{7,6},{0,7},{9,8},{10,9},{11,1... | collective-permute-start | bytes 122888 | tf_op jit(solution)/shard_map/ppermute | solution.py:486
  11.9 0.8 copy.14
  12.7 0.7 reshape.20.anchors
  13.4 1.7 %collective-permute-done.xlo = f32[5,16,128]{2,1,0:T(8,128)S(1)} collective-permute-done((f32[5,16,128]{2,1,0:T(8,128)S(1)}, f32[5,16,128]{2,1,0:T(8,128)S(1)}, u32[]{:S(2)}, u32[]{:S(2)}) %collective-permute-start) | collective-permute-done | bytes 40992 | tf_op jit(solution)/shard_map/ppermute | solution.py:486
  15.1 0.6 copy-done.3
  15.7 0.0 copy-done.4
  15.7 8.1 %shard_map.59 = (f32[5,16,16,128]{3,2,1,0:T(8,128)}, f32[6,5,16,128]{3,2,1,0:T(8,128)}, f32[16,64,128]{2,1,0:T(8,128)}) custom-call(s32[1]{0:T(128)} %bitcast.me_ref, s32[192]{0:T(256)} %reshape.20.anchors, s32[16]{0:T(128)} %bitcast.40, f32[5,16,16,128]{3,2,1,0:T(8,128)} %field.1, f32[5,16,128]{2,1,0:T(8,128)} %copy-done.3, f32[5,16,128]{2,1,0:T(8,128)} %copy-done.2, ...), custom_call_target="tpu_custom_call" | custom-call | flops 10000000 | bytes 4000000 | tf_op jit(solution)/shard_map/pallas_call | solution.py:517
  23.9 5.2 %all-to-all-start = ((f32[16,64,128]{2,1,0:T(8,128)}), f32[16,64,128]{2,1,0:T(8,128)S(1)}, u32[]{:S(2)}, u32[]{:S(2)}) async-start(f32[16,64,128]{2,1,0:T(8,128)} %get-tuple-element.15), calls=%async_computation | async-start | bytes 1048576 | tf_op jit(solution)/shard_map/all_to_all | solution.py:499
  29.0 1.3 copy.21
  30.3 0.8 slice_bitcast_fusion.2
  31.2 5.2 %collective-permute-start.5 = (f32[5,16,128]{2,1,0:T(8,128)S(1)}, f32[5,16,128]{2,1,0:T(8,128)S(1)}, u32[]{:S(2)}, u32[]{:S(2)}) collective-permute-start(f32[5,16,128]{2,1,0:T(8,128)S(1)} %get-tuple-element.22), channel_id=1, source_target_pairs={{8,0},{16,8},{24,16},{32,24},{40,32},{48,40},{56,48},{64,56},{72,6... | collective-permute-start | bytes 122888 | tf_op jit(solution)/shard_map/ppermute | solution.py:486
  36.4 2.1 %collective-permute-start.7 = (f32[5,16,128]{2,1,0:T(8,128)S(1)}, f32[5,16,128]{2,1,0:T(8,128)S(1)}, u32[]{:S(2)}, u32[]{:S(2)}) collective-permute-start(f32[5,16,128]{2,1,0:T(8,128)S(1)} %get-tuple-element.20), channel_id=1, source_target_pairs={{1,0},{2,1},{3,2},{4,3},{5,4},{6,5},{7,6},{0,7},{9,8},{10,9},{11,1... | collective-permute-start | bytes 122888 | tf_op jit(solution)/shard_map/ppermute | solution.py:486
  38.6 5.2 %collective-permute-done.4.xlo = f32[5,16,128]{2,1,0:T(8,128)S(1)} collective-permute-done((f32[5,16,128]{2,1,0:T(8,128)S(1)}, f32[5,16,128]{2,1,0:T(8,128)S(1)}, u32[]{:S(2)}, u32[]{:S(2)}) %collective-permute-start.4) | collective-permute-done | bytes 40992 | tf_op jit(solution)/shard_map/ppermute | solution.py:486
  43.8 0.6 copy-done.11
  44.4 0.6 copy-done.13
  45.0 3.2 %shard_map.61 = f32[16,64,128]{2,1,0:T(8,128)} custom-call(s32[1]{0:T(128)} %bitcast.me_ref, s32[192]{0:T(256)} %reshape.20.anchors, s32[16]{0:T(128)} %bitcast.41, f32[5,16,16,128]{3,2,1,0:T(8,128)} %get-tuple-element.11.field.adv, f32[5,16,128]{2,1,0:T(8,128)} %copy-done.11, f32[5,16,128]{2,1,0:T(8,128)} %copy-done.10, f32[5,16,128]{2,1,0:T(8,128)} %copy-done.13, ...), custom_call_target="tpu_custom_call" | custom-call | flops 1000000 | bytes 4000000 | tf_op jit(solution)/shard_map/pallas_call | solution.py:527
  48.2 5.3 %all-to-all-start.1 = ((f32[16,64,128]{2,1,0:T(8,128)}), f32[16,64,128]{2,1,0:T(8,128)S(1)}, u32[]{:S(2)}, u32[]{:S(2)}) async-start(f32[16,64,128]{2,1,0:T(8,128)} %shard_map.61), calls=%async_computation.1 | async-start | bytes 1048576 | tf_op jit(solution)/shard_map/all_to_all | solution.py:499
  53.5 17.6 %shard_map.60 = (f32[5,32,32,128]{3,2,1,0:T(8,128)}, f32[6,5,32,128]{3,2,1,0:T(8,128)}) custom-call(f32[4,5,32,1024]{3,2,1,0:T(8,128)} %bitcast.36), custom_call_target="tpu_custom_call" | custom-call | flops 50000000 | bytes 4000000 | tf_op jit(solution)/shard_map/pallas_call | solution.py:515
  71.0 0.8 copy-done.1
  71.8 31.9 %shard_map.62 = (f32[4,5,32,1024]{3,2,1,0:T(8,128)}, f32[16,64,128]{2,1,0:T(8,128)}) custom-call(s32[1]{0:T(128)} %bitcast.me_ref, s32[192]{0:T(256)} %reshape.20.anchors, s32[16]{0:T(128)} %bitcast.42, f32[4,5,32,1024]{3,2,1,0:T(8,128)} %bitcast.37, f32[5,32,32,128]{3,2,1,0:T(8,128)} %get-tuple-element.13.W_in, f32[6,5,32,128]{3,2,1,0:T(8,128)} %get-tuple-element.14.B, ...), custom_call_target="tpu_custom_call" | custom-call | flops 50000000 | bytes 4000000 | tf_op jit(solution)/shard_map/pallas_call | solution.py:529
  103.7 17.5 %all_to_all.15.got = f32[16,64,128]{2,1,0:T(8,128)} all-to-all(f32[16,64,128]{2,1,0:T(8,128)} %get-tuple-element.16), channel_id=1, replica_groups=mesh['gx'=16,'gy'=8] {'gx'}, dimensions={0} | all-to-all | bytes 1048576 | tf_op jit(solution)/shard_map/all_to_all | solution.py:499
  121.2 4.6 %shard_map.63 = (f32[5,16,16,128]{3,2,1,0:T(8,128)}, f32[4,5,16,128]{3,2,1,0:T(8,128)}) custom-call(s32[1]{0:T(128)} %bitcast.me_ref, s32[192]{0:T(256)} %reshape.20.anchors, s32[16]{0:T(128)} %bitcast.43, f32[5,16,16,128]{3,2,1,0:T(8,128)} %get-tuple-element.11.field.adv, f32[6,5,16,128]{3,2,1,0:T(8,128)} %get-tuple-element.12.FP, ...), custom_call_target="tpu_custom_call" | custom-call | flops 1000000 | bytes 4000000 | tf_op jit(solution)/shard_map/pallas_call | solution.py:538
  125.8 0.8 slice_bitcast_fusion.4
  126.7 2.9 %collective-permute-start.10 = (f32[5,16,128]{2,1,0:T(8,128)S(1)}, f32[5,16,128]{2,1,0:T(8,128)S(1)}, u32[]{:S(2)}, u32[]{:S(2)}) collective-permute-start(f32[5,16,128]{2,1,0:T(8,128)S(1)} %get-tuple-element.29), channel_id=1, source_target_pairs={{1,0},{2,1},{3,2},{4,3},{5,4},{6,5},{7,6},{0,7},{9,8},{10,9},{11,1... | collective-permute-start | bytes 122888 | tf_op jit(solution)/shard_map/ppermute | solution.py:486
  129.6 0.6 collective-permute-start.9
  130.2 4.8 %collective-permute-start.8 = (f32[5,16,128]{2,1,0:T(8,128)S(1)}, f32[5,16,128]{2,1,0:T(8,128)S(1)}, u32[]{:S(2)}, u32[]{:S(2)}) collective-permute-start(f32[5,16,128]{2,1,0:T(8,128)S(1)} %get-tuple-element.31), channel_id=1, source_target_pairs={{8,0},{16,8},{24,16},{32,24},{40,32},{48,40},{56,48},{64,56},{72,6... | collective-permute-start | bytes 122888 | tf_op jit(solution)/shard_map/ppermute | solution.py:486
  135.0 2.0 %collective-permute-done.9.x_down = f32[5,16,128]{2,1,0:T(8,128)S(1)} collective-permute-done((f32[5,16,128]{2,1,0:T(8,128)S(1)}, f32[5,16,128]{2,1,0:T(8,128)S(1)}, u32[]{:S(2)}, u32[]{:S(2)}) %collective-permute-start.9) | collective-permute-done | bytes 40992 | tf_op jit(solution)/shard_map/ppermute | solution.py:486
  137.0 0.6 copy-done.8
  137.6 2.1 %shard_map.64 = f32[5,16,16,128]{3,2,1,0:T(8,128)} custom-call(f32[5,16,16,128]{3,2,1,0:T(8,128)} %get-tuple-element.17.field, f32[5,16,128]{2,1,0:T(8,128)} %copy-done.9, f32[5,16,128]{2,1,0:T(8,128)} %copy-done.8, f32[5,16,128]{2,1,0:T(8,128)} %copy-done.7, f32[5,16,128]{2,1,0:T(8,128)} %copy-done.6), custom_call_target="tpu_custom_call" | custom-call | flops 1000000 | bytes 4000000 | tf_op jit(solution)/shard_map/pallas_call | solution.py:541
  (39 shorter events, 0.2 us)
Async XLA Ops:
  1.4 12.0 %collective-permute-start.1 = (f32[5,16,128]{2,1,0:T(8,128)S(1)}, f32[5,16,128]{2,1,0:T(8,128)S(1)}, u32[]{:S(2)}, u32[]{:S(2)}) collective-permute-start(f32[5,16,128]{2,1,0:T(8,128)S(1)} %get-tuple-element.26), channel_id=1, source_target_pairs={{8,0},{16,8},{24,16},{32,24},{40,32},{48,40},{56,48},{64,56},{72,6... | collective-permute-start | bytes 122888 | tf_op jit(solution)/shard_map/ppermute | solution.py:486
  7.8 7.3 %collective-permute-start = (f32[5,16,128]{2,1,0:T(8,128)S(1)}, f32[5,16,128]{2,1,0:T(8,128)S(1)}, u32[]{:S(2)}, u32[]{:S(2)}) collective-permute-start(f32[5,16,128]{2,1,0:T(8,128)S(1)} %get-tuple-element.27), channel_id=1, source_target_pairs={{0,8},{8,16},{16,24},{24,32},{32,40},{40,48},{48,56},{56,64},{64,7... | collective-permute-start | bytes 122888 | tf_op jit(solution)/shard_map/ppermute | solution.py:486
  8.9 6.2 %collective-permute-start.2 = (f32[5,16,128]{2,1,0:T(8,128)S(1)}, f32[5,16,128]{2,1,0:T(8,128)S(1)}, u32[]{:S(2)}, u32[]{:S(2)}) collective-permute-start(f32[5,16,128]{2,1,0:T(8,128)S(1)} %bitcast.39), channel_id=1, source_target_pairs={{0,1},{1,2},{2,3},{3,4},{4,5},{5,6},{6,7},{7,0},{8,9},{9,10},{10,1... | collective-permute-start | bytes 122888 | tf_op jit(solution)/shard_map/ppermute | solution.py:486
  8.9 6.2 %collective-permute-start.3 = (f32[5,16,128]{2,1,0:T(8,128)S(1)}, f32[5,16,128]{2,1,0:T(8,128)S(1)}, u32[]{:S(2)}, u32[]{:S(2)}) collective-permute-start(f32[5,16,128]{2,1,0:T(8,128)S(1)} %bitcast.38), channel_id=1, source_target_pairs={{1,0},{2,1},{3,2},{4,3},{5,4},{6,5},{7,6},{0,7},{9,8},{10,9},{11,1... | collective-permute-start | bytes 122888 | tf_op jit(solution)/shard_map/ppermute | solution.py:486
  13.4 1.7 %copy-start.2 = (f32[5,16,128]{2,1,0:T(8,128)}, f32[5,16,128]{2,1,0:T(8,128)S(1)}, u32[]{:S(2)}) copy-start(f32[5,16,128]{2,1,0:T(8,128)S(1)} %collective-permute-done.1.xhi) | copy-start | bytes 122884
  15.1 0.6 copy-start.3
  15.1 0.6 copy-start.4
  15.1 0.6 copy-start.5
  23.9 24.3 %all-to-all-start = ((f32[16,64,128]{2,1,0:T(8,128)}), f32[16,64,128]{2,1,0:T(8,128)S(1)}, u32[]{:S(2)}, u32[]{:S(2)}) async-start(f32[16,64,128]{2,1,0:T(8,128)} %get-tuple-element.15), calls=%async_computation | async-start | bytes 1048576 | tf_op jit(solution)/shard_map/all_to_all | solution.py:499
  31.2 7.4 %collective-permute-start.5 = (f32[5,16,128]{2,1,0:T(8,128)S(1)}, f32[5,16,128]{2,1,0:T(8,128)S(1)}, u32[]{:S(2)}, u32[]{:S(2)}) collective-permute-start(f32[5,16,128]{2,1,0:T(8,128)S(1)} %get-tuple-element.22), channel_id=1, source_target_pairs={{8,0},{16,8},{24,16},{32,24},{40,32},{48,40},{56,48},{64,56},{72,6... | collective-permute-start | bytes 122888 | tf_op jit(solution)/shard_map/ppermute | solution.py:486
  36.4 7.3 %collective-permute-start.4 = (f32[5,16,128]{2,1,0:T(8,128)S(1)}, f32[5,16,128]{2,1,0:T(8,128)S(1)}, u32[]{:S(2)}, u32[]{:S(2)}) collective-permute-start(f32[5,16,128]{2,1,0:T(8,128)S(1)} %get-tuple-element.23), channel_id=1, source_target_pairs={{0,8},{8,16},{16,24},{24,32},{32,40},{40,48},{48,56},{56,64},{64,7... | collective-permute-start | bytes 122888 | tf_op jit(solution)/shard_map/ppermute | solution.py:486
  36.4 7.3 %collective-permute-start.7 = (f32[5,16,128]{2,1,0:T(8,128)S(1)}, f32[5,16,128]{2,1,0:T(8,128)S(1)}, u32[]{:S(2)}, u32[]{:S(2)}) collective-permute-start(f32[5,16,128]{2,1,0:T(8,128)S(1)} %get-tuple-element.20), channel_id=1, source_target_pairs={{1,0},{2,1},{3,2},{4,3},{5,4},{6,5},{7,6},{0,7},{9,8},{10,9},{11,1... | collective-permute-start | bytes 122888 | tf_op jit(solution)/shard_map/ppermute | solution.py:486
  38.5 5.2 %collective-permute-start.6 = (f32[5,16,128]{2,1,0:T(8,128)S(1)}, f32[5,16,128]{2,1,0:T(8,128)S(1)}, u32[]{:S(2)}, u32[]{:S(2)}) collective-permute-start(f32[5,16,128]{2,1,0:T(8,128)S(1)} %get-tuple-element.21), channel_id=1, source_target_pairs={{0,1},{1,2},{2,3},{3,4},{4,5},{5,6},{6,7},{7,0},{8,9},{9,10},{10,1... | collective-permute-start | bytes 122888 | tf_op jit(solution)/shard_map/ppermute | solution.py:486
  38.5 5.2 %copy-start.10 = (f32[5,16,128]{2,1,0:T(8,128)}, f32[5,16,128]{2,1,0:T(8,128)S(1)}, u32[]{:S(2)}) copy-start(f32[5,16,128]{2,1,0:T(8,128)S(1)} %collective-permute-done.5.xhi) | copy-start | bytes 122884
  43.7 0.6 copy-start.11
  43.7 0.6 copy-start.12
  44.4 0.6 copy-start.13
  48.2 22.9 %copy-start = (f32[16,64,128]{2,1,0:T(8,128)}, f32[16,64,128]{2,1,0:T(8,128)S(1)}, u32[]{:S(2)}) copy-start(f32[16,64,128]{2,1,0:T(8,128)S(1)} %all-to-all-done.old) | copy-start | bytes 1572868
  48.2 22.9 %all-to-all-start.1 = ((f32[16,64,128]{2,1,0:T(8,128)}), f32[16,64,128]{2,1,0:T(8,128)S(1)}, u32[]{:S(2)}, u32[]{:S(2)}) async-start(f32[16,64,128]{2,1,0:T(8,128)} %shard_map.61), calls=%async_computation.1 | async-start | bytes 1048576 | tf_op jit(solution)/shard_map/all_to_all | solution.py:499
  71.0 0.8 copy-start.1
  126.7 8.3 %collective-permute-start.11 = (f32[5,16,128]{2,1,0:T(8,128)S(1)}, f32[5,16,128]{2,1,0:T(8,128)S(1)}, u32[]{:S(2)}, u32[]{:S(2)}) collective-permute-start(f32[5,16,128]{2,1,0:T(8,128)S(1)} %get-tuple-element.28), channel_id=1, source_target_pairs={{0,1},{1,2},{2,3},{3,4},{4,5},{5,6},{6,7},{7,0},{8,9},{9,10},{10,1... | collective-permute-start | bytes 122888 | tf_op jit(solution)/shard_map/ppermute | solution.py:486
  126.7 8.3 %collective-permute-start.10 = (f32[5,16,128]{2,1,0:T(8,128)S(1)}, f32[5,16,128]{2,1,0:T(8,128)S(1)}, u32[]{:S(2)}, u32[]{:S(2)}) collective-permute-start(f32[5,16,128]{2,1,0:T(8,128)S(1)} %get-tuple-element.29), channel_id=1, source_target_pairs={{1,0},{2,1},{3,2},{4,3},{5,4},{6,5},{7,6},{0,7},{9,8},{10,9},{11,1... | collective-permute-start | bytes 122888 | tf_op jit(solution)/shard_map/ppermute | solution.py:486
  129.6 7.3 %collective-permute-start.9 = (f32[5,16,128]{2,1,0:T(8,128)S(1)}, f32[5,16,128]{2,1,0:T(8,128)S(1)}, u32[]{:S(2)}, u32[]{:S(2)}) collective-permute-start(f32[5,16,128]{2,1,0:T(8,128)S(1)} %get-tuple-element.30), channel_id=1, source_target_pairs={{0,8},{8,16},{16,24},{24,32},{32,40},{40,48},{48,56},{56,64},{64,7... | collective-permute-start | bytes 122888 | tf_op jit(solution)/shard_map/ppermute | solution.py:486
  130.2 6.8 %collective-permute-start.8 = (f32[5,16,128]{2,1,0:T(8,128)S(1)}, f32[5,16,128]{2,1,0:T(8,128)S(1)}, u32[]{:S(2)}, u32[]{:S(2)}) collective-permute-start(f32[5,16,128]{2,1,0:T(8,128)S(1)} %get-tuple-element.31), channel_id=1, source_target_pairs={{8,0},{16,8},{24,16},{32,24},{40,32},{48,40},{56,48},{64,56},{72,6... | collective-permute-start | bytes 122888 | tf_op jit(solution)/shard_map/ppermute | solution.py:486
  135.0 2.0 %copy-start.6 = (f32[5,16,128]{2,1,0:T(8,128)}, f32[5,16,128]{2,1,0:T(8,128)S(1)}, u32[]{:S(2)}) copy-start(f32[5,16,128]{2,1,0:T(8,128)S(1)} %collective-permute-done.11.y_down) | copy-start | bytes 122884
  135.0 2.0 %copy-start.7 = (f32[5,16,128]{2,1,0:T(8,128)}, f32[5,16,128]{2,1,0:T(8,128)S(1)}, u32[]{:S(2)}) copy-start(f32[5,16,128]{2,1,0:T(8,128)S(1)} %collective-permute-done.10.y_up) | copy-start | bytes 122884
  137.0 0.6 copy-start.8
  137.0 0.6 copy-start.9

commit v2 on v1

--- a/solution.py
+++ b/solution.py
@@ -8,6 +8,7 @@
 COURANT = 0.12
 VMEM_LIMIT = 56 * 1024 * 1024
 F32 = jnp.float32
+MESH = pl.DeviceIdType.MESH
 
 
 def rcp(x):
@@ -125,11 +126,8 @@
     lax.fori_loop(0, 8, body, 0)
 
 
-def fine_interior(W, Q, FY, B):
+def fine_edges(W, FY, B):
     shape = (32, 128)
-    row = lax.broadcasted_iota(jnp.int32, shape, 0)
-    lane = lanes(shape) % 32
-    keep_x, keep_z = row < 31, lane < 31
     for c in range(5):
         FY[c] = jnp.zeros(shape, F32)
         B[2, c] = W[c, :, 0, :]
@@ -139,6 +137,13 @@
         B[0, c] = W[c, 0]
         B[1, c] = W[c, 0]
 
+
+def fine_interior(W, Q, FY, B, first, last):
+    shape = (32, 128)
+    row = lax.broadcasted_iota(jnp.int32, shape, 0)
+    lane = lanes(shape) % 32
+    keep_x, keep_z = row < 31, lane < 31
+
     def body(y, _):
         up = jnp.minimum(y + 1, 31)
         U = [W[c, y] for c in range(5)]
@@ -164,7 +169,7 @@
             W[c, y] = U[c] - COURANT * total[c]
         return 0
 
-    lax.fori_loop(0, 32, body, 0)
+    lax.fori_loop(first, last, body, 0)
 
 
 def fine_shells(got, sources, S, mix=None):
@@ -304,8 +309,7 @@
             PZ[zb, 16 * g : 16 * g + 16] = value
 
 
-def coarse_kernel(me_ref, anchors, counts, field, xlo, xhi, ylo, yhi, adv, FP, dense, C, Q, FX, PZ):
-    owners = dense.shape[0]
+def coarse_step(field, xlo, xhi, ylo, yhi, adv, FP, C, Q, FX):
     for c in range(5):
         for x in range(16):
             C[c, x, 0:16] = field[c, x]
@@ -360,30 +364,119 @@
     for c in range(5):
         FP[3, c] = FX[c]
         FP[1, c] = roll(FP[0, c], -16, 1)
-    shell_kernel(me_ref, anchors, counts, field, xlo, xhi, ylo, yhi, dense, PZ)
-
-
-def shell_kernel(me_ref, anchors, counts, field, xlo, xhi, ylo, yhi, dense, PZ):
-    owners = dense.shape[0]
-    me = me_ref[0]
-    build_shells(field, (xlo, xhi, ylo, yhi), None, PZ)
+
+
+def in_pencil(anchors, counts, me, o, s):
+    at = 12 * o + 3 * s
+    return jnp.logical_and(s < counts[o], anchors[at] == 16 * me), anchors[at + 2] // 16
+
+
+def pack_shells(anchors, counts, me, owners, field, sides, PZ, dense):
+    build_shells(field, sides, None, PZ)
     for o in range(owners):
         block = jnp.int32(0)
         for s in range(4):
-            at = 12 * o + 3 * s
-            mine = jnp.logical_and(s < counts[o], anchors[at] == 16 * me)
-            block = block + jnp.where(mine, anchors[at + 2] // 16, 0)
+            mine, zb = in_pencil(anchors, counts, me, o, s)
+            block = block + jnp.where(mine, zb, 0)
         dense[o] = PZ[block]
 
 
-def interior_kernel(patch, W, B, Q, FY):
+class Place:
+    def __init__(self):
+        self.i, self.j = lax.axis_index("gx"), lax.axis_index("gy")
+        self.ni, self.nj = lax.axis_size("gx"), lax.axis_size("gy")
+
+    def along_x(self, d):
+        return (lax.rem(self.i + (d + self.ni), self.ni), self.j)
+
+    def along_y(self, d):
+        return (self.i, lax.rem(self.j + (d + self.nj), self.nj))
+
+    def greet(self):
+        barrier = pltpu.get_barrier_semaphore()
+        for d in range(1, self.ni):
+            pl.semaphore_signal(barrier, inc=1, device_id=self.along_x(d), device_id_type=MESH)
+        for d in (1, -1):
+            pl.semaphore_signal(barrier, inc=1, device_id=self.along_y(d), device_id_type=MESH)
+
+    def greeted(self):
+        pl.semaphore_wait(pltpu.get_barrier_semaphore(), self.ni + 1)
+
+    def send(self, src, dst, send_sem, recv_sem, to):
+        copy = pltpu.make_async_remote_copy(
+            src_ref=src,
+            dst_ref=dst,
+            send_sem=send_sem,
+            recv_sem=recv_sem,
+            device_id=to,
+            device_id_type=MESH,
+        )
+        copy.start()
+        return copy
+
+    def neighbours(self, planes, sides, sems):
+        to = (self.along_x(1), self.along_x(-1), self.along_y(1), self.along_y(-1))
+        return [
+            self.send(planes[k], sides[k], sems.at[0, k], sems.at[1, k], to[k]) for k in range(4)
+        ]
+
+    def exchange(self, dense, got, sems):
+        got[self.i] = dense[self.i]
+        copies = []
+        for d in range(1, self.ni):
+            to = self.along_x(d)
+            copies.append(
+                self.send(dense.at[to[0]], got.at[self.i], sems.at[0, d], sems.at[1, d], to)
+            )
+        return copies
+
+
+def wait(copies):
+    for copy in copies:
+        copy.wait()
+
+
+def edge_planes(field, edges):
+    for c in range(5):
+        edges[0, c] = field[c, :, 15, :]
+        edges[1, c] = field[c, :, 0, :]
+    return (field.at[:, 15], field.at[:, 0], edges.at[0], edges.at[1])
+
+
+def first_kernel(
+    anchors, counts, patch, field, W, B, S1, S2, adv, FP,
+    Q, FY, C, CQ, FX, PZ, dense_old, dense_new, got_old, got_new, edges, sides, near_sems, far_sems,
+):
+    place = Place()
+    me = place.i
+    sources = [anchors[12 * me + 3 * s] // 16 for s in range(4)]
+    place.greet()
     fine_load(patch, W, Q)
-    fine_interior(W, Q, FY, B)
-
-
-def fine_kernel(
-    me_ref, anchors, counts, patch, W_in, B, old, new, out, outgoing, W, Q, FY, S, FB, FS, PS, B2
-):
+    fine_edges(W, FY, B)
+    planes = edge_planes(field, edges.at[0])
+    old = [sides.at[0, k] for k in range(4)]
+    new = [sides.at[1, k] for k in range(4)]
+    place.greeted()
+    near = place.neighbours(planes, old, near_sems.at[0])
+    fine_interior(W, Q, FY, B, 0, 6)
+    wait(near)
+    pack_shells(anchors, counts, me, place.ni, field, old, PZ, dense_old)
+    far_old = place.exchange(dense_old, got_old, far_sems.at[0])
+    coarse_step(field, *old, adv, FP, C, CQ, FX)
+    planes = edge_planes(adv, edges.at[1])
+    near = place.neighbours(planes, new, near_sems.at[1])
+    fine_interior(W, Q, FY, B, 6, 14)
+    wait(near)
+    pack_shells(anchors, counts, me, place.ni, adv, new, PZ, dense_new)
+    far_new = place.exchange(dense_new, got_new, far_sems.at[1])
+    fine_interior(W, Q, FY, B, 14, 32)
+    wait(far_old)
+    fine_shells(got_old, sources, S1)
+    wait(far_new)
+    fine_shells(got_old, sources, S2, got_new)
+
+
+def fine_kernel(anchors, counts, me_ref, patch, W_in, B, S1, S2, out, outgoing, W, Q, FY, FB, FS, PS, B2):
     owners = outgoing.shape[0]
     me = me_ref[0]
     count = counts[me]
@@ -395,12 +488,11 @@
         return 0
 
     lax.fori_loop(0, 32, copy, 0)
-    fine_shells(old, sources, S)
-    fine_boundary(B, S, FB, FS, W, True)
+    fine_boundary(B, S1, FB, FS, W, True)
     fine_again(W, FB, Q)
-    fine_interior(W, Q, FY, B2)
-    fine_shells(old, sources, S, new)
-    fine_boundary(B2, S, FB, FS, W, False)
+    fine_edges(W, FY, B2)
+    fine_interior(W, Q, FY, B2, 0, 32)
+    fine_boundary(B2, S2, FB, FS, W, False)
     fine_pack(FS, PS)
     for i in range(owners):
         slot = jnp.int32(0)
@@ -410,18 +502,14 @@
     fine_store(W, FB, patch, count, out)
 
 
-def reflux_kernel(me_ref, anchors, counts, adv, FP, got, out, D):
-    owners = got.shape[0]
-    me = me_ref[0]
+def reflux(anchors, counts, me, owners, adv, FP, got, out, D):
     shape = (16, 128)
     lane = lanes(shape)
     owner = [jnp.int32(0)] * 8
     present = [jnp.int32(0)] * 8
     for o in range(owners):
         for s in range(4):
-            at = 12 * o + 3 * s
-            mine = jnp.logical_and(s < counts[o], anchors[at] == 16 * me)
-            block = anchors[at + 2] // 16
+            mine, block = in_pencil(anchors, counts, me, o, s)
             for zb in range(8):
                 hit = jnp.logical_and(mine, block == zb)
                 owner[zb] = jnp.where(hit, o, owner[zb])
@@ -456,47 +544,37 @@
             out[c, x] = value
 
 
-def rim_kernel(field, x_up, x_down, y_up, y_down, out):
-    out[...] = field[...]
-    for c in range(5):
-        out[c, 15] = out[c, 15] + x_up[c]
-        out[c, 0] = out[c, 0] + x_down[c]
-        out[c, :, 15, :] = out[c, :, 15, :] + y_up[c]
-        out[c, :, 0, :] = out[c, :, 0, :] + y_down[c]
-
-
-def call(kernel, outs, n_scalar, n_vector, scratch=(), flops=1000000):
+def last_kernel(
+    anchors, counts, outgoing, adv, FP, out, got, D, rims, near_sems, far_sems
+):
+    place = Place()
+    place.greet()
+    place.greeted()
+    wait(place.exchange(outgoing, got, far_sems))
+    reflux(anchors, counts, place.i, place.ni, adv, FP, got, out, D)
+    planes = [D.at[1], D.at[0], D.at[3], D.at[2]]
+    wait(place.neighbours(planes, [rims.at[k] for k in range(4)], near_sems))
+    for c in range(5):
+        out[c, 0] = out[c, 0] + rims[0, c]
+        out[c, 15] = out[c, 15] + rims[1, c]
+        out[c, :, 0, :] = out[c, :, 0, :] + rims[2, c]
+        out[c, :, 15, :] = out[c, :, 15, :] + rims[3, c]
+
+
+def call(kernel, outs, n_scalar, n_vector, scratch=(), collective=None):
+    more = {}
+    if collective is not None:
+        more = {"collective_id": collective, "has_side_effects": True}
     return pl.pallas_call(
         kernel,
         out_shape=[jax.ShapeDtypeStruct(shape, F32) for shape in outs],
         in_specs=[pl.BlockSpec(memory_space=pltpu.SMEM)] * n_scalar
         + [pl.BlockSpec(memory_space=pltpu.VMEM)] * n_vector,
         out_specs=[pl.BlockSpec(memory_space=pltpu.VMEM)] * len(outs),
-        scratch_shapes=[pltpu.VMEM(shape, F32) for shape in scratch],
-        compiler_params=pltpu.CompilerParams(vmem_limit_bytes=VMEM_LIMIT),
-        cost_estimate=pl.CostEstimate(flops=flops, bytes_accessed=4000000, transcendentals=0),
+        scratch_shapes=[pltpu.VMEM(s, F32) if isinstance(s, tuple) else s for s in scratch],
+        compiler_params=pltpu.CompilerParams(vmem_limit_bytes=VMEM_LIMIT, **more),
+        cost_estimate=pl.CostEstimate(flops=10000000, bytes_accessed=4000000, transcendentals=0),
     )
-
-
-def shift(x, axis, up):
-    count = lax.axis_size(axis)
-    pairs = [(i, (i + 1) % count) for i in range(count)]
-    if not up:
-        pairs = [(b, a) for a, b in pairs]
-    return lax.ppermute(x, axis, pairs)
-
-
-def halos(field):
-    return (
-        shift(field[:, 15], "gx", True),
-        shift(field[:, 0], "gx", False),
-        shift(field[:, :, 15], "gy", True),
-        shift(field[:, :, 0], "gy", False),
-    )
-
-
-def exchange(x):
-    return lax.all_to_all(x, "gx", split_axis=0, concat_axis=0, tiled=True)
 
 
 def shards(coarse_state, patch_state, patch_anchor, patch_count):
@@ -504,47 +582,40 @@
     me = lax.axis_index("gx").astype(jnp.int32).reshape(1)
     anchors = patch_anchor.reshape(-1)
     counts = patch_count.reshape(-1)
-    meta = (me, anchors, counts)
     patch = patch_state.reshape(4, 5, 32, 1024)
     cube = (5, 32, 32, 128)
     prim = (7, 32, 32, 128)
     planes = (6, 5, 32, 128)
     field = (5, 16, 16, 128)
+    side = (5, 16, 128)
     dense = (owners, 64, 128)
-
-    W, B = call(interior_kernel, [cube, planes], 0, 1, [prim, (5, 32, 128)], 50000000)(patch)
-    sides = halos(coarse_state)
-    advanced, FP, dense_old = call(
-        coarse_kernel,
-        [field, (6, 5, 16, 128), dense],
-        3,
-        5,
-        [(5, 17, 24, 128), (7, 17, 24, 128), (5, 16, 128), (8, 64, 128)],
-        10000000,
-    )(*meta, coarse_state, *sides)
-    old = exchange(dense_old)
-    sides = halos(advanced)
-    (dense_new,) = call(shell_kernel, [dense], 3, 5, [(8, 64, 128)])(*meta, advanced, *sides)
-    new = exchange(dense_new)
+    dma = pltpu.SemaphoreType.DMA
+
+    W, B, S1, S2, advanced, FP = call(
+        first_kernel,
+        [cube, planes, planes, planes, field, (6,) + side],
+        2,
+        2,
+        [prim, (5, 32, 128), (5, 17, 24, 128), (7, 17, 24, 128), side, (8, 64, 128)]
+        + [dense] * 4
+        + [(2, 2) + side, (2, 4) + side, dma((2, 2, 4)), dma((2, 2, owners))],
+        0,
+    )(anchors, counts, patch, coarse_state)
     out, outgoing = call(
         fine_kernel,
         [(4, 5, 32, 1024), dense],
         3,
         5,
-        [cube, prim, (5, 32, 128), planes, planes, planes, (4, 64, 128), planes],
-        50000000,
-    )(*meta, patch, W, B, old, new)
-    arrived = exchange(outgoing)
-    field_next, D = call(reflux_kernel, [field, (4, 5, 16, 128)], 3, 3)(
-        *meta, advanced, FP, arrived
-    )
-    (coarse_next,) = call(rim_kernel, [field], 0, 5)(
-        field_next,
-        shift(D[0], "gx", False),
-        shift(D[1], "gx", True),
-        shift(D[2], "gy", False),
-        shift(D[3], "gy", True),
-    )
+        [cube, prim, (5, 32, 128), planes, planes, (4, 64, 128), planes],
+    )(anchors, counts, me, patch, W, B, S1, S2)
+    (coarse_next,) = call(
+        last_kernel,
+        [field],
+        2,
+        3,
+        [dense, (4,) + side, (4,) + side, dma((2, 4)), dma((2, owners))],
+        1,
+    )(anchors, counts, outgoing, advanced, FP)
     return (coarse_next, out.reshape(patch_state.shape))
 
 

time: 141 us -> 90.7 us (0.64)
  starting transfers between devices: 35.4 us -> 0 us
  Pallas kernels: 67.6 us -> 86.3 us
  blocking collectives: 17.5 us -> 0 us
  waiting for transfers between devices: 8.85 us -> 0 us
  local copies, waits for them, and re-layouts: 9.7 us -> 3.52 us
    ppermute x12 -> x0, starting transfers between devices: 25 us -> none  [shift(): return lax.ppermute(x, axis, pairs)]
    pallas_call x5 -> x2, Pallas kernels: 35.7 us -> 55.3 us  [the longest x1 34.6 us: shards(): call(first_kernel, [cube, planes, planes, planes, field, (6,) + side], 2,...]
    all_to_all x1 -> x0, blocking collectives: 17.5 us -> none  [exchange(): return lax.all_to_all(x, 'gx', split_axis=0, concat_axis=0, tiled=True)]
    all_to_all x2 -> x0, starting transfers between devices: 10.4 us -> none  [exchange(): return lax.all_to_all(x, 'gx', split_axis=0, concat_axis=0, tiled=True)]
    ppermute x12 -> x0, waiting for transfers between devices: 8.84 us -> none  [shift(): return lax.ppermute(x, axis, pairs)]
    squeeze x4 -> x0, local copies, waits for them, and re-layouts: 2.48 us -> none  [the longest x2 1.62 us: halos(): field[:, 0]]
    unnamed x29 -> x2, local copies, waits for them, and re-layouts: 4.05 us -> 2.78 us
  transfers between devices with their start and end apart: 14 -> 0, of which waited for: 3 -> 0; matrix products, arithmetic and copies ran while one was open for 3% -> 0% of each run, Pallas kernels for 15% -> 0%
where the time goes in v2:
time: 90.7 us; the launch traced here: 90.4 us
  Pallas kernels  86.3 us (95%)
  local copies, waits for them, and re-layouts  3.52 us (4%)
    pallas_call x1, Pallas kernels, shards(): call(first_kernel, [cube, planes, planes, planes, field, (6,) + side], 2,...  34.6 us
    pallas_call x1, Pallas kernels, shards(): call(fine_kernel, [(4, 5, 32, 1024), dense], 3, 5, [cube, prim, (5, 32, 1...  31 us
    pallas_call x1, Pallas kernels, shards(): call(last_kernel, [field], 2, 3, [dense, (4,) + side, (4,) + side, dma((2...  20.7 us
    unnamed x2, local copies, waits for them, and re-layouts  2.78 us

profile of v2, /device:TPU:0, one launch (start us, length us, event | category | flops | bytes accessed | tf_op | source)
XLA Modules:
  0.0 90.4 jit_solution(2650860590078802576)
XLA Ops:
  0.6 0.8 copy.6
  1.4 0.7 reshape.19.anchors
  2.2 34.6 %shard_map.59 = (f32[5,32,32,128]{3,2,1,0:T(8,128)}, f32[6,5,32,128]{3,2,1,0:T(8,128)}, f32[6,5,32,128]{3,2,1,0:T(8,128)}, f32[6,5,32,128]{3,2,1,0:T(8,128)}, f3...) custom-call(s32[192]{0:T(256)} %reshape.19.anchors, s32[16]{0:T(128)} %bitcast.8, f32[4,5,32,1024]{3,2,1,0:T(8,128)} %bitcast.6, ...), custom_call_target="tpu_custom_call" | custom-call | flops 10000000 | bytes 4000000 | tf_op jit(solution)/shard_map/pallas_call | solution.py:594
  36.8 31.0 %shard_map.60 = (f32[4,5,32,1024]{3,2,1,0:T(8,128)}, f32[16,64,128]{2,1,0:T(8,128)}) custom-call(s32[192]{0:T(256)} %reshape.19.anchors, s32[16]{0:T(128)} %bitcast.9, s32[1]{0:T(128)} %bitcast.1.me_ref, f32[4,5,32,1024]{3,2,1,0:T(8,128)} %bitcast.7, f32[5,32,32,128]{3,2,1,0:T(8,128)} %get-tuple-element.10.W_in, f32[6,5,32,128]{3,2,1,0:T(8,128)} %get-tuple-element.11.B, ...), custom_call_target="tpu_custom_call" | custom-call | flops 10000000 | bytes 4000000 | tf_op jit(solution)/shard_map/pallas_call | solution.py:604
  67.8 20.7 %shard_map.61 = f32[5,16,16,128]{3,2,1,0:T(8,128)} custom-call(s32[192]{0:T(256)} %reshape.19.anchors, s32[16]{0:T(128)} %bitcast.10, f32[16,64,128]{2,1,0:T(8,128)} %get-tuple-element.14.outgoing, f32[5,16,16,128]{3,2,1,0:T(8,128)} %get-tuple-element.15.adv, f32[6,5,16,128]{3,2,1,0:T(8,128)} %get-tuple-element.16.FP), custom_call_target="tpu_custom_call" | custom-call | flops 10000000 | bytes 4000000 | tf_op jit(solution)/shard_map/pallas_call | solution.py:611
  88.5 2.0 %copy.8 = f32[5,16,16,128]{3,2,1,0:T(8,128)} copy(f32[5,16,16,128]{3,2,1,0:T(8,128)} %shard_map.61) | data formatting | bytes 1310720

commit v3 on v2

--- a/solution.py
+++ b/solution.py
@@ -109,7 +109,19 @@
 NORMAL = (2, 2, 0, 0, 1, 1)
 
 
-def fine_load(patch, W, Q):
+def collect(U, y, lane, B):
+    here = lane == y
+    for c in range(5):
+        B[0, c] = jnp.where(here, pltpu.roll(U[c], y, 1), B[0, c])
+        B[1, c] = jnp.where(here, pltpu.roll(U[c], y + 97, 1), B[1, c])
+
+
+def fine_load(patch, W, Q, B):
+    lane = lanes((32, 128)) % 32
+    for c in range(5):
+        B[0, c] = jnp.zeros((32, 128), F32)
+        B[1, c] = jnp.zeros((32, 128), F32)
+
     def body(yg, _):
         at = pl.ds(pl.multiple_of(yg * 128, 128), 128)
         U = [[None] * 5 for _ in range(4)]
@@ -119,6 +131,7 @@
                 W[c, 4 * yg + j] = vs[j]
                 U[j][c] = vs[j]
         for j in range(4):
+            collect(U[j], 4 * yg + j, lane, B)
             for k, q in enumerate(primitives(U[j])):
                 Q[k, 4 * yg + j] = q
         return 0
@@ -134,11 +147,9 @@
         B[3, c] = W[c, :, 31, :]
         B[4, c] = W[c, 0]
         B[5, c] = W[c, 31]
-        B[0, c] = W[c, 0]
-        B[1, c] = W[c, 0]
-
-
-def fine_interior(W, Q, FY, B, first, last):
+
+
+def fine_interior(W, Q, FY, first, last):
     shape = (32, 128)
     row = lax.broadcasted_iota(jnp.int32, shape, 0)
     lane = lanes(shape) % 32
@@ -148,10 +159,6 @@
         up = jnp.minimum(y + 1, 31)
         U = [W[c, y] for c in range(5)]
         S = [Q[k, y] for k in range(7)]
-        here = lane == y
-        for c in range(5):
-            B[0, c] = jnp.where(here, pltpu.roll(U[c], y, 1), B[0, c])
-            B[1, c] = jnp.where(here, pltpu.roll(U[c], y + 97, 1), B[1, c])
         total = []
         F = face_flux(U, S, [roll(a, -1, 1) for a in U], [roll(a, -1, 1) for a in S], 2, keep_z)
         for c in range(5):
@@ -196,7 +203,7 @@
                 S[q // 5, q % 5, pl.ds(1, 16, 2), :] = out
 
 
-def fine_boundary(B, S, FB, FS, W, first):
+def fine_boundary(B, S, FB, FS, first):
     def body(e2, _):
         for side in range(2):
             face = 2 * e2 + side
@@ -219,6 +226,9 @@
         return 0
 
     lax.fori_loop(0, 3, body, 0)
+
+
+def add_boundary(W, FB):
     for c in range(5):
         W[c, :, 0, :] = W[c, :, 0, :] + COURANT * FB[2, c]
         W[c, :, 31, :] = W[c, :, 31, :] - COURANT * FB[3, c]
@@ -231,7 +241,7 @@
     return value - jnp.where(lane == 31, COURANT * pltpu.roll(FB[1, c], 159 - y, 1), 0.0)
 
 
-def fine_again(W, FB, Q):
+def fine_again(W, FB, Q, B):
     lane = lanes((32, 128)) % 32
 
     def body(y, _):
@@ -239,6 +249,7 @@
         for c in range(5):
             U.append(z_boundary(W[c, y], FB, c, y, lane))
             W[c, y] = U[c]
+        collect(U, y, lane, B)
         for k, q in enumerate(primitives(U)):
             Q[k, y] = q
         return 0
@@ -366,19 +377,22 @@
         FP[1, c] = roll(FP[0, c], -16, 1)
 
 
-def in_pencil(anchors, counts, me, o, s):
-    at = 12 * o + 3 * s
-    return jnp.logical_and(s < counts[o], anchors[at] == 16 * me), anchors[at + 2] // 16
-
-
-def pack_shells(anchors, counts, me, owners, field, sides, PZ, dense):
+def owned_blocks(anchors, counts, me, owners):
+    blocks = []
+    for o in range(owners):
+        block = jnp.int32(-1)
+        for s in range(4):
+            at = 12 * o + 3 * s
+            mine = jnp.logical_and(s < counts[o], anchors[at] == 16 * me)
+            block = jnp.where(mine, anchors[at + 2] // 16, block)
+        blocks.append(block)
+    return blocks
+
+
+def pack_shells(blocks, field, sides, PZ, dense):
     build_shells(field, sides, None, PZ)
-    for o in range(owners):
-        block = jnp.int32(0)
-        for s in range(4):
-            mine, zb = in_pencil(anchors, counts, me, o, s)
-            block = block + jnp.where(mine, zb, 0)
-        dense[o] = PZ[block]
+    for o, block in enumerate(blocks):
+        dense[o] = PZ[jnp.maximum(block, 0)]
 
 
 class Place:
@@ -443,77 +457,75 @@
     return (field.at[:, 15], field.at[:, 0], edges.at[0], edges.at[1])
 
 
-def first_kernel(
-    anchors, counts, patch, field, W, B, S1, S2, adv, FP,
-    Q, FY, C, CQ, FX, PZ, dense_old, dense_new, got_old, got_new, edges, sides, near_sems, far_sems,
+def step_kernel(
+    anchors, counts, patch, field, out_field, out,
+    W, Q, B, S1, S2, FB, FS, FY, PS, C, CQ, FX, adv, FP, PZ,
+    dense_old, dense_new, dense_back, got_old, got_new, got_back, edges, D, sides, near_sems, far_sems,
 ):
     place = Place()
     me = place.i
+    count = counts[me]
     sources = [anchors[12 * me + 3 * s] // 16 for s in range(4)]
+    old, new, rims = ([sides.at[n, k] for k in range(4)] for n in range(3))
     place.greet()
-    fine_load(patch, W, Q)
+    planes = edge_planes(field, edges.at[0])
+    blocks = owned_blocks(anchors, counts, me, place.ni)
+    fine_load(patch, W, Q, B)
     fine_edges(W, FY, B)
-    planes = edge_planes(field, edges.at[0])
-    old = [sides.at[0, k] for k in range(4)]
-    new = [sides.at[1, k] for k in range(4)]
     place.greeted()
     near = place.neighbours(planes, old, near_sems.at[0])
-    fine_interior(W, Q, FY, B, 0, 6)
+    fine_interior(W, Q, FY, 0, 6)
     wait(near)
-    pack_shells(anchors, counts, me, place.ni, field, old, PZ, dense_old)
+    pack_shells(blocks, field, old, PZ, dense_old)
     far_old = place.exchange(dense_old, got_old, far_sems.at[0])
     coarse_step(field, *old, adv, FP, C, CQ, FX)
     planes = edge_planes(adv, edges.at[1])
     near = place.neighbours(planes, new, near_sems.at[1])
-    fine_interior(W, Q, FY, B, 6, 14)
+    fine_interior(W, Q, FY, 6, 14)
     wait(near)
-    pack_shells(anchors, counts, me, place.ni, adv, new, PZ, dense_new)
+    pack_shells(blocks, adv, new, PZ, dense_new)
     far_new = place.exchange(dense_new, got_new, far_sems.at[1])
-    fine_interior(W, Q, FY, B, 14, 32)
+    fine_interior(W, Q, FY, 14, 32)
     wait(far_old)
     fine_shells(got_old, sources, S1)
+    fine_boundary(B, S1, FB, FS, True)
+    add_boundary(W, FB)
+    fine_again(W, FB, Q, B)
+    fine_edges(W, FY, B)
     wait(far_new)
     fine_shells(got_old, sources, S2, got_new)
-
-
-def fine_kernel(anchors, counts, me_ref, patch, W_in, B, S1, S2, out, outgoing, W, Q, FY, FB, FS, PS, B2):
-    owners = outgoing.shape[0]
-    me = me_ref[0]
-    count = counts[me]
-    sources = [anchors[12 * me + 3 * s] // 16 for s in range(4)]
-
-    def copy(y, _):
-        for c in range(5):
-            W[c, y] = W_in[c, y]
-        return 0
-
-    lax.fori_loop(0, 32, copy, 0)
-    fine_boundary(B, S1, FB, FS, W, True)
-    fine_again(W, FB, Q)
-    fine_edges(W, FY, B2)
-    fine_interior(W, Q, FY, B2, 0, 32)
-    fine_boundary(B2, S2, FB, FS, W, False)
+    fine_boundary(B, S2, FB, FS, False)
     fine_pack(FS, PS)
-    for i in range(owners):
+    for i in range(place.ni):
         slot = jnp.int32(0)
         for s in range(1, 4):
             slot = jnp.where(jnp.logical_and(s < count, sources[s] == i), s, slot)
-        outgoing[i] = PS[slot]
+        dense_back[i] = PS[slot]
+    back = place.exchange(dense_back, got_back, far_sems.at[2])
+    fine_interior(W, Q, FY, 0, 22)
+    wait(back)
+    reflux(blocks, adv, FP, got_back, out_field, D)
+    near = place.neighbours([D.at[1], D.at[0], D.at[3], D.at[2]], rims, near_sems.at[2])
+    fine_interior(W, Q, FY, 22, 32)
+    add_boundary(W, FB)
     fine_store(W, FB, patch, count, out)
-
-
-def reflux(anchors, counts, me, owners, adv, FP, got, out, D):
+    wait(near)
+    for c in range(5):
+        out_field[c, 0] = out_field[c, 0] + sides[2, 0, c]
+        out_field[c, 15] = out_field[c, 15] + sides[2, 1, c]
+        out_field[c, :, 0, :] = out_field[c, :, 0, :] + sides[2, 2, c]
+        out_field[c, :, 15, :] = out_field[c, :, 15, :] + sides[2, 3, c]
+
+
+def reflux(blocks, adv, FP, got, out, D):
     shape = (16, 128)
     lane = lanes(shape)
     owner = [jnp.int32(0)] * 8
     present = [jnp.int32(0)] * 8
-    for o in range(owners):
-        for s in range(4):
-            mine, block = in_pencil(anchors, counts, me, o, s)
-            for zb in range(8):
-                hit = jnp.logical_and(mine, block == zb)
-                owner[zb] = jnp.where(hit, o, owner[zb])
-                present[zb] = jnp.where(hit, 1, present[zb])
+    for o, block in enumerate(blocks):
+        for zb in range(8):
+            owner[zb] = jnp.where(block == zb, o, owner[zb])
+            present[zb] = jnp.where(block == zb, 1, present[zb])
     live = jnp.zeros(shape, jnp.int32)
     for zb in range(8):
         live = jnp.where(lane // 16 == zb, present[zb], live)
@@ -544,23 +556,6 @@
             out[c, x] = value
 
 
-def last_kernel(
-    anchors, counts, outgoing, adv, FP, out, got, D, rims, near_sems, far_sems
-):
-    place = Place()
-    place.greet()
-    place.greeted()
-    wait(place.exchange(outgoing, got, far_sems))
-    reflux(anchors, counts, place.i, place.ni, adv, FP, got, out, D)
-    planes = [D.at[1], D.at[0], D.at[3], D.at[2]]
-    wait(place.neighbours(planes, [rims.at[k] for k in range(4)], near_sems))
-    for c in range(5):
-        out[c, 0] = out[c, 0] + rims[0, c]
-        out[c, 15] = out[c, 15] + rims[1, c]
-        out[c, :, 0, :] = out[c, :, 0, :] + rims[2, c]
-        out[c, :, 15, :] = out[c, :, 15, :] + rims[3, c]
-
-
 def call(kernel, outs, n_scalar, n_vector, scratch=(), collective=None):
     more = {}
     if collective is not None:
@@ -579,7 +574,6 @@
 
 def shards(coarse_state, patch_state, patch_anchor, patch_count):
     owners = lax.axis_size("gx")
-    me = lax.axis_index("gx").astype(jnp.int32).reshape(1)
     anchors = patch_anchor.reshape(-1)
     counts = patch_count.reshape(-1)
     patch = patch_state.reshape(4, 5, 32, 1024)
@@ -591,31 +585,17 @@
     dense = (owners, 64, 128)
     dma = pltpu.SemaphoreType.DMA
 
-    W, B, S1, S2, advanced, FP = call(
-        first_kernel,
-        [cube, planes, planes, planes, field, (6,) + side],
+    coarse_next, out = call(
+        step_kernel,
+        [field, (4, 5, 32, 1024)],
         2,
         2,
-        [prim, (5, 32, 128), (5, 17, 24, 128), (7, 17, 24, 128), side, (8, 64, 128)]
-        + [dense] * 4
-        + [(2, 2) + side, (2, 4) + side, dma((2, 2, 4)), dma((2, 2, owners))],
+        [cube, prim] + [planes] * 5 + [(5, 32, 128), (4, 64, 128)]
+        + [(5, 17, 24, 128), (7, 17, 24, 128), side, field, (6,) + side, (8, 64, 128)]
+        + [dense] * 6
+        + [(2, 2) + side, (4,) + side, (3, 4) + side, dma((3, 2, 4)), dma((3, 2, owners))],
         0,
     )(anchors, counts, patch, coarse_state)
-    out, outgoing = call(
-        fine_kernel,
-        [(4, 5, 32, 1024), dense],
-        3,
-        5,
-        [cube, prim, (5, 32, 128), planes, planes, (4, 64, 128), planes],
-    )(anchors, counts, me, patch, W, B, S1, S2)
-    (coarse_next,) = call(
-        last_kernel,
-        [field],
-        2,
-        3,
-        [dense, (4,) + side, (4,) + side, dma((2, 4)), dma((2, owners))],
-        1,
-    )(anchors, counts, outgoing, advanced, FP)
     return (coarse_next, out.reshape(patch_state.shape))
 
 

time: 90.7 us -> 74.2 us (0.82)
  Pallas kernels: 86.3 us -> 65.9 us
  local copies, waits for them, and re-layouts: 3.52 us -> 7.05 us
    pallas_call x3 -> x1, Pallas kernels: 86.3 us -> 65.9 us  [shards(): call(step_kernel, [field, (4, 5, 32, 1024)], 2, 2, [cube, prim] + [planes...]
    unnamed x2 -> x3, local copies, waits for them, and re-layouts: 2.78 us -> 6.34 us
where the time goes in v3:
time: 74.2 us; the launch traced here: 73.6 us
  Pallas kernels  65.9 us (89%)
  local copies, waits for them, and re-layouts  7.05 us (10%)
    pallas_call x1, Pallas kernels, shards(): call(step_kernel, [field, (4, 5, 32, 1024)], 2, 2, [cube, prim] + [planes...  65.9 us
    unnamed x3, local copies, waits for them, and re-layouts  6.34 us

profile of v3, /device:TPU:0, one launch (start us, length us, event | category | flops | bytes accessed | tf_op | source)
XLA Modules:
  0.0 73.6 jit_solution(16790460508692399125)
XLA Ops:
  0.6 0.8 %copy.6 = s32[16,1,4,3]{3,2,0,1:T(4,128)S(1)} copy(s32[16,1,4,3]{0,2,3,1:T(4,128)} %param.6) | data formatting | bytes 1536 | tf_op args[2]
  1.4 0.7 reshape.16.anchors
  2.1 65.9 %shard_map.59 = (f32[5,16,16,128]{3,2,1,0:T(8,128)}, f32[4,5,32,1024]{3,2,1,0:T(8,128)}) custom-call(s32[192]{0:T(256)} %reshape.16.anchors, s32[16]{0:T(128)} %bitcast.7, f32[4,5,32,1024]{3,2,1,0:T(8,128)} %bitcast.5, f32[5,16,16,128]{3,2,1,0:T(8,128)} %field.1), custom_call_target="tpu_custom_call" | custom-call | flops 10000000 | bytes 4000000 | tf_op jit(solution)/shard_map/pallas_call | solution.py:588
  68.0 2.0 %copy.9 = f32[5,16,16,128]{3,2,1,0:T(8,128)} copy(f32[5,16,16,128]{3,2,1,0:T(8,128)} %get-tuple-element.8) | data formatting | bytes 1310720
  70.0 3.6 %copy.10 = f32[1,1,4,5,32,1024]{5,4,3,2,1,0:T(8,128)} copy(f32[1,1,4,5,32,1024]{5,4,3,2,1,0:T(8,128)} %bitcast.6) | data formatting | bytes 5242880

commit v4 on v3

--- a/solution.py
+++ b/solution.py
@@ -6,7 +6,7 @@
 from jax.sharding import PartitionSpec as P
 
 COURANT = 0.12
-VMEM_LIMIT = 56 * 1024 * 1024
+VMEM_LIMIT = 36 * 1024 * 1024
 F32 = jnp.float32
 MESH = pl.DeviceIdType.MESH
 
@@ -23,19 +23,22 @@
     r = rcp(U[0])
     u, v, w = U[1] * r, U[2] * r, U[3] * r
     p = 0.4 * (U[4] - 0.5 * (U[1] * u + U[2] * v + U[3] * w))
-    c5 = root((35.0 * p) * r)
+    cc = 1.4 * (p * r)
+    c5 = 5.0 * root(cc)
     cg5 = c5 * jnp.exp2(jnp.log2(p) * (-1.0 / 7.0))
     sa = root(r * (1.0 / 1.2))
-    return [u, v, w, p, c5, cg5, sa]
+    return [u, v, w, p, c5, cg5, sa, cc, 1.2 * r]
+
+
+PRIMS = 9
 
 
 def newton(s, z, scaled, L, R, du):
     value, slope = du, None
-    for p6, p7, c5, cg5, sa in (L, R):
-        t = s + p6
-        q = lax.rsqrt(t)
+    for p, p7, c5, cg5, sa in (L, R):
+        d = s - p
+        q = lax.rsqrt(d + p7)
         rt = sa * q
-        d = t - p7
         shock = d * rt
         shock_slope = rt * (1.0 + p7 * (q * q))
         rare = cg5 * z - c5
@@ -47,27 +50,24 @@
     return s - (value + value) * rcp(slope)
 
 
-def face_flux(UL, QL, UR, QR, n, keep=None):
+def face_flux(UL, QL, UR, QR, n, scale=COURANT):
     uL, pL, c5L, cg5L, saL = QL[n], QL[3], QL[4], QL[5], QL[6]
     uR, pR, c5R, cg5R, saR = QR[n], QR[3], QR[4], QR[5], QR[6]
     du = uR - uL
-    L = (pL * (1.0 / 6.0), pL * (7.0 / 6.0), c5L, cg5L, saL)
-    R = (pR * (1.0 / 6.0), pR * (7.0 / 6.0), c5R, cg5R, saR)
+    L = (pL, pL * (7.0 / 6.0), c5L, cg5L, saL)
+    R = (pR, pR * (7.0 / 6.0), c5R, cg5R, saR)
     z = (c5L + c5R - du) * rcp(cg5L + cg5R)
     z2 = z * z
     z6 = z2 * z2 * z2
     s = newton(z6 * z, z, (2.0 / 7.0) * rcp(z6), L, R, du)
     z = jnp.exp2(jnp.log2(s) * (1.0 / 7.0))
     s = newton(s, z, (2.0 / 7.0) * z * rcp(s), L, R, du)
-    waves = []
-    for c5, sa in ((c5L, saL), (c5R, saR)):
-        cc = c5 * c5
-        waves.append(0.2 * root(jnp.maximum(cc, (cc + (252.0 * s) * (sa * sa)) * (1.0 / 7.0))))
-    low = jnp.minimum(uL - waves[0], 0.0)
-    high = jnp.maximum(uR + waves[1], 0.0)
-    inv = rcp(high - low)
-    if keep is not None:
-        inv = jnp.where(keep, inv, 0.0)
+    low, high = (
+        root(jnp.maximum(q[7], q[7] * (1.0 / 7.0) + s * q[8])) for q in (QL, QR)
+    )
+    low = jnp.minimum(uL - low, 0.0)
+    high = jnp.maximum(uR + high, 0.0)
+    inv = rcp(high - low) * scale
     wL, wR = high * inv, low * inv
     a, b = wL * (uL - low), wR * (high - uR)
     eL, eR = wL * pL, wR * pR
@@ -109,6 +109,14 @@
 NORMAL = (2, 2, 0, 0, 1, 1)
 
 
+def next_x(a):
+    return jnp.concatenate([a[8:32], roll(a[0:8], -1, 0)], axis=0)
+
+
+def last_x(a):
+    return jnp.concatenate([roll(a[24:32], 1, 0), a[0:24]], axis=0)
+
+
 def collect(U, y, lane, B):
     here = lane == y
     for c in range(5):
@@ -116,7 +124,7 @@
         B[1, c] = jnp.where(here, pltpu.roll(U[c], y + 97, 1), B[1, c])
 
 
-def fine_load(patch, W, Q, B):
+def fine_load(patch, W, Q, B, T):
     lane = lanes((32, 128)) % 32
     for c in range(5):
         B[0, c] = jnp.zeros((32, 128), F32)
@@ -128,8 +136,11 @@
         for c in range(5):
             vs = block_transpose([patch[s, c, :, at] for s in range(4)], 32)
             for j in range(4):
-                W[c, 4 * yg + j] = vs[j]
-                U[j][c] = vs[j]
+                T[c, j] = vs[j]
+        for c in range(5):
+            for j in range(4):
+                U[j][c] = jnp.concatenate([T[c, j, pl.ds(v, 8, 4), :] for v in range(4)], axis=0)
+                W[c, 4 * yg + j] = U[j][c]
         for j in range(4):
             collect(U[j], 4 * yg + j, lane, B)
             for k, q in enumerate(primitives(U[j])):
@@ -140,9 +151,8 @@
 
 
 def fine_edges(W, FY, B):
-    shape = (32, 128)
-    for c in range(5):
-        FY[c] = jnp.zeros(shape, F32)
+    for c in range(5):
+        FY[c] = jnp.zeros((32, 128), F32)
         B[2, c] = W[c, :, 0, :]
         B[3, c] = W[c, :, 31, :]
         B[4, c] = W[c, 0]
@@ -152,38 +162,40 @@
 def fine_interior(W, Q, FY, first, last):
     shape = (32, 128)
     row = lax.broadcasted_iota(jnp.int32, shape, 0)
-    lane = lanes(shape) % 32
-    keep_x, keep_z = row < 31, lane < 31
-
-    def body(y, _):
-        up = jnp.minimum(y + 1, 31)
-        U = [W[c, y] for c in range(5)]
-        S = [Q[k, y] for k in range(7)]
-        total = []
-        F = face_flux(U, S, [roll(a, -1, 1) for a in U], [roll(a, -1, 1) for a in S], 2, keep_z)
+    scale_x = jnp.where(row < 31, COURANT, 0.0)
+    scale_z = jnp.where(lanes(shape) % 32 < 31, COURANT, 0.0)
+
+    def body(pair, _):
+        ys = (2 * pair, 2 * pair + 1, jnp.minimum(2 * pair + 2, 31))
+        U = [[W[c, y] for c in range(5)] for y in ys]
+        S = [[Q[k, y] for k in range(PRIMS)] for y in ys]
+        before = [FY[c] for c in range(5)]
+        results = []
+        for n in range(2):
+            scale = COURANT if n == 0 else jnp.where(jnp.broadcast_to(pair, shape) < 15, COURANT, 0.0)
+            F = face_flux(U[n], S[n], U[n + 1], S[n + 1], 1, scale)
+            total = [F[c] - before[c] for c in range(5)]
+            before = F
+            F = face_flux(
+                U[n], S[n], [roll(a, -1, 1) for a in U[n]], [roll(a, -1, 1) for a in S[n]], 2, scale_z
+            )
+            total = [total[c] + (F[c] - roll(F[c], 1, 1)) for c in range(5)]
+            F = face_flux(
+                U[n], S[n], [next_x(a) for a in U[n]], [next_x(a) for a in S[n]], 0, scale_x
+            )
+            results.append([U[n][c] - (total[c] + (F[c] - last_x(F[c]))) for c in range(5)])
         for c in range(5):
-            total.append(F[c] - roll(F[c], 1, 1))
-        F = face_flux(U, S, [roll(a, -1, 0) for a in U], [roll(a, -1, 0) for a in S], 0, keep_x)
-        for c in range(5):
-            total[c] = total[c] + (F[c] - roll(F[c], 1, 0))
-        keep = jnp.broadcast_to(y, shape) < 31
-        F = face_flux(
-            U, S, [W[c, up] for c in range(5)], [Q[k, up] for k in range(7)], 1, keep
-        )
-        for c in range(5):
-            total[c] = total[c] + (F[c] - FY[c])
-            FY[c] = F[c]
-            W[c, y] = U[c] - COURANT * total[c]
+            W[c, ys[0]] = results[0][c]
+            W[c, ys[1]] = results[1][c]
+            FY[c] = before[c]
         return 0
 
-    lax.fori_loop(first, last, body, 0)
-
-
-def fine_shells(got, sources, S, mix=None):
-    shape = (16, 128)
-    lane = lanes(shape)
-    slot = lane // 32
-    column = (lane % 32) // 2
+    lax.fori_loop(first // 2, last // 2, body, 0)
+
+
+def fine_shells(got, sources, S, T16, mix=None):
+    zeros = jnp.zeros((16, 128), F32)
+    twice = lanes((16, 128)) // 2
     for g in range(4):
         blocks = []
         for s in range(4):
@@ -192,82 +204,79 @@
             if mix is not None:
                 block = 0.5 * (block + mix[sources[s], at, :])
             blocks.append(block)
+        pieces = block_transpose(blocks + [zeros] * 4, 16)
         for k in range(8):
             q = 8 * g + k
             if q < 30:
-                out = None
-                for s in range(4):
-                    piece = pick(blocks[s], 16 * k + column)
-                    out = piece if out is None else jnp.where(slot == s, piece, out)
-                S[q // 5, q % 5, pl.ds(0, 16, 2), :] = out
-                S[q // 5, q % 5, pl.ds(1, 16, 2), :] = out
+                e, c = q // 5, q % 5
+                out = pick(pieces[k], twice)
+                if e in (2, 3):
+                    S[e, c, pl.ds(0, 16, 2), :] = out
+                    S[e, c, pl.ds(1, 16, 2), :] = out
+                else:
+                    T16[q] = out
+                    even, odd = T16[q, pl.ds(0, 8, 2), :], T16[q, pl.ds(1, 8, 2), :]
+                    S[e, c] = jnp.concatenate([even, even, odd, odd], axis=0)
 
 
 def fine_boundary(B, S, FB, FS, first):
-    def body(e2, _):
-        for side in range(2):
-            face = 2 * e2 + side
+    for n in range(3):
+        for face in (2 * n, 2 * n + 1):
             inner = [B[face, c] for c in range(5)]
             outer = [S[face, c] for c in range(5)]
-            for n in range(3):
-                axis = (2, 0, 1)[n]
-
-                @pl.when(e2 == n)
-                def _():
-                    qi, qo = primitives(inner), primitives(outer)
-                    if side == 0:
-                        F = face_flux(outer, qo, inner, qi, axis)
-                    else:
-                        F = face_flux(inner, qi, outer, qo, axis)
-                    for c in range(5):
-                        FB[face, c] = F[c]
-                        FS[face, c] = F[c] if first else FS[face, c] + F[c]
-
-        return 0
-
-    lax.fori_loop(0, 3, body, 0)
+            qi, qo = primitives(inner), primitives(outer)
+            if face % 2 == 0:
+                F = face_flux(outer, qo, inner, qi, NORMAL[face])
+            else:
+                F = face_flux(inner, qi, outer, qo, NORMAL[face])
+            for c in range(5):
+                FB[face, c] = F[c]
+                FS[face, c] = F[c] if first else FS[face, c] + F[c]
 
 
 def add_boundary(W, FB):
     for c in range(5):
-        W[c, :, 0, :] = W[c, :, 0, :] + COURANT * FB[2, c]
-        W[c, :, 31, :] = W[c, :, 31, :] - COURANT * FB[3, c]
-        W[c, 0] = W[c, 0] + COURANT * FB[4, c]
-        W[c, 31] = W[c, 31] - COURANT * FB[5, c]
+        W[c, :, 0, :] = W[c, :, 0, :] + FB[2, c]
+        W[c, :, 31, :] = W[c, :, 31, :] - FB[3, c]
+        W[c, 0] = W[c, 0] + FB[4, c]
+        W[c, 31] = W[c, 31] - FB[5, c]
 
 
 def z_boundary(value, FB, c, y, lane):
-    value = value + jnp.where(lane == 0, COURANT * pltpu.roll(FB[0, c], 128 - y, 1), 0.0)
-    return value - jnp.where(lane == 31, COURANT * pltpu.roll(FB[1, c], 159 - y, 1), 0.0)
+    value = value + jnp.where(lane == 0, pltpu.roll(FB[0, c], 128 - y, 1), 0.0)
+    return value - jnp.where(lane == 31, pltpu.roll(FB[1, c], 159 - y, 1), 0.0)
 
 
 def fine_again(W, FB, Q, B):
     lane = lanes((32, 128)) % 32
 
-    def body(y, _):
-        U = []
-        for c in range(5):
-            U.append(z_boundary(W[c, y], FB, c, y, lane))
-            W[c, y] = U[c]
-        collect(U, y, lane, B)
-        for k, q in enumerate(primitives(U)):
-            Q[k, y] = q
+    def body(pair, _):
+        for y in (2 * pair, 2 * pair + 1):
+            U = []
+            for c in range(5):
+                U.append(z_boundary(W[c, y], FB, c, y, lane))
+                W[c, y] = U[c]
+            collect(U, y, lane, B)
+            for k, q in enumerate(primitives(U)):
+                Q[k, y] = q
         return 0
 
-    lax.fori_loop(0, 32, body, 0)
-
-
-def fine_store(W, FB, patch, count, out):
+    lax.fori_loop(0, 16, body, 0)
+
+
+def fine_store(W, FB, patch, count, out, T):
     lane = lanes((32, 128)) % 32
 
     def body(yg, _):
         at = pl.ds(pl.multiple_of(yg * 128, 128), 128)
         for c in range(5):
-            vs = []
             for j in range(4):
                 y = 4 * yg + j
-                vs.append(z_boundary(W[c, y], FB, c, y, lane))
-            vs = block_transpose(vs, 32)
+                value = z_boundary(W[c, y], FB, c, y, lane)
+                for v in range(4):
+                    T[c, j, pl.ds(v, 8, 4), :] = value[8 * v : 8 * v + 8]
+        for c in range(5):
+            vs = block_transpose([T[c, j] for j in range(4)], 32)
             for s in range(4):
                 out[s, c, :, at] = jnp.where(s < count, vs[s], patch[s, c, :, at])
         return 0
@@ -275,19 +284,24 @@
     lax.fori_loop(0, 8, body, 0)
 
 
-def fine_pack(FS, PS):
-    shape = (16, 128)
-    lane = lanes(shape)
+def fine_pack(FS, PS, T16):
+    half = (lanes((16, 128)) * 2) % 128
     for g in range(4):
-        outs = [jnp.zeros(shape, F32) for _ in range(4)]
+        pieces = []
         for k in range(8):
             q = 8 * g + k
-            if q < 30:
-                m = FS[q // 5, q % 5, pl.ds(0, 16, 2), :] + FS[q // 5, q % 5, pl.ds(1, 16, 2), :]
-                m = m + roll(m, -1, 1)
-                for s in range(4):
-                    piece = pick(m, 32 * s + 2 * (lane % 16))
-                    outs[s] = jnp.where(lane // 16 == k, piece, outs[s])
+            if q >= 30:
+                pieces.append(jnp.zeros((16, 128), F32))
+                continue
+            e, c = q // 5, q % 5
+            if e in (2, 3):
+                m = FS[e, c, pl.ds(0, 16, 2), :] + FS[e, c, pl.ds(1, 16, 2), :]
+            else:
+                T16[q, pl.ds(0, 8, 2), :] = FS[e, c, 0:8] + FS[e, c, 8:16]
+                T16[q, pl.ds(1, 8, 2), :] = FS[e, c, 16:24] + FS[e, c, 24:32]
+                m = T16[q]
+            pieces.append(pick(m + roll(m, -1, 1), half))
+        outs = block_transpose(pieces, 16)
         for s in range(4):
             PS[s, pl.ds(16 * g, 16), :] = outs[s]
 
@@ -328,12 +342,15 @@
         C[c, 16, 0:16] = xhi[c]
         C[c, 16, 16:24] = xhi[c, 8:16]
 
-    def cells(x, _):
-        for k, q in enumerate(primitives([C[c, x] for c in range(5)])):
-            Q[k, x] = q
+    def cells(x4, _):
+        for x in range(4):
+            for k, q in enumerate(primitives([C[c, 4 * x4 + x] for c in range(5)])):
+                Q[k, 4 * x4 + x] = q
         return 0
 
-    lax.fori_loop(0, 17, cells, 0)
+    lax.fori_loop(0, 4, cells, 0)
+    for k, q in enumerate(primitives([C[c, 16] for c in range(5)])):
+        Q[k, 16] = q
     R = [field[c, 0] for c in range(5)]
     L = [xlo[c] for c in range(5)]
     F = face_flux(L, primitives(L), R, primitives(R), 0)
@@ -349,29 +366,42 @@
     lane = lanes((16, 128)) % 16
     row = lax.broadcasted_iota(jnp.int32, (16, 128), 0)
 
-    def body(x, _):
-        U24 = [C[c, x] for c in range(5)]
-        S24 = [Q[k, x] for k in range(7)]
-        U, S = [a[0:16] for a in U24], [a[0:16] for a in S24]
-        F = face_flux(U, S, [roll(a, -1, 1) for a in U], [roll(a, -1, 1) for a in S], 2)
-        total = []
+    def body(pair, _):
+        xs = (2 * pair, 2 * pair + 1, 2 * pair + 2)
+        U24 = [[C[c, x] for c in range(5)] for x in xs]
+        S24 = [[Q[k, x] for k in range(PRIMS)] for x in xs]
+        U = [[a[0:16] for a in As] for As in U24]
+        S = [[a[0:16] for a in As] for As in S24]
+        below = [FX[c] for c in range(5)]
+        corner = [[FP[4, c, pl.ds(x, 1), :] for c in range(5)] for x in xs[:2]]
+        zs = [FP[0, c] for c in range(5)]
+        results, tops = [], []
+        for n in range(2):
+            F = face_flux(U[n], S[n], U[n + 1], S[n + 1], 0)
+            total = [F[c] - below[c] for c in range(5)]
+            below = F
+            F = face_flux(
+                U[n], S[n], [roll(a, -1, 1) for a in U[n]], [roll(a, -1, 1) for a in S[n]], 2
+            )
+            for c in range(5):
+                zs[c] = jnp.where(lane == xs[n], pltpu.roll(F[c], xs[n] + 1, 1), zs[c])
+                total[c] = total[c] + (F[c] - roll(F[c], 1, 1))
+            up = [[roll(a, -1, 0)[0:16] for a in As] for As in (U24[n], S24[n])]
+            F = face_flux(U[n], S[n], up[0], up[1], 1)
+            tops.append([a[15:16] for a in F])
+            for c in range(5):
+                before = jnp.where(row == 0, corner[n][c], roll(F[c], 1, 0))
+                total[c] = total[c] + (F[c] - before)
+            results.append([U[n][c] - total[c] for c in range(5)])
         for c in range(5):
-            FP[0, c] = jnp.where(lane == x, pltpu.roll(F[c], x + 1, 1), FP[0, c])
-            total.append(F[c] - roll(F[c], 1, 1))
-        F = face_flux(U, S, [roll(a, -1, 0)[0:16] for a in U24], [roll(a, -1, 0)[0:16] for a in S24], 1)
-        for c in range(5):
-            before = jnp.where(row == 0, FP[4, c, pl.ds(x, 1), :], roll(F[c], 1, 0))
-            total[c] = total[c] + (F[c] - before)
-            FP[5, c, pl.ds(x, 1), :] = F[c][15:16]
-        F = face_flux(
-            U, S, [C[c, x + 1, 0:16] for c in range(5)], [Q[k, x + 1, 0:16] for k in range(7)], 0
-        )
-        for c in range(5):
-            adv[c, x] = U[c] - COURANT * (total[c] + (F[c] - FX[c]))
-            FX[c] = F[c]
+            for n in range(2):
+                adv[c, xs[n]] = results[n][c]
+                FP[5, c, pl.ds(xs[n], 1), :] = tops[n][c]
+            FP[0, c] = zs[c]
+            FX[c] = below[c]
         return 0
 
-    lax.fori_loop(0, 16, body, 0)
+    lax.fori_loop(0, 8, body, 0)
     for c in range(5):
         FP[3, c] = FX[c]
         FP[1, c] = roll(FP[0, c], -16, 1)
@@ -382,9 +412,8 @@
     for o in range(owners):
         block = jnp.int32(-1)
         for s in range(4):
-            at = 12 * o + 3 * s
-            mine = jnp.logical_and(s < counts[o], anchors[at] == 16 * me)
-            block = jnp.where(mine, anchors[at + 2] // 16, block)
+            mine = jnp.logical_and(s < counts[o], anchors[0, s, o] == 16 * me)
+            block = jnp.where(mine, anchors[2, s, o] // 16, block)
         blocks.append(block)
     return blocks
 
@@ -460,17 +489,17 @@
 def step_kernel(
     anchors, counts, patch, field, out_field, out,
     W, Q, B, S1, S2, FB, FS, FY, PS, C, CQ, FX, adv, FP, PZ,
-    dense_old, dense_new, dense_back, got_old, got_new, got_back, edges, D, sides, near_sems, far_sems,
+    dense_old, dense_new, dense_back, got_old, got_new, got_back, edges, D, sides, near_sems, far_sems, T, T16,
 ):
     place = Place()
     me = place.i
     count = counts[me]
-    sources = [anchors[12 * me + 3 * s] // 16 for s in range(4)]
+    sources = [anchors[0, s, me] // 16 for s in range(4)]
     old, new, rims = ([sides.at[n, k] for k in range(4)] for n in range(3))
     place.greet()
     planes = edge_planes(field, edges.at[0])
     blocks = owned_blocks(anchors, counts, me, place.ni)
-    fine_load(patch, W, Q, B)
+    fine_load(patch, W, Q, B, T)
     fine_edges(W, FY, B)
     place.greeted()
     near = place.neighbours(planes, old, near_sems.at[0])
@@ -487,15 +516,15 @@
     far_new = place.exchange(dense_new, got_new, far_sems.at[1])
     fine_interior(W, Q, FY, 14, 32)
     wait(far_old)
-    fine_shells(got_old, sources, S1)
+    fine_shells(got_old, sources, S1, T16)
     fine_boundary(B, S1, FB, FS, True)
     add_boundary(W, FB)
     fine_again(W, FB, Q, B)
     fine_edges(W, FY, B)
     wait(far_new)
-    fine_shells(got_old, sources, S2, got_new)
+    fine_shells(got_old, sources, S2, T16, got_new)
     fine_boundary(B, S2, FB, FS, False)
-    fine_pack(FS, PS)
+    fine_pack(FS, PS, T16)
     for i in range(place.ni):
         slot = jnp.int32(0)
         for s in range(1, 4):
@@ -508,7 +537,7 @@
     near = place.neighbours([D.at[1], D.at[0], D.at[3], D.at[2]], rims, near_sems.at[2])
     fine_interior(W, Q, FY, 22, 32)
     add_boundary(W, FB)
-    fine_store(W, FB, patch, count, out)
+    fine_store(W, FB, patch, count, out, T)
     wait(near)
     for c in range(5):
         out_field[c, 0] = out_field[c, 0] + sides[2, 0, c]
@@ -542,7 +571,7 @@
             if q < 30:
                 e, c = q // 5, q % 5
                 mean = 0.125 * (turned[16 * k : 16 * k + 16] if q < 10 else vs[k])
-                value = COURANT * (FP[e, c] - mean) if e % 2 == 0 else COURANT * (mean - FP[e, c])
+                value = FP[e, c] - mean if e % 2 == 0 else mean - FP[e, c]
                 value = jnp.where(live, value, 0.0)
                 if e < 2:
                     delta[e, c] = value
@@ -574,11 +603,11 @@
 
 def shards(coarse_state, patch_state, patch_anchor, patch_count):
     owners = lax.axis_size("gx")
-    anchors = patch_anchor.reshape(-1)
+    anchors = jnp.transpose(patch_anchor[:, 0], (2, 1, 0))
     counts = patch_count.reshape(-1)
     patch = patch_state.reshape(4, 5, 32, 1024)
     cube = (5, 32, 32, 128)
-    prim = (7, 32, 32, 128)
+    prim = (PRIMS, 32, 32, 128)
     planes = (6, 5, 32, 128)
     field = (5, 16, 16, 128)
     side = (5, 16, 128)
@@ -591,9 +620,9 @@
         2,
         2,
         [cube, prim] + [planes] * 5 + [(5, 32, 128), (4, 64, 128)]
-        + [(5, 17, 24, 128), (7, 17, 24, 128), side, field, (6,) + side, (8, 64, 128)]
+        + [(5, 17, 24, 128), (PRIMS, 17, 24, 128), side, field, (6,) + side, (8, 64, 128)]
         + [dense] * 6
-        + [(2, 2) + side, (4,) + side, (3, 4) + side, dma((3, 2, 4)), dma((3, 2, owners))],
+        + [(2, 2) + side, (4,) + side, (3, 4) + side, dma((3, 2, 4)), dma((3, 2, owners)), (5, 4, 32, 128), (30, 16, 128)],
         0,
     )(anchors, counts, patch, coarse_state)
     return (coarse_next, out.reshape(patch_state.shape))

time: 74.2 us -> 63.1 us (0.85)
  Pallas kernels: 65.9 us -> 54.8 us
    pallas_call x1, Pallas kernels: 65.9 us -> 54.8 us  [shards(): call(step_kernel, [field, (4, 5, 32, 1024)], 2, 2, [cube, prim] + [planes...]
    unnamed x3 -> x10, local copies, waits for them, and re-layouts: 6.34 us -> 6.5 us
where the time goes in v4:
time: 63.1 us; the launch traced here: 61.9 us
  Pallas kernels  54.8 us (87%)
  local copies, waits for them, and re-layouts  6.5 us (10%)
  between operations  0.65 us (1%)
    pallas_call x1, Pallas kernels, shards(): call(step_kernel, [field, (4, 5, 32, 1024)], 2, 2, [cube, prim] + [planes...  54.8 us
    unnamed x10, local copies, waits for them, and re-layouts  6.5 us

profile of v4, /device:TPU:0, one launch (start us, length us, event | category | flops | bytes accessed | tf_op | source)
XLA Modules:
  0.0 61.9 jit_solution(12684130256342652376)
XLA Ops:
  0.6 0.0 copy-start
  0.6 1.7 %copy-done = f32[1,1,4,5,32,1024]{5,4,3,2,1,0:T(8,128)S(1)} copy-done((f32[1,1,4,5,32,1024]{5,4,3,2,1,0:T(8,128)S(1)}, f32[1,1,4,5,32,1024]{5,4,3,2,1,0:T(8,128)}, u32[]{:S(2)}) %copy-start) | copy-done | bytes 2621464
  2.4 0.0 copy-start.1
  2.4 1.1 %copy-done.1 = f32[5,16,16,128]{3,2,1,0:T(8,128)S(1)} copy-done((f32[5,16,16,128]{3,2,1,0:T(8,128)S(1)}, f32[5,16,16,128]{3,2,1,0:T(8,128)}, u32[]{:S(2)}) %copy-start.1) | copy-done | bytes 655384
  3.5 0.0 copy-start.2
  3.5 0.7 %copy-done.2 = s32[16,1,4,3]{0,2,3,1:T(4,128)S(1)} copy-done((s32[16,1,4,3]{0,2,3,1:T(4,128)S(1)}, s32[16,1,4,3]{0,2,3,1:T(4,128)}, u32[]{:S(2)}) %copy-start.2) | copy-done | bytes 792
  4.2 0.0 copy-start.3
  4.2 0.7 %copy-done.3 = s32[16,1]{0,1:T(1,128)S(1)} copy-done((s32[16,1]{0,1:T(1,128)S(1)}, s32[16,1]{0,1:T(1,128)}, u32[]{:S(2)}) %copy-start.3) | copy-done | bytes 88
  4.8 54.8 %shard_map.59 = (f32[5,16,16,128]{3,2,1,0:T(8,128)S(1)}, f32[4,5,32,1024]{3,2,1,0:T(8,128)S(1)}) custom-call(s32[3,4,16]{2,1,0:T(4,128)S(1)} %bitcast.8, s32[16]{0:T(128)S(1)} %bitcast.9, f32[4,5,32,1024]{3,2,1,0:T(8,128)S(1)} %bitcast.6, f32[5,16,16,128]{3,2,1,0:T(8,128)S(1)} %copy-done.1), custom_call_target="tpu_custom_call" | custom-call | flops 10000000 | bytes 4000000 | tf_op jit(solution)/shard_map/pallas_call | solution.py:617
  59.6 0.8 %copy.8 = f32[5,16,16,128]{3,2,1,0:T(8,128)} copy(f32[5,16,16,128]{3,2,1,0:T(8,128)S(1)} %get-tuple-element.8) | data formatting | bytes 1310720
  60.4 1.5 %copy.9 = f32[1,1,4,5,32,1024]{5,4,3,2,1,0:T(8,128)} copy(f32[1,1,4,5,32,1024]{5,4,3,2,1,0:T(8,128)S(1)} %bitcast.7) | data formatting | bytes 5242880
Async XLA Ops:
  0.6 1.7 %copy-start = (f32[1,1,4,5,32,1024]{5,4,3,2,1,0:T(8,128)S(1)}, f32[1,1,4,5,32,1024]{5,4,3,2,1,0:T(8,128)}, u32[]{:S(2)}) copy-start(f32[1,1,4,5,32,1024]{5,4,3,2,1,0:T(8,128)} %param.5) | copy-start | bytes 7864324
  2.4 1.1 %copy-start.1 = (f32[5,16,16,128]{3,2,1,0:T(8,128)S(1)}, f32[5,16,16,128]{3,2,1,0:T(8,128)}, u32[]{:S(2)}) copy-start(f32[5,16,16,128]{3,2,1,0:T(8,128)} %field.1) | copy-start | bytes 1966084
  3.5 0.7 %copy-start.2 = (s32[16,1,4,3]{0,2,3,1:T(4,128)S(1)}, s32[16,1,4,3]{0,2,3,1:T(4,128)}, u32[]{:S(2)}) copy-start(s32[16,1,4,3]{0,2,3,1:T(4,128)} %param.6) | copy-start | bytes 2308
  4.2 0.7 %copy-start.3 = (s32[16,1]{0,1:T(1,128)S(1)}, s32[16,1]{0,1:T(1,128)}, u32[]{:S(2)}) copy-start(s32[16,1]{0,1:T(1,128)} %param.7) | copy-start | bytes 196

commit v5 on v4

--- a/solution.py
+++ b/solution.py
@@ -6,8 +6,9 @@
 from jax.sharding import PartitionSpec as P
 
 COURANT = 0.12
-VMEM_LIMIT = 36 * 1024 * 1024
+VMEM_LIMIT = 50 * 1024 * 1024
 F32 = jnp.float32
+BF16 = jnp.bfloat16
 MESH = pl.DeviceIdType.MESH
 
 
@@ -33,16 +34,19 @@
 PRIMS = 9
 
 
-def newton(s, z, scaled, L, R, du):
+def newton(s, z, L, R, du):
     value, slope = du, None
-    for p, p7, c5, cg5, sa in (L, R):
+    scaled = (2.0 / 7.0) * rcp(s)
+    for p, c5, cg5, sa in (L, R):
+        p7 = p * (7.0 / 6.0)
         d = s - p
         q = lax.rsqrt(d + p7)
         rt = sa * q
         shock = d * rt
         shock_slope = rt * (1.0 + p7 * (q * q))
-        rare = cg5 * z - c5
-        rare_slope = cg5 * scaled
+        power = cg5 * z
+        rare = power - c5
+        rare_slope = power * scaled
         up = d > 0.0
         value = value + jnp.where(up, shock, rare)
         term = jnp.where(up, shock_slope, rare_slope)
@@ -50,18 +54,20 @@
     return s - (value + value) * rcp(slope)
 
 
+def first_star(L, R, du):
+    z = (L[1] + R[1] - du) * rcp(L[2] + R[2])
+    z2 = z * z
+    z3 = z2 * z
+    return newton(z3 * z3 * z, z, L, R, du)
+
+
 def face_flux(UL, QL, UR, QR, n, scale=COURANT):
-    uL, pL, c5L, cg5L, saL = QL[n], QL[3], QL[4], QL[5], QL[6]
-    uR, pR, c5R, cg5R, saR = QR[n], QR[3], QR[4], QR[5], QR[6]
+    uL, pL, uR, pR = QL[n], QL[3], QR[n], QR[3]
     du = uR - uL
-    L = (pL, pL * (7.0 / 6.0), c5L, cg5L, saL)
-    R = (pR, pR * (7.0 / 6.0), c5R, cg5R, saR)
-    z = (c5L + c5R - du) * rcp(cg5L + cg5R)
-    z2 = z * z
-    z6 = z2 * z2 * z2
-    s = newton(z6 * z, z, (2.0 / 7.0) * rcp(z6), L, R, du)
+    s = first_star([q.astype(BF16) for q in QL[3:7]], [q.astype(BF16) for q in QR[3:7]], du.astype(BF16))
+    s = s.astype(F32)
     z = jnp.exp2(jnp.log2(s) * (1.0 / 7.0))
-    s = newton(s, z, (2.0 / 7.0) * z * rcp(s), L, R, du)
+    s = newton(s, z, QL[3:7], QR[3:7], du)
     low, high = (
         root(jnp.maximum(q[7], q[7] * (1.0 / 7.0) + s * q[8])) for q in (QL, QR)
     )
@@ -118,13 +124,14 @@
 
 
 def collect(U, y, lane, B):
-    here = lane == y
-    for c in range(5):
-        B[0, c] = jnp.where(here, pltpu.roll(U[c], y, 1), B[0, c])
-        B[1, c] = jnp.where(here, pltpu.roll(U[c], y + 97, 1), B[1, c])
-
-
-def fine_load(patch, W, Q, B, T):
+    lower, upper = lane == y, (lane + 1) % 32 == y
+    for c in range(5):
+        turned = pltpu.roll(U[c], y, 1)
+        B[0, c] = jnp.where(lower, turned, B[0, c])
+        B[1, c] = jnp.where(upper, turned, B[1, c])
+
+
+def fine_load(patch, W, Q, B, T, arrived):
     lane = lanes((32, 128)) % 32
     for c in range(5):
         B[0, c] = jnp.zeros((32, 128), F32)
@@ -132,6 +139,7 @@
 
     def body(yg, _):
         at = pl.ds(pl.multiple_of(yg * 128, 128), 128)
+        arrived(yg)
         U = [[None] * 5 for _ in range(4)]
         for c in range(5):
             vs = block_transpose([patch[s, c, :, at] for s in range(4)], 32)
@@ -153,6 +161,7 @@
 def fine_edges(W, FY, B):
     for c in range(5):
         FY[c] = jnp.zeros((32, 128), F32)
+        B[1, c] = roll(B[1, c], -31, 1)
         B[2, c] = W[c, :, 0, :]
         B[3, c] = W[c, :, 31, :]
         B[4, c] = W[c, 0]
@@ -236,6 +245,7 @@
 
 def add_boundary(W, FB):
     for c in range(5):
+        FB[1, c] = roll(FB[1, c], 31, 1)
         W[c, :, 0, :] = W[c, :, 0, :] + FB[2, c]
         W[c, :, 31, :] = W[c, :, 31, :] - FB[3, c]
         W[c, 0] = W[c, 0] + FB[4, c]
@@ -243,8 +253,8 @@
 
 
 def z_boundary(value, FB, c, y, lane):
-    value = value + jnp.where(lane == 0, pltpu.roll(FB[0, c], 128 - y, 1), 0.0)
-    return value - jnp.where(lane == 31, pltpu.roll(FB[1, c], 159 - y, 1), 0.0)
+    upper = jnp.where((lane + 1) % 32 == y, -FB[1, c], 0.0)
+    return value + pltpu.roll(jnp.where(lane == y, FB[0, c], upper), 128 - y, 1)
 
 
 def fine_again(W, FB, Q, B):
@@ -487,19 +497,37 @@
 
 
 def step_kernel(
-    anchors, counts, patch, field, out_field, out,
+    anchors_hbm, counts_hbm, patch_hbm, field_hbm, out_field, out, anchors, counts, patch, field, load_sems,
     W, Q, B, S1, S2, FB, FS, FY, PS, C, CQ, FX, adv, FP, PZ,
     dense_old, dense_new, dense_back, got_old, got_new, got_back, edges, D, sides, near_sems, far_sems, T, T16,
 ):
     place = Place()
     me = place.i
+
+    def chunk(yg):
+        at = pl.ds(pl.multiple_of(yg * 128, 128), 128)
+        return pltpu.make_async_copy(
+            patch_hbm.at[:, :, :, at], patch.at[:, :, :, at], load_sems.at[yg]
+        )
+
+    small = [
+        pltpu.make_async_copy(field_hbm, field, load_sems.at[8]),
+        pltpu.make_async_copy(anchors_hbm, anchors, load_sems.at[9]),
+        pltpu.make_async_copy(counts_hbm, counts, load_sems.at[10]),
+    ]
+    chunk(0).start()
+    for copy in small:
+        copy.start()
+    for yg in range(1, 8):
+        chunk(yg).start()
+    old, new, rims = ([sides.at[n, k] for k in range(4)] for n in range(3))
+    place.greet()
+    fine_load(patch, W, Q, B, T, lambda yg: chunk(yg).wait())
+    wait(small)
+    planes = edge_planes(field, edges.at[0])
     count = counts[me]
     sources = [anchors[0, s, me] // 16 for s in range(4)]
-    old, new, rims = ([sides.at[n, k] for k in range(4)] for n in range(3))
-    place.greet()
-    planes = edge_planes(field, edges.at[0])
     blocks = owned_blocks(anchors, counts, me, place.ni)
-    fine_load(patch, W, Q, B, T)
     fine_edges(W, FY, B)
     place.greeted()
     near = place.neighbours(planes, old, near_sems.at[0])
@@ -531,11 +559,11 @@
             slot = jnp.where(jnp.logical_and(s < count, sources[s] == i), s, slot)
         dense_back[i] = PS[slot]
     back = place.exchange(dense_back, got_back, far_sems.at[2])
-    fine_interior(W, Q, FY, 0, 22)
+    fine_interior(W, Q, FY, 0, 26)
     wait(back)
     reflux(blocks, adv, FP, got_back, out_field, D)
     near = place.neighbours([D.at[1], D.at[0], D.at[3], D.at[2]], rims, near_sems.at[2])
-    fine_interior(W, Q, FY, 22, 32)
+    fine_interior(W, Q, FY, 26, 32)
     add_boundary(W, FB)
     fine_store(W, FB, patch, count, out, T)
     wait(near)
@@ -585,15 +613,14 @@
             out[c, x] = value
 
 
-def call(kernel, outs, n_scalar, n_vector, scratch=(), collective=None):
+def call(kernel, outs, n_in, scratch=(), collective=None):
     more = {}
     if collective is not None:
         more = {"collective_id": collective, "has_side_effects": True}
     return pl.pallas_call(
         kernel,
         out_shape=[jax.ShapeDtypeStruct(shape, F32) for shape in outs],
-        in_specs=[pl.BlockSpec(memory_space=pltpu.SMEM)] * n_scalar
-        + [pl.BlockSpec(memory_space=pltpu.VMEM)] * n_vector,
+        in_specs=[pl.BlockSpec(memory_space=pltpu.HBM)] * n_in,
         out_specs=[pl.BlockSpec(memory_space=pltpu.VMEM)] * len(outs),
         scratch_shapes=[pltpu.VMEM(s, F32) if isinstance(s, tuple) else s for s in scratch],
         compiler_params=pltpu.CompilerParams(vmem_limit_bytes=VMEM_LIMIT, **more),
@@ -617,9 +644,9 @@
     coarse_next, out = call(
         step_kernel,
         [field, (4, 5, 32, 1024)],
-        2,
-        2,
-        [cube, prim] + [planes] * 5 + [(5, 32, 128), (4, 64, 128)]
+        4,
+        [pltpu.SMEM((3, 4, owners), jnp.int32), pltpu.SMEM((owners,), jnp.int32)]
+        + [(4, 5, 32, 1024), field, dma((11,)), cube, prim] + [planes] * 5 + [(5, 32, 128), (4, 64, 128)]
         + [(5, 17, 24, 128), (PRIMS, 17, 24, 128), side, field, (6,) + side, (8, 64, 128)]
         + [dense] * 6
         + [(2, 2) + side, (4,) + side, (3, 4) + side, dma((3, 2, 4)), dma((3, 2, owners)), (5, 4, 32, 128), (30, 16, 128)],

time: 63.1 us -> 55.2 us (0.87); the launches traced: 61.9 us -> 54.8 us
  Pallas kernels: 54.8 us -> 49.4 us
  local copies, waits for them, and re-layouts: 6.5 us -> 4.76 us
    pallas_call x1, Pallas kernels: 54.8 us -> 49.4 us  [shards(): call(step_kernel, [field, (4, 5, 32, 1024)], 4, [pltpu.SMEM((3, 4, owners...]
    unnamed x10 -> x8, local copies, waits for them, and re-layouts: 6.5 us -> 4.76 us
where the time goes in v5:
time: 55.2 us; the launch traced here: 54.8 us
  Pallas kernels  49.4 us (89%)
  local copies, waits for them, and re-layouts  4.76 us (9%)
  between operations  0.65 us (1%)
    pallas_call x1, Pallas kernels, shards(): call(step_kernel, [field, (4, 5, 32, 1024)], 4, [pltpu.SMEM((3, 4, owners...  49.4 us
    unnamed x8, local copies, waits for them, and re-layouts  4.76 us

profile of v5, /device:TPU:0, one launch (start us, length us, event | category | flops | bytes accessed | tf_op | source)
XLA Modules:
  0.0 54.8 jit_solution(6010629850239015775)
XLA Ops:
  0.6 0.0 copy-start
  0.6 1.1 %copy-done = f32[5,16,16,128]{3,2,1,0:T(8,128)S(1)} copy-done((f32[5,16,16,128]{3,2,1,0:T(8,128)S(1)}, f32[5,16,16,128]{3,2,1,0:T(8,128)}, u32[]{:S(2)}) %copy-start) | copy-done | bytes 655384
  1.7 0.0 copy-start.1
  1.7 0.7 %copy-done.1 = s32[16,1,4,3]{0,2,3,1:T(4,128)S(1)} copy-done((s32[16,1,4,3]{0,2,3,1:T(4,128)S(1)}, s32[16,1,4,3]{0,2,3,1:T(4,128)}, u32[]{:S(2)}) %copy-start.1) | copy-done | bytes 792
  2.4 0.0 copy-start.2
  2.4 0.7 %copy-done.2 = s32[16,1]{0,1:T(1,128)S(1)} copy-done((s32[16,1]{0,1:T(1,128)S(1)}, s32[16,1]{0,1:T(1,128)}, u32[]{:S(2)}) %copy-start.2) | copy-done | bytes 88
  3.1 49.4 %shard_map.59 = (f32[5,16,16,128]{3,2,1,0:T(8,128)S(1)}, f32[4,5,32,1024]{3,2,1,0:T(8,128)S(1)}) custom-call(s32[3,4,16]{2,1,0:T(4,128)S(1)} %bitcast.7, s32[16]{0:T(128)S(1)} %bitcast.8, f32[4,5,32,1024]{3,2,1,0:T(8,128)} %bitcast.9, f32[5,16,16,128]{3,2,1,0:T(8,128)S(1)} %copy-done), custom_call_target="tpu_custom_call" | custom-call | flops 10000000 | bytes 4000000 | tf_op jit(solution)/shard_map/pallas_call | solution.py:644
  52.5 0.8 %copy.8 = f32[5,16,16,128]{3,2,1,0:T(8,128)} copy(f32[5,16,16,128]{3,2,1,0:T(8,128)S(1)} %get-tuple-element.8) | data formatting | bytes 1310720
  53.4 1.5 %copy.9 = f32[1,1,4,5,32,1024]{5,4,3,2,1,0:T(8,128)} copy(f32[1,1,4,5,32,1024]{5,4,3,2,1,0:T(8,128)S(1)} %bitcast.6) | data formatting | bytes 5242880
Async XLA Ops:
  0.6 1.1 %copy-start = (f32[5,16,16,128]{3,2,1,0:T(8,128)S(1)}, f32[5,16,16,128]{3,2,1,0:T(8,128)}, u32[]{:S(2)}) copy-start(f32[5,16,16,128]{3,2,1,0:T(8,128)} %field_hbm.1) | copy-start | bytes 1966084
  1.7 0.7 %copy-start.1 = (s32[16,1,4,3]{0,2,3,1:T(4,128)S(1)}, s32[16,1,4,3]{0,2,3,1:T(4,128)}, u32[]{:S(2)}) copy-start(s32[16,1,4,3]{0,2,3,1:T(4,128)} %param.6) | copy-start | bytes 2308
  2.4 0.7 %copy-start.2 = (s32[16,1]{0,1:T(1,128)S(1)}, s32[16,1]{0,1:T(1,128)}, u32[]{:S(2)}) copy-start(s32[16,1]{0,1:T(1,128)} %param.7) | copy-start | bytes 196

commit v6 on v5

--- a/solution.py
+++ b/solution.py
@@ -27,23 +27,20 @@
     cc = 1.4 * (p * r)
     c5 = 5.0 * root(cc)
     cg5 = c5 * jnp.exp2(jnp.log2(p) * (-1.0 / 7.0))
-    sa = root(r * (1.0 / 1.2))
-    return [u, v, w, p, c5, cg5, sa, cc, 1.2 * r]
-
-
-PRIMS = 9
+    return [u, v, w, p, c5, cg5, 1.2 * U[0], p * (1.0 / 6.0), cc, 1.2 * r]
+
+
+PRIMS = 10
 
 
 def newton(s, z, L, R, du):
     value, slope = du, None
     scaled = (2.0 / 7.0) * rcp(s)
-    for p, c5, cg5, sa in (L, R):
-        p7 = p * (7.0 / 6.0)
+    for p, c5, cg5, r12, p6 in (L, R):
         d = s - p
-        q = lax.rsqrt(d + p7)
-        rt = sa * q
+        rt = lax.rsqrt((s + p6) * r12)
         shock = d * rt
-        shock_slope = rt * (1.0 + p7 * (q * q))
+        shock_slope = rt * (2.0 - (shock * rt) * r12)
         power = cg5 * z
         rare = power - c5
         rare_slope = power * scaled
@@ -64,13 +61,11 @@
 def face_flux(UL, QL, UR, QR, n, scale=COURANT):
     uL, pL, uR, pR = QL[n], QL[3], QR[n], QR[3]
     du = uR - uL
-    s = first_star([q.astype(BF16) for q in QL[3:7]], [q.astype(BF16) for q in QR[3:7]], du.astype(BF16))
+    s = first_star([q.astype(BF16) for q in QL[3:8]], [q.astype(BF16) for q in QR[3:8]], du.astype(BF16))
     s = s.astype(F32)
     z = jnp.exp2(jnp.log2(s) * (1.0 / 7.0))
-    s = newton(s, z, QL[3:7], QR[3:7], du)
-    low, high = (
-        root(jnp.maximum(q[7], q[7] * (1.0 / 7.0) + s * q[8])) for q in (QL, QR)
-    )
+    s = newton(s, z, QL[3:8], QR[3:8], du)
+    low, high = (root(jnp.maximum(q[8], (s + q[7]) * q[9])) for q in (QL, QR))
     low = jnp.minimum(uL - low, 0.0)
     high = jnp.maximum(uR + high, 0.0)
     inv = rcp(high - low) * scale
@@ -228,12 +223,18 @@
                     S[e, c] = jnp.concatenate([even, even, odd, odd], axis=0)
 
 
-def fine_boundary(B, S, FB, FS, first):
+def fine_boundary(B, Q, S, FB, FS, first):
     for n in range(3):
         for face in (2 * n, 2 * n + 1):
             inner = [B[face, c] for c in range(5)]
             outer = [S[face, c] for c in range(5)]
-            qi, qo = primitives(inner), primitives(outer)
+            qo = primitives(outer)
+            if n == 0:
+                qi = primitives(inner)
+            elif n == 1:
+                qi = [Q[k, :, 31 * (face % 2), :] for k in range(PRIMS)]
+            else:
+                qi = [Q[k, 31 * (face % 2)] for k in range(PRIMS)]
             if face % 2 == 0:
                 F = face_flux(outer, qo, inner, qi, NORMAL[face])
             else:
@@ -531,27 +532,27 @@
     fine_edges(W, FY, B)
     place.greeted()
     near = place.neighbours(planes, old, near_sems.at[0])
-    fine_interior(W, Q, FY, 0, 6)
+    fine_interior(W, Q, FY, 0, 4)
     wait(near)
     pack_shells(blocks, field, old, PZ, dense_old)
     far_old = place.exchange(dense_old, got_old, far_sems.at[0])
     coarse_step(field, *old, adv, FP, C, CQ, FX)
     planes = edge_planes(adv, edges.at[1])
     near = place.neighbours(planes, new, near_sems.at[1])
-    fine_interior(W, Q, FY, 6, 14)
+    fine_interior(W, Q, FY, 4, 10)
     wait(near)
     pack_shells(blocks, adv, new, PZ, dense_new)
     far_new = place.exchange(dense_new, got_new, far_sems.at[1])
-    fine_interior(W, Q, FY, 14, 32)
+    fine_interior(W, Q, FY, 10, 32)
     wait(far_old)
     fine_shells(got_old, sources, S1, T16)
-    fine_boundary(B, S1, FB, FS, True)
+    fine_boundary(B, Q, S1, FB, FS, True)
     add_boundary(W, FB)
     fine_again(W, FB, Q, B)
     fine_edges(W, FY, B)
     wait(far_new)
     fine_shells(got_old, sources, S2, T16, got_new)
-    fine_boundary(B, S2, FB, FS, False)
+    fine_boundary(B, Q, S2, FB, FS, False)
     fine_pack(FS, PS, T16)
     for i in range(place.ni):
         slot = jnp.int32(0)
@@ -559,11 +560,11 @@
             slot = jnp.where(jnp.logical_and(s < count, sources[s] == i), s, slot)
         dense_back[i] = PS[slot]
     back = place.exchange(dense_back, got_back, far_sems.at[2])
-    fine_interior(W, Q, FY, 0, 26)
+    fine_interior(W, Q, FY, 0, 28)
     wait(back)
     reflux(blocks, adv, FP, got_back, out_field, D)
     near = place.neighbours([D.at[1], D.at[0], D.at[3], D.at[2]], rims, near_sems.at[2])
-    fine_interior(W, Q, FY, 26, 32)
+    fine_interior(W, Q, FY, 28, 32)
     add_boundary(W, FB)
     fine_store(W, FB, patch, count, out, T)
     wait(near)
@@ -651,7 +652,7 @@
         + [dense] * 6
         + [(2, 2) + side, (4,) + side, (3, 4) + side, dma((3, 2, 4)), dma((3, 2, owners)), (5, 4, 32, 128), (30, 16, 128)],
         0,
-    )(anchors, counts, patch, coarse_state)
+    )(*(pltpu.with_memory_space_constraint(a, pltpu.HBM) for a in (anchors, counts, patch, coarse_state)))
     return (coarse_next, out.reshape(patch_state.shape))
 
 

time: 55.2 us -> 54.1 us (0.980)
  local copies, waits for them, and re-layouts: 4.76 us -> 2.33 us
  Pallas kernels: 49.4 us -> 50.8 us
    unnamed x8 -> x2, local copies, waits for them, and re-layouts: 4.76 us -> 2.33 us
    pallas_call x1, Pallas kernels: 49.4 us -> 50.8 us  [shards(): call(step_kernel, [field, (4, 5, 32, 1024)], 4, [pltpu.SMEM((3, 4, owners...]
where the time goes in v6:
time: 54.1 us; the launch traced here: 53.8 us
  Pallas kernels  50.8 us (94%)
  local copies, waits for them, and re-layouts  2.33 us (4%)
  between operations  0.64 us (1%)
    pallas_call x1, Pallas kernels, shards(): call(step_kernel, [field, (4, 5, 32, 1024)], 4, [pltpu.SMEM((3, 4, owners...  50.8 us
    unnamed x2, local copies, waits for them, and re-layouts  2.33 us

profile of v6, /device:TPU:0, one launch (start us, length us, event | category | flops | bytes accessed | tf_op | source)
XLA Modules:
  0.0 53.8 jit_solution(18023892301701233175)
XLA Ops:
  0.6 50.8 %shard_map.59 = (f32[5,16,16,128]{3,2,1,0:T(8,128)S(1)}, f32[4,5,32,1024]{3,2,1,0:T(8,128)S(1)}) custom-call(s32[3,4,16]{2,1,0:T(4,128)} %bitcast.8, s32[16]{0:T(128)} %bitcast.9, f32[4,5,32,1024]{3,2,1,0:T(8,128)} %bitcast.7, f32[5,16,16,128]{3,2,1,0:T(8,128)} %field_hbm.1), custom_call_target="tpu_custom_call" | custom-call | flops 10000000 | bytes 4000000 | tf_op jit(solution)/shard_map/pallas_call | solution.py:645
  51.5 0.8 %copy.8 = f32[5,16,16,128]{3,2,1,0:T(8,128)} copy(f32[5,16,16,128]{3,2,1,0:T(8,128)S(1)} %get-tuple-element.8) | data formatting | bytes 1310720
  52.3 1.5 %copy.9 = f32[1,1,4,5,32,1024]{5,4,3,2,1,0:T(8,128)} copy(f32[1,1,4,5,32,1024]{5,4,3,2,1,0:T(8,128)S(1)} %bitcast.6) | data formatting | bytes 5242880

commit v7 on v6

--- a/solution.py
+++ b/solution.py
@@ -118,12 +118,22 @@
     return jnp.concatenate([roll(a[24:32], 1, 0), a[0:24]], axis=0)
 
 
-def collect(U, y, lane, B):
+def collect(U, y, lane, planes):
     lower, upper = lane == y, (lane + 1) % 32 == y
     for c in range(5):
         turned = pltpu.roll(U[c], y, 1)
-        B[0, c] = jnp.where(lower, turned, B[0, c])
-        B[1, c] = jnp.where(upper, turned, B[1, c])
+        planes[0][c] = jnp.where(lower, turned, planes[0][c])
+        planes[1][c] = jnp.where(upper, turned, planes[1][c])
+
+
+def z_planes(B):
+    return [[B[side, c] for c in range(5)] for side in range(2)]
+
+
+def put_planes(B, planes):
+    for side in range(2):
+        for c in range(5):
+            B[side, c] = planes[side][c]
 
 
 def fine_load(patch, W, Q, B, T, arrived):
@@ -144,8 +154,11 @@
             for j in range(4):
                 U[j][c] = jnp.concatenate([T[c, j, pl.ds(v, 8, 4), :] for v in range(4)], axis=0)
                 W[c, 4 * yg + j] = U[j][c]
+        planes = z_planes(B)
         for j in range(4):
-            collect(U[j], 4 * yg + j, lane, B)
+            collect(U[j], 4 * yg + j, lane, planes)
+        put_planes(B, planes)
+        for j in range(4):
             for k, q in enumerate(primitives(U[j])):
                 Q[k, 4 * yg + j] = q
         return 0
@@ -261,18 +274,20 @@
 def fine_again(W, FB, Q, B):
     lane = lanes((32, 128)) % 32
 
-    def body(pair, _):
-        for y in (2 * pair, 2 * pair + 1):
-            U = []
+    def body(yg, _):
+        planes = z_planes(B)
+        for j in range(4):
+            y = 4 * yg + j
+            U = [z_boundary(W[c, y], FB, c, y, lane) for c in range(5)]
             for c in range(5):
-                U.append(z_boundary(W[c, y], FB, c, y, lane))
                 W[c, y] = U[c]
-            collect(U, y, lane, B)
+            collect(U, y, lane, planes)
             for k, q in enumerate(primitives(U)):
                 Q[k, y] = q
+        put_planes(B, planes)
         return 0
 
-    lax.fori_loop(0, 16, body, 0)
+    lax.fori_loop(0, 8, body, 0)
 
 
 def fine_store(W, FB, patch, count, out, T):
@@ -326,8 +341,10 @@
         here = lane % 16 == x
         for c in range(5):
             U = field[c, x, 0:16, :]
-            T[c] = jnp.where(here, roll(U, x + 1, 1), T[c])
-            T[5 + c] = jnp.where(here, roll(U, x - 16, 1), T[5 + c])
+            turned = roll(U, x, 1)
+            T[c] = jnp.where((lane + 1) % 16 == x, turned, T[c])
+            T[5 + c] = jnp.where(here, turned, T[5 + c])
+    T = [roll(a, 1, 1) for a in T[:5]] + [roll(a, -16, 1) for a in T[5:]]
     z0 = jnp.concatenate(T[:8], axis=0).T
     z1 = jnp.concatenate(T[8:] + [zeros] * 6, axis=0).T
     for zb in range(8):
@@ -575,6 +592,16 @@
         out_field[c, :, 15, :] = out_field[c, :, 15, :] + sides[2, 3, c]
 
 
+def write_kernel(field, patch, out_field, out, sems):
+    copies = [
+        pltpu.make_async_copy(patch, out, sems.at[0]),
+        pltpu.make_async_copy(field, out_field, sems.at[1]),
+    ]
+    for copy in copies:
+        copy.start()
+    wait(copies)
+
+
 def reflux(blocks, adv, FP, got, out, D):
     shape = (16, 128)
     lane = lanes(shape)
@@ -606,23 +633,23 @@
                     delta[e, c] = value
                 else:
                     D[e - 2, c] = value
-    for c in range(5):
+    column = lane % 16
+    for c in range(5):
+        lower, upper = roll(delta[0, c], -1, 1), roll(delta[1, c], 16, 1)
         for x in range(16):
-            value = adv[c, x]
-            value = value + jnp.where(lane % 16 == 15, roll(delta[0, c], -(x + 1), 1), 0.0)
-            value = value + jnp.where(lane % 16 == 0, roll(delta[1, c], 16 - x, 1), 0.0)
-            out[c, x] = value
-
-
-def call(kernel, outs, n_in, scratch=(), collective=None):
+            both = jnp.where((column + 1) % 16 == x, lower, 0.0)
+            out[c, x] = adv[c, x] + roll(jnp.where(column == x, upper, both), -x, 1)
+
+
+def call(kernel, outs, n_in, spaces, scratch=(), collective=None):
     more = {}
     if collective is not None:
         more = {"collective_id": collective, "has_side_effects": True}
     return pl.pallas_call(
         kernel,
         out_shape=[jax.ShapeDtypeStruct(shape, F32) for shape in outs],
-        in_specs=[pl.BlockSpec(memory_space=pltpu.HBM)] * n_in,
-        out_specs=[pl.BlockSpec(memory_space=pltpu.VMEM)] * len(outs),
+        in_specs=[pl.BlockSpec(memory_space=spaces[0])] * n_in,
+        out_specs=[pl.BlockSpec(memory_space=spaces[1])] * len(outs),
         scratch_shapes=[pltpu.VMEM(s, F32) if isinstance(s, tuple) else s for s in scratch],
         compiler_params=pltpu.CompilerParams(vmem_limit_bytes=VMEM_LIMIT, **more),
         cost_estimate=pl.CostEstimate(flops=10000000, bytes_accessed=4000000, transcendentals=0),
@@ -642,10 +669,12 @@
     dense = (owners, 64, 128)
     dma = pltpu.SemaphoreType.DMA
 
-    coarse_next, out = call(
+    results = [field, (4, 5, 32, 1024)]
+    made = call(
         step_kernel,
-        [field, (4, 5, 32, 1024)],
+        results,
         4,
+        (pltpu.HBM, pltpu.VMEM),
         [pltpu.SMEM((3, 4, owners), jnp.int32), pltpu.SMEM((owners,), jnp.int32)]
         + [(4, 5, 32, 1024), field, dma((11,)), cube, prim] + [planes] * 5 + [(5, 32, 128), (4, 64, 128)]
         + [(5, 17, 24, 128), (PRIMS, 17, 24, 128), side, field, (6,) + side, (8, 64, 128)]
@@ -653,6 +682,8 @@
         + [(2, 2) + side, (4,) + side, (3, 4) + side, dma((3, 2, 4)), dma((3, 2, owners)), (5, 4, 32, 128), (30, 16, 128)],
         0,
     )(*(pltpu.with_memory_space_constraint(a, pltpu.HBM) for a in (anchors, counts, patch, coarse_state)))
+    made = (pltpu.with_memory_space_constraint(a, pltpu.VMEM) for a in made)
+    coarse_next, out = call(write_kernel, results, 2, (pltpu.VMEM, pltpu.HBM), [dma((2,))])(*made)
     return (coarse_next, out.reshape(patch_state.shape))
 
 

time: 54.1 us -> 52.9 us (0.978)
  local copies, waits for them, and re-layouts: 2.33 us -> 0 us
  Pallas kernels: 50.8 us -> 51.9 us
    unnamed x2 -> x0, local copies, waits for them, and re-layouts: 2.33 us -> none
    pallas_call x1 -> x2, Pallas kernels: 50.8 us -> 51.9 us  [the longest x1 50.2 us: shards(): call(step_kernel, results, 4, (pltpu.HBM, pltpu.VMEM), [pltpu.SMEM((3, 4,...]
where the time goes in v7:
time: 52.9 us; the launch traced here: 52.5 us
  Pallas kernels  51.9 us (98%)
  between operations  0.64 us (1%)
    pallas_call x1, Pallas kernels, shards(): call(step_kernel, results, 4, (pltpu.HBM, pltpu.VMEM), [pltpu.SMEM((3, 4,...  50.2 us
    pallas_call x1, Pallas kernels, shards(): call(write_kernel, results, 2, (pltpu.VMEM, pltpu.HBM), [dma((2,))])(*made)  1.72 us

profile of v7, /device:TPU:0, one launch (start us, length us, event | category | flops | bytes accessed | tf_op | source)
XLA Modules:
  0.0 52.5 jit_solution(6365450190109258746)
XLA Ops:
  0.6 50.2 %shard_map.59 = (f32[5,16,16,128]{3,2,1,0:T(8,128)S(1)}, f32[4,5,32,1024]{3,2,1,0:T(8,128)S(1)}) custom-call(s32[3,4,16]{2,1,0:T(4,128)} %bitcast.7, s32[16]{0:T(128)} %bitcast.8, f32[4,5,32,1024]{3,2,1,0:T(8,128)} %bitcast.6, f32[5,16,16,128]{3,2,1,0:T(8,128)} %field_hbm.1), custom_call_target="tpu_custom_call" | custom-call | flops 10000000 | bytes 4000000 | tf_op jit(solution)/shard_map/pallas_call | solution.py:673
  50.8 1.7 %shard_map.60 = (f32[5,16,16,128]{3,2,1,0:T(8,128)}, f32[4,5,32,1024]{3,2,1,0:T(8,128)}) custom-call(f32[5,16,16,128]{3,2,1,0:T(8,128)S(1)} %get-tuple-element.6.field, f32[4,5,32,1024]{3,2,1,0:T(8,128)S(1)} %get-tuple-element.7.patch), custom_call_target="tpu_custom_call" | custom-call | flops 10000000 | bytes 4000000 | tf_op jit(solution)/shard_map/pallas_call | solution.py:686

commit v8 on v7

--- a/solution.py
+++ b/solution.py
@@ -105,9 +105,6 @@
 
 def pick(x, index):
     return jnp.take_along_axis(x, index, axis=1)
-
-
-NORMAL = (2, 2, 0, 0, 1, 1)
 
 
 def next_x(a):
@@ -236,25 +233,25 @@
                     S[e, c] = jnp.concatenate([even, even, odd, odd], axis=0)
 
 
-def fine_boundary(B, Q, S, FB, FS, first):
-    for n in range(3):
-        for face in (2 * n, 2 * n + 1):
-            inner = [B[face, c] for c in range(5)]
-            outer = [S[face, c] for c in range(5)]
-            qo = primitives(outer)
-            if n == 0:
-                qi = primitives(inner)
-            elif n == 1:
-                qi = [Q[k, :, 31 * (face % 2), :] for k in range(PRIMS)]
+def fine_boundary(B, S, FB, FS, first):
+    def body(n, _):
+        axis = lax.rem(n + 2, 3)
+        order = (0, 1 + axis, 1 + lax.rem(axis + 1, 3), 1 + lax.rem(axis + 2, 3), 4)
+        for side in range(2):
+            face = 2 * n + side
+            inner = [B[face, c] for c in order]
+            outer = [S[face, c] for c in order]
+            qi, qo = primitives(inner), primitives(outer)
+            if side == 0:
+                F = face_flux(outer, qo, inner, qi, 0)
             else:
-                qi = [Q[k, 31 * (face % 2)] for k in range(PRIMS)]
-            if face % 2 == 0:
-                F = face_flux(outer, qo, inner, qi, NORMAL[face])
-            else:
-                F = face_flux(inner, qi, outer, qo, NORMAL[face])
-            for c in range(5):
-                FB[face, c] = F[c]
-                FS[face, c] = F[c] if first else FS[face, c] + F[c]
+                F = face_flux(inner, qi, outer, qo, 0)
+            for k, c in enumerate(order):
+                FB[face, c] = F[k]
+                FS[face, c] = F[k] if first else FS[face, c] + F[k]
+        return 0
+
+    lax.fori_loop(0, 3, body, 0)
 
 
 def add_boundary(W, FB):
@@ -336,14 +333,17 @@
     shape = (16, 128)
     lane = lanes(shape)
     zeros = jnp.zeros(shape, F32)
-    T = [zeros] * 10
-    for x in range(16):
-        here = lane % 16 == x
-        for c in range(5):
-            U = field[c, x, 0:16, :]
-            turned = roll(U, x, 1)
-            T[c] = jnp.where((lane + 1) % 16 == x, turned, T[c])
-            T[5 + c] = jnp.where(here, turned, T[5 + c])
+
+    def collected(x, T):
+        lower, upper = (lane + 1) % 16 == x, lane % 16 == x
+        out = list(T)
+        for c in range(5):
+            turned = pltpu.roll(field[c, x], x, 1)
+            out[c] = jnp.where(lower, turned, T[c])
+            out[5 + c] = jnp.where(upper, turned, T[5 + c])
+        return tuple(out)
+
+    T = lax.fori_loop(0, 16, collected, (zeros,) * 10)
     T = [roll(a, 1, 1) for a in T[:5]] + [roll(a, -16, 1) for a in T[5:]]
     z0 = jnp.concatenate(T[:8], axis=0).T
     z1 = jnp.concatenate(T[8:] + [zeros] * 6, axis=0).T
@@ -363,10 +363,14 @@
 
 
 def coarse_step(field, xlo, xhi, ylo, yhi, adv, FP, C, Q, FX):
-    for c in range(5):
-        for x in range(16):
+    def fill(x, _):
+        for c in range(5):
             C[c, x, 0:16] = field[c, x]
-            C[c, x, 16:24] = jnp.broadcast_to(yhi[c, x : x + 1], (8, 128))
+            C[c, x, 16:24] = jnp.broadcast_to(yhi[c, pl.ds(x, 1), :], (8, 128))
+        return 0
+
+    lax.fori_loop(0, 16, fill, 0)
+    for c in range(5):
         C[c, 16, 0:16] = xhi[c]
         C[c, 16, 16:24] = xhi[c, 8:16]
 
@@ -549,27 +553,27 @@
     fine_edges(W, FY, B)
     place.greeted()
     near = place.neighbours(planes, old, near_sems.at[0])
-    fine_interior(W, Q, FY, 0, 4)
+    fine_interior(W, Q, FY, 0, 10)
     wait(near)
     pack_shells(blocks, field, old, PZ, dense_old)
     far_old = place.exchange(dense_old, got_old, far_sems.at[0])
     coarse_step(field, *old, adv, FP, C, CQ, FX)
     planes = edge_planes(adv, edges.at[1])
     near = place.neighbours(planes, new, near_sems.at[1])
-    fine_interior(W, Q, FY, 4, 10)
+    fine_interior(W, Q, FY, 10, 14)
     wait(near)
     pack_shells(blocks, adv, new, PZ, dense_new)
     far_new = place.exchange(dense_new, got_new, far_sems.at[1])
-    fine_interior(W, Q, FY, 10, 32)
+    fine_interior(W, Q, FY, 14, 32)
     wait(far_old)
     fine_shells(got_old, sources, S1, T16)
-    fine_boundary(B, Q, S1, FB, FS, True)
+    fine_boundary(B, S1, FB, FS, True)
     add_boundary(W, FB)
     fine_again(W, FB, Q, B)
     fine_edges(W, FY, B)
     wait(far_new)
     fine_shells(got_old, sources, S2, T16, got_new)
-    fine_boundary(B, Q, S2, FB, FS, False)
+    fine_boundary(B, S2, FB, FS, False)
     fine_pack(FS, PS, T16)
     for i in range(place.ni):
         slot = jnp.int32(0)
@@ -593,10 +597,8 @@
 
 
 def write_kernel(field, patch, out_field, out, sems):
-    copies = [
-        pltpu.make_async_copy(patch, out, sems.at[0]),
-        pltpu.make_async_copy(field, out_field, sems.at[1]),
-    ]
+    copies = [pltpu.make_async_copy(patch.at[s], out.at[s], sems.at[s]) for s in range(4)]
+    copies.append(pltpu.make_async_copy(field, out_field, sems.at[4]))
     for copy in copies:
         copy.start()
     wait(copies)
@@ -634,11 +636,16 @@
                 else:
                     D[e - 2, c] = value
     column = lane % 16
-    for c in range(5):
-        lower, upper = roll(delta[0, c], -1, 1), roll(delta[1, c], 16, 1)
-        for x in range(16):
-            both = jnp.where((column + 1) % 16 == x, lower, 0.0)
-            out[c, x] = adv[c, x] + roll(jnp.where(column == x, upper, both), -x, 1)
+    lower = [roll(delta[0, c], -1, 1) for c in range(5)]
+    upper = [roll(delta[1, c], 16, 1) for c in range(5)]
+
+    def put(x, _):
+        for c in range(5):
+            both = jnp.where((column + 1) % 16 == x, lower[c], 0.0)
+            out[c, x] = adv[c, x] + pltpu.roll(jnp.where(column == x, upper[c], both), 128 - x, 1)
+        return 0
+
+    lax.fori_loop(0, 16, put, 0)
 
 
 def call(kernel, outs, n_in, spaces, scratch=(), collective=None):
@@ -683,7 +690,7 @@
         0,
     )(*(pltpu.with_memory_space_constraint(a, pltpu.HBM) for a in (anchors, counts, patch, coarse_state)))
     made = (pltpu.with_memory_space_constraint(a, pltpu.VMEM) for a in made)
-    coarse_next, out = call(write_kernel, results, 2, (pltpu.VMEM, pltpu.HBM), [dma((2,))])(*made)
+    coarse_next, out = call(write_kernel, results, 2, (pltpu.VMEM, pltpu.HBM), [dma((5,))])(*made)
     return (coarse_next, out.reshape(patch_state.shape))
 
 

time: 52.9 us -> 54.5 us (1.030)
  Pallas kernels: 51.9 us -> 53.5 us
    pallas_call x1, Pallas kernels: 50.2 us -> 51.7 us  [shards(): call(step_kernel, results, 4, (pltpu.HBM, pltpu.VMEM), [pltpu.SMEM((3, 4,...]
where the time goes in v8:
time: 54.5 us; the launch traced here: 54.1 us
  Pallas kernels  53.5 us (98%)
  between operations  0.64 us (1%)
    pallas_call x1, Pallas kernels, shards(): call(step_kernel, results, 4, (pltpu.HBM, pltpu.VMEM), [pltpu.SMEM((3, 4,...  51.7 us
    pallas_call x1, Pallas kernels, shards(): call(write_kernel, results, 2, (pltpu.VMEM, pltpu.HBM), [dma((5,))])(*made)  1.74 us

profile of v8, /device:TPU:0, one launch (start us, length us, event | category | flops | bytes accessed | tf_op | source)
XLA Modules:
  0.0 54.1 jit_solution(11908200026602678348)
XLA Ops:
  0.6 51.7 %shard_map.59 = (f32[5,16,16,128]{3,2,1,0:T(8,128)S(1)}, f32[4,5,32,1024]{3,2,1,0:T(8,128)S(1)}) custom-call(s32[3,4,16]{2,1,0:T(4,128)} %bitcast.7, s32[16]{0:T(128)} %bitcast.8, f32[4,5,32,1024]{3,2,1,0:T(8,128)} %bitcast.6, f32[5,16,16,128]{3,2,1,0:T(8,128)} %field_hbm.1), custom_call_target="tpu_custom_call" | custom-call | flops 10000000 | bytes 4000000 | tf_op jit(solution)/shard_map/pallas_call | solution.py:680
  52.4 1.7 %shard_map.60 = (f32[5,16,16,128]{3,2,1,0:T(8,128)}, f32[4,5,32,1024]{3,2,1,0:T(8,128)}) custom-call(f32[5,16,16,128]{3,2,1,0:T(8,128)S(1)} %get-tuple-element.6.field, f32[4,5,32,1024]{3,2,1,0:T(8,128)S(1)} %get-tuple-element.7.patch), custom_call_target="tpu_custom_call" | custom-call | flops 10000000 | bytes 4000000 | tf_op jit(solution)/shard_map/pallas_call | solution.py:693

commit v9 on v7

--- a/solution.py
+++ b/solution.py
@@ -533,34 +533,32 @@
         pltpu.make_async_copy(anchors_hbm, anchors, load_sems.at[9]),
         pltpu.make_async_copy(counts_hbm, counts, load_sems.at[10]),
     ]
-    chunk(0).start()
     for copy in small:
         copy.start()
-    for yg in range(1, 8):
+    for yg in range(8):
         chunk(yg).start()
     old, new, rims = ([sides.at[n, k] for k in range(4)] for n in range(3))
     place.greet()
-    fine_load(patch, W, Q, B, T, lambda yg: chunk(yg).wait())
     wait(small)
     planes = edge_planes(field, edges.at[0])
+    place.greeted()
+    near = place.neighbours(planes, old, near_sems.at[0])
+    fine_load(patch, W, Q, B, T, lambda yg: chunk(yg).wait())
     count = counts[me]
     sources = [anchors[0, s, me] // 16 for s in range(4)]
     blocks = owned_blocks(anchors, counts, me, place.ni)
     fine_edges(W, FY, B)
-    place.greeted()
-    near = place.neighbours(planes, old, near_sems.at[0])
-    fine_interior(W, Q, FY, 0, 4)
     wait(near)
     pack_shells(blocks, field, old, PZ, dense_old)
     far_old = place.exchange(dense_old, got_old, far_sems.at[0])
     coarse_step(field, *old, adv, FP, C, CQ, FX)
     planes = edge_planes(adv, edges.at[1])
     near = place.neighbours(planes, new, near_sems.at[1])
-    fine_interior(W, Q, FY, 4, 10)
+    fine_interior(W, Q, FY, 0, 4)
     wait(near)
     pack_shells(blocks, adv, new, PZ, dense_new)
     far_new = place.exchange(dense_new, got_new, far_sems.at[1])
-    fine_interior(W, Q, FY, 10, 32)
+    fine_interior(W, Q, FY, 4, 32)
     wait(far_old)
     fine_shells(got_old, sources, S1, T16)
     fine_boundary(B, Q, S1, FB, FS, True)

time: 52.9 us -> 52.1 us (0.985)
    pallas_call x1, Pallas kernels: 50.2 us -> 49.6 us  [shards(): call(step_kernel, results, 4, (pltpu.HBM, pltpu.VMEM), [pltpu.SMEM((3, 4,...]
where the time goes in v9:
time: 52.1 us; the launch traced here: 52 us
  Pallas kernels  51.4 us (99%)
  between operations  0.64 us (1%)
    pallas_call x1, Pallas kernels, shards(): call(step_kernel, results, 4, (pltpu.HBM, pltpu.VMEM), [pltpu.SMEM((3, 4,...  49.6 us
    pallas_call x1, Pallas kernels, shards(): call(write_kernel, results, 2, (pltpu.VMEM, pltpu.HBM), [dma((2,))])(*made)  1.72 us

profile of v9, /device:TPU:0, one launch (start us, length us, event | category | flops | bytes accessed | tf_op | source)
XLA Modules:
  0.0 52.0 jit_solution(17679330283620490312)
XLA Ops:
  0.6 49.6 %shard_map.59 = (f32[5,16,16,128]{3,2,1,0:T(8,128)S(1)}, f32[4,5,32,1024]{3,2,1,0:T(8,128)S(1)}) custom-call(s32[3,4,16]{2,1,0:T(4,128)} %bitcast.7, s32[16]{0:T(128)} %bitcast.8, f32[4,5,32,1024]{3,2,1,0:T(8,128)} %bitcast.6, f32[5,16,16,128]{3,2,1,0:T(8,128)} %field_hbm.1), custom_call_target="tpu_custom_call" | custom-call | flops 10000000 | bytes 4000000 | tf_op jit(solution)/shard_map/pallas_call | solution.py:671
  50.3 1.7 %shard_map.60 = (f32[5,16,16,128]{3,2,1,0:T(8,128)}, f32[4,5,32,1024]{3,2,1,0:T(8,128)}) custom-call(f32[5,16,16,128]{3,2,1,0:T(8,128)S(1)} %get-tuple-element.6.field, f32[4,5,32,1024]{3,2,1,0:T(8,128)S(1)} %get-tuple-element.7.patch), custom_call_target="tpu_custom_call" | custom-call | flops 10000000 | bytes 4000000 | tf_op jit(solution)/shard_map/pallas_call | solution.py:684

commit v10 on v9

--- a/solution.py
+++ b/solution.py
@@ -549,16 +549,15 @@
     blocks = owned_blocks(anchors, counts, me, place.ni)
     fine_edges(W, FY, B)
     wait(near)
-    pack_shells(blocks, field, old, PZ, dense_old)
-    far_old = place.exchange(dense_old, got_old, far_sems.at[0])
     coarse_step(field, *old, adv, FP, C, CQ, FX)
     planes = edge_planes(adv, edges.at[1])
     near = place.neighbours(planes, new, near_sems.at[1])
-    fine_interior(W, Q, FY, 0, 4)
+    pack_shells(blocks, field, old, PZ, dense_old)
+    far_old = place.exchange(dense_old, got_old, far_sems.at[0])
     wait(near)
     pack_shells(blocks, adv, new, PZ, dense_new)
     far_new = place.exchange(dense_new, got_new, far_sems.at[1])
-    fine_interior(W, Q, FY, 4, 32)
+    fine_interior(W, Q, FY, 0, 32)
     wait(far_old)
     fine_shells(got_old, sources, S1, T16)
     fine_boundary(B, Q, S1, FB, FS, True)

time: 52.1 us -> 52.2 us (level)
  no operation moved by 1% of the time
where the time goes in v10:
time: 52.2 us; the launch traced here: 51.9 us
  Pallas kernels  51.3 us (98%)
  between operations  0.64 us (1%)
    pallas_call x1, Pallas kernels, shards(): call(step_kernel, results, 4, (pltpu.HBM, pltpu.VMEM), [pltpu.SMEM((3, 4,...  49.5 us
    pallas_call x1, Pallas kernels, shards(): call(write_kernel, results, 2, (pltpu.VMEM, pltpu.HBM), [dma((2,))])(*made)  1.72 us

profile of v10, /device:TPU:0, one launch (start us, length us, event | category | flops | bytes accessed | tf_op | source)
XLA Modules:
  0.0 51.9 jit_solution(7784480522738867911)
XLA Ops:
  0.6 49.5 %shard_map.59 = (f32[5,16,16,128]{3,2,1,0:T(8,128)S(1)}, f32[4,5,32,1024]{3,2,1,0:T(8,128)S(1)}) custom-call(s32[3,4,16]{2,1,0:T(4,128)} %bitcast.7, s32[16]{0:T(128)} %bitcast.8, f32[4,5,32,1024]{3,2,1,0:T(8,128)} %bitcast.6, f32[5,16,16,128]{3,2,1,0:T(8,128)} %field_hbm.1), custom_call_target="tpu_custom_call" | custom-call | flops 10000000 | bytes 4000000 | tf_op jit(solution)/shard_map/pallas_call | solution.py:670
  50.2 1.7 %shard_map.60 = (f32[5,16,16,128]{3,2,1,0:T(8,128)}, f32[4,5,32,1024]{3,2,1,0:T(8,128)}) custom-call(f32[5,16,16,128]{3,2,1,0:T(8,128)S(1)} %get-tuple-element.6.field, f32[4,5,32,1024]{3,2,1,0:T(8,128)S(1)} %get-tuple-element.7.patch), custom_call_target="tpu_custom_call" | custom-call | flops 10000000 | bytes 4000000 | tf_op jit(solution)/shard_map/pallas_call | solution.py:683
